TPU v7x, 32 devices: a whole 2x2x4 slice. The times are simulated.
32 devices in a mesh: row: 8 (over y, x, core), col: 4 (over z).
Axes of the slice: x: 2, y: 2, z: 4, core: 2. Of those that a mesh axis runs over, the one named last changes fastest.
Arguments:
- features: bfloat16 [8, 4, 128, 128], P('row', 'col'), may hold values from -6 to 6
- tiles: bfloat16 [8, 4, 128, 128, 128], P('row', 'col'), may hold values from -0.3984375 to 0.3984375
- tile_coords: int32 [8, 4, 128, 2], P('row', 'col'), may hold values from 0 to 7, as said below
- tile_count: int32 [8, 4], P('row', 'col'), may hold values from 1 to 128, as said below
- batch_mask: int32 [8, 4, 128], P('row', 'col'), may hold values 0 or 1
- history: bfloat16 [8, 4, 128, 256], P('row', 'col'), may hold values from 0 to 1.5
- weight_one: bfloat16 [128, 256], replicated, may hold values from -0.5 to 0.5
- bias_one: float32 [256], replicated, may hold values from -3 to 3
- weight_two: bfloat16 [256, 172], replicated, may hold values from -0.375 to 0.375
- bias_two: float32 [172], replicated, may hold values from -3 to 3
Outputs:
- new_history: bfloat16 [8, 4, 128, 256], P('row', 'col')
- logits: float32 [8, 4, 128, 172], P('row', 'col')
Inputs may be any that keep to these rules, and one draw needn't show every extreme that they name: `tile_coords`: column 0 is below 4 and column 1 below 8; coordinates may repeat. `tile_count`: some device has all 128 slots live.
All inputs are finite; a program needn't handle non-finite values. No bound on the sum of `batch_mask` on one device may be relied on, other than what follows from the above.
Results may differ from a plain program's by a relative error of at most 0.024.
Values may be sent and summed in bfloat16 or wider, within the bound.
No kernel may reach another device: no remote copies, remote signals or barrier semaphores. Data moves between devices by JAX's collectives and lax.ppermute only.
A program may use at most 64 MiB of HBM per device.

v0:
```python
import functools

import jax
import jax.numpy as jnp
from jax import lax
from jax.experimental import pallas as pl
from jax.experimental.pallas import tpu as pltpu
from jax.sharding import PartitionSpec as P

BF16 = jnp.bfloat16
F32 = jnp.float32
VMEM_LIMIT = 48 * 1024 * 1024


def partner(index, slot):
    return index ^ slot


def turned(slot):
    return slot ^ (((slot >> 1) ^ (slot >> 2)) & 1) * 6


def seen(slot, index):
    return slot ^ (index & 1) * (turned(slot) ^ slot)


def order(size):
    return [0, *reversed(range(3, size, 2))]


def column_order(size):
    return order(size) + [turned(slot) ^ 1 for slot in order(size)]


def permuted(block, axis, size, slot):
    return lax.ppermute(block, axis, [(i, partner(i, slot)) for i in range(size)])


def fetched(block, axis, size, slot):
    return lax.ppermute(block, axis, [(partner(i, seen(slot, i)), i) for i in range(size)])


def fetch_chips(block, axis, size):
    return [fetched(block, axis, size, slot) for slot in order(size)[1:]]


def fetch_core(blocks, axis, size):
    return permuted(blocks, axis, size, 1)


def both_cores(blocks, axis, size):
    found = jnp.concatenate([blocks, fetch_core(blocks, axis, size)])
    return found[jnp.argsort(jnp.array(column_order(size)))]


def send_across(blocks, n_row, n_col):
    arrived = []
    for slot in reversed(range(n_col)):
        pairs = [
            (row * n_col + col, partner(row, 1) * n_col + partner(col, slot))
            for row in range(n_row)
            for col in range(n_col)
        ]
        arrived.append(lax.ppermute(blocks[slot], ("row", "col"), pairs))
    return arrived


def send_each(blocks, axis, size):
    return [permuted(blocks[slot], axis, size, slot) for slot in reversed(range(1, size))]


def call(kernel, out_shape, operands, specs=None, scratch=(), cost=None, out_specs=None):
    vmem = pl.BlockSpec(memory_space=pltpu.VMEM)
    return pl.pallas_call(
        kernel,
        out_shape=out_shape,
        in_specs=specs or [vmem] * len(operands),
        out_specs=out_specs or jax.tree.map(lambda _: vmem, out_shape),
        scratch_shapes=list(scratch),
        cost_estimate=cost,
        compiler_params=pltpu.CompilerParams(vmem_limit_bytes=VMEM_LIMIT),
    )(*operands)


def dot_nt(left, right):
    return lax.dot_general(left, right, (((1,), (1,)), ((), ())), preferred_element_type=F32)


def build_kernel(
    n_row, n_col, chunks, count, coords_hbm, tiles_hbm, dense_ref, coords, tiles, first, second, sems, coords_sem
):
    slots, block = tiles.shape[0], tiles.shape[1]
    per, part = slots // chunks, block // 2
    copies = [
        pltpu.make_async_copy(
            tiles_hbm.at[pl.ds(i * per, per)], tiles.at[pl.ds(i * per, per)], sems.at[i]
        )
        for i in range(chunks)
    ]
    coords_copy = pltpu.make_async_copy(coords_hbm, coords, coords_sem)
    coords_copy.start()
    live = count[0, 0]
    for i, copy in enumerate(copies):
        pl.when(i * per < live)(copy.start)
    row, col = lax.axis_index("row"), lax.axis_index("col")
    first[...] = jnp.zeros_like(first)
    second[...] = jnp.zeros_like(second)
    coords_copy.wait()

    def place(t):
        at = partner(coords[0, t], col) * n_row + seen(partner(coords[1, t], row), row)
        return jnp.where(t < live, at, n_row * n_col)

    for i in range(chunks):

        @pl.when(i * per < live)
        def _():
            copies[i].wait()

            @pl.loop(0, per, unroll=8)
            def _(step):
                t = i * per + step
                at = place(t)
                first[at] += tiles[t, :part].astype(F32)
                second[at] += tiles[t, part:].astype(F32)

    for k in range(n_col):
        for j, slot in enumerate(column_order(n_row)):
            at = k * n_row + slot
            columns = slice(j * block, (j + 1) * block)
            dense_ref[k * block : k * block + part, columns] = first[at].astype(BF16)
            dense_ref[k * block + part : (k + 1) * block, columns] = second[at].astype(BF16)


def prepare_kernel(mask, bias, history, *refs):
    kept_out, bias_out, wide = refs[-3:]
    block, classes = history.shape[0], bias.shape[1]
    mask_cols = jnp.broadcast_to(mask[...].astype(F32), (block, block)).T
    chosen = jnp.concatenate([mask_cols] * (history.shape[1] // block), axis=1) == 1.0
    kept_out[...] = jnp.where(chosen, -1.0, history[...].astype(F32)).astype(BF16)
    wide[...] = jnp.zeros_like(wide)
    wide[:, :classes] = jnp.broadcast_to(bias[...], (block, classes))
    bias_out[...] = wide[...].T[:classes]


def join_rows_kernel(places, *refs):
    out = refs[-1]
    block = refs[0].shape[0]
    for ref, place in zip(refs, places):
        out[place * block : (place + 1) * block, :] = ref[...]


def half_one_kernel(dense_ref, mine_ref, out):
    half = mine_ref.shape[0]
    out[...] = jnp.dot(dense_ref[:, :half], mine_ref[...], preferred_element_type=F32)


def layer_one_kernel(dense_ref, first_ref, other_ref, *outputs):
    half, block = other_ref.shape[0], dense_ref.shape[0] // len(outputs)
    total = first_ref[...] + jnp.dot(
        dense_ref[:, half:], other_ref[...], preferred_element_type=F32
    )
    for k, out in enumerate(outputs):
        out[...] = total[k * block : (k + 1) * block, :].astype(BF16)


def hidden_kernel(n_col, *refs):
    parts = refs[:n_col]
    feats, w_one, b_one, w_two, kept, pushed_ref, proj_ref = refs[n_col:]
    total = feats[: kept.shape[0], :].astype(F32)
    for part in parts:
        total += part[...].astype(F32)
    pre = jnp.dot(total.astype(BF16), w_one[...], preferred_element_type=F32) + b_one[...]
    hidden = jnp.maximum(pre, 0.0)
    old = kept[...].astype(F32)
    pushed = jnp.where(old < 0.0, hidden, old).astype(BF16)
    pushed_ref[...] = pushed
    proj_ref[...] = dot_nt(w_two[...], pushed).astype(BF16)


def write_kernel(value, out):
    out[...] = value[...]


def late_kernel(value, after, out):
    del after
    out[...] = value[...]


def lanes(refs, scratch, places=None):
    block = refs[0].shape[1]
    for i, ref in zip(places or range(len(refs)), refs):
        scratch[:, i * block : (i + 1) * block] = ref[...]
    return scratch[...]


def half_two_kernel(places, dense_ref, *refs):
    blocks, (out, scratch) = refs[:-2], refs[-2:]
    half = dense_ref.shape[1] // 2
    out[...] = dot_nt(
        lanes(blocks, scratch, places), dense_ref[:, half : half + scratch.shape[1]]
    )


def layer_two_kernel(n_col, dense_ref, first_ref, own_ref, near_ref, *refs):
    blocks, outputs, scratch = refs[: -n_col - 1], refs[-n_col - 1 : -1], refs[-1]
    block, half = near_ref.shape[1], scratch.shape[1]
    rest = lanes([own_ref, *blocks], scratch)
    total = first_ref[...] + dot_nt(rest, dense_ref[:, :half])
    total += dot_nt(near_ref[...], dense_ref[:, dense_ref.shape[1] - block :])
    for k, out in enumerate(outputs):
        out[...] = total[:, k * block : (k + 1) * block].astype(BF16)


def logits_kernel(n_col, pieces, *refs):
    parts = refs[:n_col]
    proj, bias, out_hbm, staged, sems = refs[n_col:]
    step = -(-staged.shape[0] // pieces // 16) * 16
    copies = []
    for i in range(pieces):
        rows = slice(i * step, (i + 1) * step if i < pieces - 1 else staged.shape[0])
        total = proj[rows, :].astype(F32) + bias[rows, :]
        for part in parts:
            total += part[rows, :].astype(F32)
        staged[rows, 0, :] = total
        copies.append(pltpu.make_async_copy(staged.at[rows], out_hbm.at[rows], sems.at[i]))
        copies[-1].start()
    for copy in copies:
        copy.wait()


def tiles_kernel(
    n_row, n_col, transposed, coords_ref, count_ref, tiles_ref, stacked_ref, out_ref, total
):
    row, col = lax.axis_index("row"), lax.axis_index("col")
    total[...] = jnp.zeros_like(total)

    @pl.loop(0, count_ref[0, 0])
    def _(t):
        k = partner(coords_ref[0, t], col)
        j = seen(partner(coords_ref[1, t], row), row)
        if transposed:
            total[k] += dot_nt(stacked_ref[j], tiles_ref[t])
        else:
            total[k] += jnp.dot(tiles_ref[t], stacked_ref[j], preferred_element_type=F32)

    out_ref[...] = total[...].astype(BF16)


def on_device(
    n_row, n_col,
    features, tiles, tile_coords, tile_count, batch_mask, history,
    weight_one, bias_one, weight_two, bias_two,
):
    feat, tile_set, hist = features[0, 0], tiles[0, 0], history[0, 0]
    coords = tile_coords[0, 0].T
    slots, block = tile_set.shape[0], tile_set.shape[1]
    f_in, hid, classes = feat.shape[1], weight_one.shape[1], weight_two.shape[1]
    w_two_t = weight_two.T
    dense_form = n_row * n_col <= slots
    smem = pl.BlockSpec(memory_space=pltpu.SMEM)
    vmem = pl.BlockSpec(memory_space=pltpu.VMEM)
    hbm = pl.BlockSpec(memory_space=pltpu.HBM)
    shape = jax.ShapeDtypeStruct

    def prepare(*after):
        return call(
            prepare_kernel,
            (shape((block, hid), BF16), shape((classes, block), F32)),
            (batch_mask[0], bias_two[None], hist, *after),
            specs=[vmem] * 3 + [pl.BlockSpec(memory_space=pl.ANY)] * len(after),
            scratch=[pltpu.VMEM((block, -(-classes // 128) * 128), F32)],
        )

    chips_one = [feat, *fetch_chips(feat, "row", n_row)]

    if dense_form:
        anywhere = pl.BlockSpec(memory_space=pl.ANY)
        chunks = 8
        dense = call(
            functools.partial(build_kernel, n_row, n_col, chunks),
            shape((n_col * block, n_row * block), BF16),
            (
                tile_count,
                pltpu.with_memory_space_constraint(coords, pltpu.HBM),
                pltpu.with_memory_space_constraint(tile_set, pltpu.HBM),
            ),
            specs=[smem, hbm, hbm],
            scratch=[
                pltpu.SMEM((2, slots), jnp.int32),
                pltpu.VMEM((slots, block, block), BF16),
                pltpu.VMEM((n_row * n_col + 1, block // 2, block), F32),
                pltpu.VMEM((n_row * n_col + 1, block // 2, block), F32),
                pltpu.SemaphoreType.DMA((chunks,)),
                pltpu.SemaphoreType.DMA(()),
            ],
            cost=pl.CostEstimate(
                flops=slots * block * block,
                bytes_accessed=2 * slots * block * block,
                transcendentals=0,
            ),
        )
        names = order(n_row)
        places_one = [0, *sorted(range(1, n_row // 2), key=lambda i: (names[i] != 5, names[i]))]
        mine_one = call(
            functools.partial(join_rows_kernel, places_one),
            shape((n_row // 2 * block, f_in), BF16),
            (*[chips_one[i] for i in places_one], dense),
            specs=[vmem] * len(chips_one) + [anywhere],
        )
        other_one = fetch_core(mine_one, "row", n_row)
        kept, bias_cols = prepare(mine_one)
        half_one = call(half_one_kernel, shape((n_col * block, f_in), F32), (dense, mine_one))
        parts_one = call(
            layer_one_kernel,
            [shape((block, f_in), BF16)] * n_col,
            (dense, half_one, other_one),
        )
    else:
        kept, bias_cols = prepare()
        summed = call(
            functools.partial(tiles_kernel, n_row, n_col, False),
            shape((n_col, block, f_in), BF16),
            (coords, tile_count, tile_set, both_cores(jnp.stack(chips_one), "row", n_row)),
            specs=[smem, smem, vmem, vmem],
            scratch=[pltpu.VMEM((n_col, block, f_in), F32)],
        )
        parts_one = [summed[k] for k in range(n_col)]
        other_one = fetch_core(feat, "row", n_row)

    arrived_one = send_across(parts_one, n_row, n_col)
    kept = fetch_core(kept, "row", n_row)
    pushed, proj = call(
        functools.partial(hidden_kernel, n_col),
        (shape((block, hid), BF16), shape((classes, block), BF16)),
        (*arrived_one, other_one, weight_one, bias_one[None], w_two_t, kept),
    )
    chips_two = [proj, *fetch_chips(proj, "row", n_row)]
    if dense_form:
        near = chips_two[order(n_row).index(5)]
        early = [x for x in chips_two if x is not near]
        near_other = fetched(proj, "row", n_row, 2)
        others_two = [fetch_core(x, "row", n_row) for x in early] + [near_other]
        own_proj = others_two[0]
    else:
        own_proj = fetch_core(proj, "row", n_row)

    if dense_form:
        late = others_two
        places_two = [0, *reversed(range(1, len(early)))]
        half_two = call(
            functools.partial(half_two_kernel, places_two),
            shape((classes, n_col * block), F32),
            (dense, *[early[i] for i in places_two]),
            scratch=[pltpu.VMEM((classes, len(early) * block), BF16)],
        )
        pushed = call(
            late_kernel, shape((block, hid), BF16), (pushed, half_two), specs=[vmem, anywhere]
        )
        parts_two = call(
            functools.partial(layer_two_kernel, n_col),
            [shape((classes, block), BF16)] * n_col,
            (dense, half_two, late[0], near, *late[1:]),
            scratch=[pltpu.VMEM((classes, len(late) * block), BF16)],
        )
    else:
        other_slots = jnp.arange(n_row) ^ 1
        summed = call(
            functools.partial(tiles_kernel, n_row, n_col, True),
            shape((n_col, classes, block), BF16),
            (coords, tile_count, tile_set, both_cores(jnp.stack(chips_two), "row", n_row)[other_slots]),
            specs=[smem, smem, vmem, vmem],
            scratch=[pltpu.VMEM((n_col, classes, block), F32)],
        )
        parts_two = [summed[k] for k in range(n_col)]

    arrived_two = send_each(parts_two, "col", n_col)
    pushed = call(write_kernel, shape((block, hid), BF16), (fetch_core(pushed, "row", n_row),))
    pieces = 4
    scores = call(
        functools.partial(logits_kernel, n_col, pieces),
        shape((classes, 1, block), F32),
        (parts_two[0], *arrived_two, own_proj, bias_cols),
        scratch=[pltpu.VMEM((classes, 1, block), F32), pltpu.SemaphoreType.DMA((pieces,))],
        out_specs=pl.BlockSpec(memory_space=pl.ANY),
    )
    return pushed[None, None], scores.transpose(1, 2, 0)[None]


def solution(mesh):
    sizes = mesh.shape
    return jax.shard_map(
        functools.partial(on_device, sizes["row"], sizes["col"]),
        mesh=mesh,
        in_specs=(
            P("row", "col", None, None),
            P("row", "col", None, None, None),
            P("row", "col", None, None),
            P("row", "col"),
            P("row", "col", None),
            P("row", "col", None, None),
            P(),
            P(),
            P(),
            P(),
        ),
        out_specs=(P("row", "col", None, None), P("row", "col", None, None)),
        check_vma=False,
    )
```

profile of v0, /device:TPU:0, one launch (start us, length us, event | category | flops | bytes accessed | tf_op | source)
XLA Modules:
  0.0 34.3 jit_solution(13926112826256678244)
XLA Ops:
  0.7 3.4 %collective-permute-start.2 = (bf16[128,128]{1,0:T(8,128)(2,1)}, bf16[128,128]{1,0:T(8,128)(2,1)S(1)}, u32[]{:S(2)}, u32[]{:S(2)}) collective-permute-start(bf16[128,128]{1,0:T(8,128)(2,1)} %bitcast.18), channel_id=1, source_target_pairs={{28,0},{24,4},{20,8},{16,12},{12,16},{8,20},{4,24},{0,28},{29,1},{... | collective-permute-start | bytes 98312 | tf_op jit(solution)/shard_map/ppermute | solution.py:40
  4.1 0.8 %collective-permute-start.1 = (bf16[128,128]{1,0:T(8,128)(2,1)}, bf16[128,128]{1,0:T(8,128)(2,1)S(1)}, u32[]{:S(2)}, u32[]{:S(2)}) collective-permute-start(bf16[128,128]{1,0:T(8,128)(2,1)} %bitcast.19), channel_id=1, source_target_pairs={{12,0},{16,4},{4,8},{24,12},{28,16},{0,20},{20,24},{8,28},{13,1},{... | collective-permute-start | bytes 98312 | tf_op jit(solution)/shard_map/ppermute | solution.py:40
  4.9 1.0 %collective-permute-start = (bf16[128,128]{1,0:T(8,128)(2,1)}, bf16[128,128]{1,0:T(8,128)(2,1)S(1)}, u32[]{:S(2)}, u32[]{:S(2)}) collective-permute-start(bf16[128,128]{1,0:T(8,128)(2,1)} %bitcast.20), channel_id=1, source_target_pairs={{20,0},{8,4},{28,8},{0,12},{4,16},{24,20},{12,24},{16,28},{21,1},{... | collective-permute-start | bytes 98312 | tf_op jit(solution)/shard_map/ppermute | solution.py:40
  6.5 1.5 %shard_map.113.refs_4_.dense_ref = bf16[512,1024]{1,0:T(8,128)(2,1)S(1)} custom-call(s32[1,1]{1,0:T(1,128)S(6)} %copy.13.count, s32[2,128]{1,0:T(2,128)} %bitcast.28, bf16[128,128,128]{2,1,0:T(8,128)(2,1)} %bitcast.25), custom_call_target="tpu_custom_call" | custom-call | flops 2097152 | bytes 4194304 | tf_op jit(solution)/shard_map/pallas_call | solution.py:74
  8.1 0.6 %collective-permute-done.refs_1_ = bf16[128,128]{1,0:T(8,128)(2,1)S(1)} collective-permute-done((bf16[128,128]{1,0:T(8,128)(2,1)}, bf16[128,128]{1,0:T(8,128)(2,1)S(1)}, u32[]{:S(2)}, u32[]{:S(2)}) %collective-permute-start) | collective-permute-done | bytes 32800 | tf_op jit(solution)/shard_map/ppermute | solution.py:40
  8.7 1.2 %collective-permute-start.3 = (bf16[512,128]{1,0:T(8,128)(2,1)S(1)}, bf16[512,128]{1,0:T(8,128)(2,1)S(1)}, u32[]{:S(2)}, u32[]{:S(2)}) collective-permute-start(bf16[512,128]{1,0:T(8,128)(2,1)S(1)} %shard_map.114.mine_ref.refs_0_), channel_id=1, source_target_pairs={{0,4},{4,0},{8,12},{12,8},{16,20},{20,16},{24,28},{28,24},{1,5},{5... | collective-permute-start | bytes 393224 | tf_op jit(solution)/shard_map/ppermute | solution.py:36
  10.5 0.5 %collective-permute-done.3.other_ref.refs_4_ = bf16[512,128]{1,0:T(8,128)(2,1)S(1)} collective-permute-done((bf16[512,128]{1,0:T(8,128)(2,1)S(1)}, bf16[512,128]{1,0:T(8,128)(2,1)S(1)}, u32[]{:S(2)}, u32[]{:S(2)}) %collective-permute-start.3) | collective-permute-done | bytes 131104 | tf_op jit(solution)/shard_map/ppermute | solution.py:36
  11.2 2.9 %collective-permute-start.4 = (bf16[128,128]{1,0:T(8,128)(2,1)S(1)}, bf16[128,128]{1,0:T(8,128)(2,1)S(1)}, u32[]{:S(2)}, u32[]{:S(2)}) collective-permute-start(bf16[128,128]{1,0:T(8,128)(2,1)S(1)} %get-tuple-element.14), channel_id=1, source_target_pairs={{0,7},{1,6},{2,5},{3,4},{4,3},{5,2},{6,1},{7,0},{8,15},{9,14},{10,... | collective-permute-start | bytes 98312 | tf_op jit(solution)/shard_map/ppermute | solution.py:64
  14.1 1.3 %collective-permute-start.6 = (bf16[128,128]{1,0:T(8,128)(2,1)S(1)}, bf16[128,128]{1,0:T(8,128)(2,1)S(1)}, u32[]{:S(2)}, u32[]{:S(2)}) collective-permute-start(bf16[128,128]{1,0:T(8,128)(2,1)S(1)} %get-tuple-element.16), channel_id=1, source_target_pairs={{0,5},{1,4},{2,7},{3,6},{4,1},{5,0},{6,3},{7,2},{8,13},{9,12},{10,... | collective-permute-start | bytes 98312 | tf_op jit(solution)/shard_map/ppermute | solution.py:64
  15.5 0.9 %collective-permute-done.4.refs_0_ = bf16[128,128]{1,0:T(8,128)(2,1)S(1)} collective-permute-done((bf16[128,128]{1,0:T(8,128)(2,1)S(1)}, bf16[128,128]{1,0:T(8,128)(2,1)S(1)}, u32[]{:S(2)}, u32[]{:S(2)}) %collective-permute-start.4) | collective-permute-done | bytes 32800 | tf_op jit(solution)/shard_map/ppermute | solution.py:64
  16.4 1.9 %collective-permute-done.5.refs_1_ = bf16[128,128]{1,0:T(8,128)(2,1)S(1)} collective-permute-done((bf16[128,128]{1,0:T(8,128)(2,1)S(1)}, bf16[128,128]{1,0:T(8,128)(2,1)S(1)}, u32[]{:S(2)}, u32[]{:S(2)}) %collective-permute-start.5) | collective-permute-done | bytes 32800 | tf_op jit(solution)/shard_map/ppermute | solution.py:64
  18.7 1.1 %collective-permute-start.10 = (bf16[172,128]{1,0:T(8,128)(2,1)S(1)}, bf16[172,128]{1,0:T(8,128)(2,1)S(1)}, u32[]{:S(2)}, u32[]{:S(2)}) collective-permute-start(bf16[172,128]{1,0:T(8,128)(2,1)S(1)} %get-tuple-element.20.refs_0_), channel_id=1, source_target_pairs={{28,0},{24,4},{20,8},{16,12},{12,16},{8,20},{4,24},{0,28},{29,1},{... | collective-permute-start | bytes 132104 | tf_op jit(solution)/shard_map/ppermute | solution.py:40
  19.8 1.1 %collective-permute-start.9 = (bf16[172,128]{1,0:T(8,128)(2,1)S(1)}, bf16[172,128]{1,0:T(8,128)(2,1)S(1)}, u32[]{:S(2)}, u32[]{:S(2)}) collective-permute-start(bf16[172,128]{1,0:T(8,128)(2,1)S(1)} %get-tuple-element.20.refs_0_), channel_id=1, source_target_pairs={{12,0},{16,4},{4,8},{24,12},{28,16},{0,20},{20,24},{8,28},{13,1},{... | collective-permute-start | bytes 132104 | tf_op jit(solution)/shard_map/ppermute | solution.py:40
  20.9 1.0 %collective-permute-start.16 = (bf16[172,128]{1,0:T(8,128)(2,1)S(1)}, bf16[172,128]{1,0:T(8,128)(2,1)S(1)}, u32[]{:S(2)}, u32[]{:S(2)}) collective-permute-start(bf16[172,128]{1,0:T(8,128)(2,1)S(1)} %get-tuple-element.20.refs_0_), channel_id=1, source_target_pairs={{8,0},{20,4},{0,8},{28,12},{24,16},{4,20},{16,24},{12,28},{9,1},{2... | collective-permute-start | bytes 132104 | tf_op jit(solution)/shard_map/ppermute | solution.py:40
  22.0 0.5 %collective-permute-start.13 = (bf16[172,128]{1,0:T(8,128)(2,1)S(1)}, bf16[172,128]{1,0:T(8,128)(2,1)S(1)}, u32[]{:S(2)}, u32[]{:S(2)}) collective-permute-start(bf16[172,128]{1,0:T(8,128)(2,1)S(1)} %get-tuple-element.20.refs_0_), channel_id=1, source_target_pairs={{20,0},{8,4},{28,8},{0,12},{4,16},{24,20},{12,24},{16,28},{21,1},{... | collective-permute-start | bytes 132104 | tf_op jit(solution)/shard_map/ppermute | solution.py:40
  22.4 0.6 %collective-permute-start.12 = (bf16[172,128]{1,0:T(8,128)(2,1)S(1)}, bf16[172,128]{1,0:T(8,128)(2,1)S(1)}, u32[]{:S(2)}, u32[]{:S(2)}) collective-permute-start(bf16[172,128]{1,0:T(8,128)(2,1)S(1)} %get-tuple-element.20.refs_0_), channel_id=1, source_target_pairs={{0,4},{4,0},{8,12},{12,8},{16,20},{20,16},{24,28},{28,24},{1,5},{5... | collective-permute-start | bytes 132104 | tf_op jit(solution)/shard_map/ppermute | solution.py:36
  24.4 0.5 %collective-permute-done.16.refs_2_ = bf16[172,128]{1,0:T(8,128)(2,1)S(1)} collective-permute-done((bf16[172,128]{1,0:T(8,128)(2,1)S(1)}, bf16[172,128]{1,0:T(8,128)(2,1)S(1)}, u32[]{:S(2)}, u32[]{:S(2)}) %collective-permute-start.16) | collective-permute-done | bytes 44064 | tf_op jit(solution)/shard_map/ppermute | solution.py:40
  25.0 0.5 %collective-permute-done.13.near_ref = bf16[172,128]{1,0:T(8,128)(2,1)S(1)} collective-permute-done((bf16[172,128]{1,0:T(8,128)(2,1)S(1)}, bf16[172,128]{1,0:T(8,128)(2,1)S(1)}, u32[]{:S(2)}, u32[]{:S(2)}) %collective-permute-start.13) | collective-permute-done | bytes 44064 | tf_op jit(solution)/shard_map/ppermute | solution.py:40
  25.8 2.8 %collective-permute-start.17 = (bf16[172,128]{1,0:T(8,128)(2,1)S(1)}, bf16[172,128]{1,0:T(8,128)(2,1)S(1)}, u32[]{:S(2)}, u32[]{:S(2)}) collective-permute-start(bf16[172,128]{1,0:T(8,128)(2,1)S(1)} %get-tuple-element.22), channel_id=1, source_target_pairs={{0,3},{1,2},{2,1},{3,0},{4,7},{5,6},{6,5},{7,4},{8,11},{9,10},{10,... | collective-permute-start | bytes 132104 | tf_op jit(solution)/shard_map/ppermute | solution.py:36
  28.6 1.7 %collective-permute-start.19 = (bf16[172,128]{1,0:T(8,128)(2,1)S(1)}, bf16[172,128]{1,0:T(8,128)(2,1)S(1)}, u32[]{:S(2)}, u32[]{:S(2)}) collective-permute-start(bf16[172,128]{1,0:T(8,128)(2,1)S(1)} %get-tuple-element.24), channel_id=1, source_target_pairs={{0,1},{1,0},{2,3},{3,2},{4,5},{5,4},{6,7},{7,6},{8,9},{9,8},{10,11... | collective-permute-start | bytes 132104 | tf_op jit(solution)/shard_map/ppermute | solution.py:36
  30.3 0.6 %shard_map.121 = bf16[128,256]{1,0:T(8,128)(2,1)} custom-call(bf16[128,256]{1,0:T(8,128)(2,1)S(1)} %collective-permute-done.11.value), custom_call_target="tpu_custom_call" | custom-call | tf_op jit(solution)/shard_map/pallas_call | solution.py:74
  30.9 1.1 %collective-permute-done.17.refs_1_ = bf16[172,128]{1,0:T(8,128)(2,1)S(1)} collective-permute-done((bf16[172,128]{1,0:T(8,128)(2,1)S(1)}, bf16[172,128]{1,0:T(8,128)(2,1)S(1)}, u32[]{:S(2)}, u32[]{:S(2)}) %collective-permute-start.17) | collective-permute-done | bytes 44064 | tf_op jit(solution)/shard_map/ppermute | solution.py:36
  32.0 1.6 %collective-permute-done.18.refs_2_ = bf16[172,128]{1,0:T(8,128)(2,1)S(1)} collective-permute-done((bf16[172,128]{1,0:T(8,128)(2,1)S(1)}, bf16[172,128]{1,0:T(8,128)(2,1)S(1)}, u32[]{:S(2)}, u32[]{:S(2)}) %collective-permute-start.18) | collective-permute-done | bytes 44064 | tf_op jit(solution)/shard_map/ppermute | solution.py:36
  33.6 0.7 %shard_map.123 = f32[172,1,128]{2,1,0:T(1,128)} custom-call(bf16[172,128]{1,0:T(8,128)(2,1)S(1)} %get-tuple-element.21.refs_0_, bf16[172,128]{1,0:T(8,128)(2,1)S(1)} %collective-permute-done.17.refs_1_, bf16[172,128]{1,0:T(8,128)(2,1)S(1)} %collective-permute-done.18.refs_2_, bf16[172,128]{1,0:T(8,128)(2,1)S(1)} %collective-permute-done.19.refs_3_, ...), custom_call_target="tpu_custom_call" | custom-call | tf_op jit(solution)/shard_map/pallas_call | solution.py:74
  (41 shorter events, 3.1 us)
Async XLA Ops:
  0.6 9.3 %copy-start.4 = (f32[172]{0:T(256)S(1)}, f32[172]{0:T(256)}, u32[]{:S(2)}) copy-start(f32[172]{0:T(256)} %param.19) | copy-start | bytes 2068
  0.7 7.4 %collective-permute-start.2 = (bf16[128,128]{1,0:T(8,128)(2,1)}, bf16[128,128]{1,0:T(8,128)(2,1)S(1)}, u32[]{:S(2)}, u32[]{:S(2)}) collective-permute-start(bf16[128,128]{1,0:T(8,128)(2,1)} %bitcast.18), channel_id=1, source_target_pairs={{28,0},{24,4},{20,8},{16,12},{12,16},{8,20},{4,24},{0,28},{29,1},{... | collective-permute-start | bytes 98312 | tf_op jit(solution)/shard_map/ppermute | solution.py:40
  4.1 4.0 %collective-permute-start.1 = (bf16[128,128]{1,0:T(8,128)(2,1)}, bf16[128,128]{1,0:T(8,128)(2,1)S(1)}, u32[]{:S(2)}, u32[]{:S(2)}) collective-permute-start(bf16[128,128]{1,0:T(8,128)(2,1)} %bitcast.19), channel_id=1, source_target_pairs={{12,0},{16,4},{4,8},{24,12},{28,16},{0,20},{20,24},{8,28},{13,1},{... | collective-permute-start | bytes 98312 | tf_op jit(solution)/shard_map/ppermute | solution.py:40
  4.9 3.8 %collective-permute-start = (bf16[128,128]{1,0:T(8,128)(2,1)}, bf16[128,128]{1,0:T(8,128)(2,1)S(1)}, u32[]{:S(2)}, u32[]{:S(2)}) collective-permute-start(bf16[128,128]{1,0:T(8,128)(2,1)} %bitcast.20), channel_id=1, source_target_pairs={{20,0},{8,4},{28,8},{0,12},{4,16},{24,20},{12,24},{16,28},{21,1},{... | collective-permute-start | bytes 98312 | tf_op jit(solution)/shard_map/ppermute | solution.py:40
  6.5 11.9 %copy-start = (bf16[256,172]{0,1:T(8,128)(2,1)S(1)}, bf16[256,172]{0,1:T(8,128)(2,1)}, u32[]{:S(2)}) copy-start(bf16[256,172]{0,1:T(8,128)(2,1)} %param.18) | copy-start | bytes 264196
  6.5 11.9 %copy-start.2 = (bf16[128,256]{1,0:T(8,128)(2,1)S(1)}, bf16[128,256]{1,0:T(8,128)(2,1)}, u32[]{:S(2)}) copy-start(bf16[128,256]{1,0:T(8,128)(2,1)} %refs_5_.1) | copy-start | bytes 196612
  6.5 11.9 %copy-start.5 = (f32[256]{0:T(256)S(1)}, f32[256]{0:T(256)}, u32[]{:S(2)}) copy-start(f32[256]{0:T(256)} %param.17) | copy-start | bytes 3076
  8.7 2.2 %collective-permute-start.3 = (bf16[512,128]{1,0:T(8,128)(2,1)S(1)}, bf16[512,128]{1,0:T(8,128)(2,1)S(1)}, u32[]{:S(2)}, u32[]{:S(2)}) collective-permute-start(bf16[512,128]{1,0:T(8,128)(2,1)S(1)} %shard_map.114.mine_ref.refs_0_), channel_id=1, source_target_pairs={{0,4},{4,0},{8,12},{12,8},{16,20},{20,16},{24,28},{28,24},{1,5},{5... | collective-permute-start | bytes 393224 | tf_op jit(solution)/shard_map/ppermute | solution.py:36
  10.1 5.5 %collective-permute-start.8 = (bf16[128,256]{1,0:T(8,128)(2,1)S(1)}, bf16[128,256]{1,0:T(8,128)(2,1)S(1)}, u32[]{:S(2)}, u32[]{:S(2)}) collective-permute-start(bf16[128,256]{1,0:T(8,128)(2,1)S(1)} %get-tuple-element.18), channel_id=1, source_target_pairs={{0,4},{4,0},{8,12},{12,8},{16,20},{20,16},{24,28},{28,24},{1,5},{5... | collective-permute-start | bytes 196616 | tf_op jit(solution)/shard_map/ppermute | solution.py:36
  11.2 5.2 %collective-permute-start.4 = (bf16[128,128]{1,0:T(8,128)(2,1)S(1)}, bf16[128,128]{1,0:T(8,128)(2,1)S(1)}, u32[]{:S(2)}, u32[]{:S(2)}) collective-permute-start(bf16[128,128]{1,0:T(8,128)(2,1)S(1)} %get-tuple-element.14), channel_id=1, source_target_pairs={{0,7},{1,6},{2,5},{3,4},{4,3},{5,2},{6,1},{7,0},{8,15},{9,14},{10,... | collective-permute-start | bytes 98312 | tf_op jit(solution)/shard_map/ppermute | solution.py:64
  14.1 4.2 %collective-permute-start.5 = (bf16[128,128]{1,0:T(8,128)(2,1)S(1)}, bf16[128,128]{1,0:T(8,128)(2,1)S(1)}, u32[]{:S(2)}, u32[]{:S(2)}) collective-permute-start(bf16[128,128]{1,0:T(8,128)(2,1)S(1)} %get-tuple-element.15), channel_id=1, source_target_pairs={{0,6},{1,7},{2,4},{3,5},{4,2},{5,3},{6,0},{7,1},{8,14},{9,15},{10,... | collective-permute-start | bytes 98312 | tf_op jit(solution)/shard_map/ppermute | solution.py:64
  14.1 4.2 %collective-permute-start.6 = (bf16[128,128]{1,0:T(8,128)(2,1)S(1)}, bf16[128,128]{1,0:T(8,128)(2,1)S(1)}, u32[]{:S(2)}, u32[]{:S(2)}) collective-permute-start(bf16[128,128]{1,0:T(8,128)(2,1)S(1)} %get-tuple-element.16), channel_id=1, source_target_pairs={{0,5},{1,4},{2,7},{3,6},{4,1},{5,0},{6,3},{7,2},{8,13},{9,12},{10,... | collective-permute-start | bytes 98312 | tf_op jit(solution)/shard_map/ppermute | solution.py:64
  15.4 3.0 %collective-permute-start.7 = (bf16[128,128]{1,0:T(8,128)(2,1)S(1)}, bf16[128,128]{1,0:T(8,128)(2,1)S(1)}, u32[]{:S(2)}, u32[]{:S(2)}) collective-permute-start(bf16[128,128]{1,0:T(8,128)(2,1)S(1)} %get-tuple-element.17), channel_id=1, source_target_pairs={{0,4},{1,5},{2,6},{3,7},{4,0},{5,1},{6,2},{7,3},{8,12},{9,13},{10,... | collective-permute-start | bytes 98312 | tf_op jit(solution)/shard_map/ppermute | solution.py:64
  18.7 4.6 %collective-permute-start.10 = (bf16[172,128]{1,0:T(8,128)(2,1)S(1)}, bf16[172,128]{1,0:T(8,128)(2,1)S(1)}, u32[]{:S(2)}, u32[]{:S(2)}) collective-permute-start(bf16[172,128]{1,0:T(8,128)(2,1)S(1)} %get-tuple-element.20.refs_0_), channel_id=1, source_target_pairs={{28,0},{24,4},{20,8},{16,12},{12,16},{8,20},{4,24},{0,28},{29,1},{... | collective-permute-start | bytes 132104 | tf_op jit(solution)/shard_map/ppermute | solution.py:40
  19.8 3.9 %collective-permute-start.9 = (bf16[172,128]{1,0:T(8,128)(2,1)S(1)}, bf16[172,128]{1,0:T(8,128)(2,1)S(1)}, u32[]{:S(2)}, u32[]{:S(2)}) collective-permute-start(bf16[172,128]{1,0:T(8,128)(2,1)S(1)} %get-tuple-element.20.refs_0_), channel_id=1, source_target_pairs={{12,0},{16,4},{4,8},{24,12},{28,16},{0,20},{20,24},{8,28},{13,1},{... | collective-permute-start | bytes 132104 | tf_op jit(solution)/shard_map/ppermute | solution.py:40
  20.9 4.0 %collective-permute-start.16 = (bf16[172,128]{1,0:T(8,128)(2,1)S(1)}, bf16[172,128]{1,0:T(8,128)(2,1)S(1)}, u32[]{:S(2)}, u32[]{:S(2)}) collective-permute-start(bf16[172,128]{1,0:T(8,128)(2,1)S(1)} %get-tuple-element.20.refs_0_), channel_id=1, source_target_pairs={{8,0},{20,4},{0,8},{28,12},{24,16},{4,20},{16,24},{12,28},{9,1},{2... | collective-permute-start | bytes 132104 | tf_op jit(solution)/shard_map/ppermute | solution.py:40
  22.0 3.5 %collective-permute-start.13 = (bf16[172,128]{1,0:T(8,128)(2,1)S(1)}, bf16[172,128]{1,0:T(8,128)(2,1)S(1)}, u32[]{:S(2)}, u32[]{:S(2)}) collective-permute-start(bf16[172,128]{1,0:T(8,128)(2,1)S(1)} %get-tuple-element.20.refs_0_), channel_id=1, source_target_pairs={{20,0},{8,4},{28,8},{0,12},{4,16},{24,20},{12,24},{16,28},{21,1},{... | collective-permute-start | bytes 132104 | tf_op jit(solution)/shard_map/ppermute | solution.py:40
  22.4 3.0 %collective-permute-start.12 = (bf16[172,128]{1,0:T(8,128)(2,1)S(1)}, bf16[172,128]{1,0:T(8,128)(2,1)S(1)}, u32[]{:S(2)}, u32[]{:S(2)}) collective-permute-start(bf16[172,128]{1,0:T(8,128)(2,1)S(1)} %get-tuple-element.20.refs_0_), channel_id=1, source_target_pairs={{0,4},{4,0},{8,12},{12,8},{16,20},{20,16},{24,28},{28,24},{1,5},{5... | collective-permute-start | bytes 132104 | tf_op jit(solution)/shard_map/ppermute | solution.py:36
  23.3 2.2 %collective-permute-start.14 = (bf16[172,128]{1,0:T(8,128)(2,1)S(1)}, bf16[172,128]{1,0:T(8,128)(2,1)S(1)}, u32[]{:S(2)}, u32[]{:S(2)}) collective-permute-start(bf16[172,128]{1,0:T(8,128)(2,1)S(1)} %collective-permute-done.10.refs_2_), channel_id=1, source_target_pairs={{0,4},{4,0},{8,12},{12,8},{16,20},{20,16},{24,28},{28,24},{1,5},{5... | collective-permute-start | bytes 132104 | tf_op jit(solution)/shard_map/ppermute | solution.py:36
  23.7 1.8 %collective-permute-start.15 = (bf16[172,128]{1,0:T(8,128)(2,1)S(1)}, bf16[172,128]{1,0:T(8,128)(2,1)S(1)}, u32[]{:S(2)}, u32[]{:S(2)}) collective-permute-start(bf16[172,128]{1,0:T(8,128)(2,1)S(1)} %collective-permute-done.9.refs_1_), channel_id=1, source_target_pairs={{0,4},{4,0},{8,12},{12,8},{16,20},{20,16},{24,28},{28,24},{1,5},{5... | collective-permute-start | bytes 132104 | tf_op jit(solution)/shard_map/ppermute | solution.py:36
  25.0 5.3 %collective-permute-start.11 = (bf16[128,256]{1,0:T(8,128)(2,1)S(1)}, bf16[128,256]{1,0:T(8,128)(2,1)S(1)}, u32[]{:S(2)}, u32[]{:S(2)}) collective-permute-start(bf16[128,256]{1,0:T(8,128)(2,1)S(1)} %shard_map.120), channel_id=1, source_target_pairs={{0,4},{4,0},{8,12},{12,8},{16,20},{20,16},{24,28},{28,24},{1,5},{5... | collective-permute-start | bytes 196616 | tf_op jit(solution)/shard_map/ppermute | solution.py:36
  25.8 6.1 %collective-permute-start.17 = (bf16[172,128]{1,0:T(8,128)(2,1)S(1)}, bf16[172,128]{1,0:T(8,128)(2,1)S(1)}, u32[]{:S(2)}, u32[]{:S(2)}) collective-permute-start(bf16[172,128]{1,0:T(8,128)(2,1)S(1)} %get-tuple-element.22), channel_id=1, source_target_pairs={{0,3},{1,2},{2,1},{3,0},{4,7},{5,6},{6,5},{7,4},{8,11},{9,10},{10,... | collective-permute-start | bytes 132104 | tf_op jit(solution)/shard_map/ppermute | solution.py:36
  28.6 4.9 %collective-permute-start.18 = (bf16[172,128]{1,0:T(8,128)(2,1)S(1)}, bf16[172,128]{1,0:T(8,128)(2,1)S(1)}, u32[]{:S(2)}, u32[]{:S(2)}) collective-permute-start(bf16[172,128]{1,0:T(8,128)(2,1)S(1)} %get-tuple-element.23), channel_id=1, source_target_pairs={{0,2},{1,3},{2,0},{3,1},{4,6},{5,7},{6,4},{7,5},{8,10},{9,11},{10,... | collective-permute-start | bytes 132104 | tf_op jit(solution)/shard_map/ppermute | solution.py:36
  28.6 4.9 %collective-permute-start.19 = (bf16[172,128]{1,0:T(8,128)(2,1)S(1)}, bf16[172,128]{1,0:T(8,128)(2,1)S(1)}, u32[]{:S(2)}, u32[]{:S(2)}) collective-permute-start(bf16[172,128]{1,0:T(8,128)(2,1)S(1)} %get-tuple-element.24), channel_id=1, source_target_pairs={{0,1},{1,0},{2,3},{3,2},{4,5},{5,4},{6,7},{7,6},{8,9},{9,8},{10,11... | collective-permute-start | bytes 132104 | tf_op jit(solution)/shard_map/ppermute | solution.py:36
  (3 other events, 26.6 us)
where the time goes:
time: 34.6 us; the launch traced here: 34.3 us
  starting transfers between devices  20.4 us (59%)
  waiting for transfers between devices  7.77 us (22%)
  Pallas kernels  4.62 us (13%)
  between operations  1.46 us (4%)
    ppermute x7, starting transfers between devices, fetched(): lax.ppermute(block, axis, [(partner(i, seen(slot, i)), i) for i in range(...  8.9 us
    ppermute x9, starting transfers between devices, permuted(): lax.ppermute(block, axis, [(i, partner(i, slot)) for i in range(size)])  7.21 us
    pallas_call x11, Pallas kernels, call(): pl.pallas_call(kernel, out_shape=out_shape, in_specs=specs or [vmem] * le...  4.62 us
    ppermute x4, starting transfers between devices, send_across(): arrived.append(lax.ppermute(blocks[slot], ('row', 'col'), pairs))  4.3 us
    ppermute x9, waiting for transfers between devices, permuted(): lax.ppermute(block, axis, [(i, partner(i, slot)) for i in range(size)])  3.11 us
    ppermute x4, waiting for transfers between devices, send_across(): arrived.append(lax.ppermute(blocks[slot], ('row', 'col'), pairs))  2.8 us
    ppermute x7, waiting for transfers between devices, fetched(): lax.ppermute(block, axis, [(partner(i, seen(slot, i)), i) for i in range(...  1.86 us
  transfers between devices with their start and end apart: 20, of which 9 were waited for; matrix products, arithmetic and copies ran while one was open for 0% of the time, Pallas kernels for 10%

commit v1 on v0

--- a/solution.py
+++ b/solution.py
@@ -155,19 +155,28 @@
     out[...] = jnp.dot(dense_ref[:, :half], mine_ref[...], preferred_element_type=F32)
 
 
-def layer_one_kernel(dense_ref, first_ref, other_ref, *outputs):
-    half, block = other_ref.shape[0], dense_ref.shape[0] // len(outputs)
-    total = first_ref[...] + jnp.dot(
-        dense_ref[:, half:], other_ref[...], preferred_element_type=F32
-    )
-    for k, out in enumerate(outputs):
-        out[...] = total[k * block : (k + 1) * block, :].astype(BF16)
-
-
-def hidden_kernel(n_col, *refs):
-    parts = refs[:n_col]
-    feats, w_one, b_one, w_two, kept, pushed_ref, proj_ref = refs[n_col:]
-    total = feats[: kept.shape[0], :].astype(F32)
+def layer_one_kernel(slots, dense_ref, first_ref, other_ref, *refs):
+    outputs = refs[-len(slots) :]
+    half, block = other_ref.shape[0], outputs[0].shape[0]
+    at = slice(slots[0] * block, (slots[-1] + 1) * block)
+    total = first_ref[at, :] + jnp.dot(
+        dense_ref[at, half:], other_ref[...], preferred_element_type=F32
+    )
+    for i, out in enumerate(outputs):
+        out[...] = total[i * block : (i + 1) * block, :].astype(BF16)
+
+
+def begin_kernel(base, *refs):
+    total = base[: refs[-1].shape[0], :].astype(F32)
+    for ref in refs[:-1]:
+        total += ref[...].astype(F32)
+    refs[-1][...] = total
+
+
+def hidden_kernel(begun, *refs):
+    parts = refs[:-6]
+    w_one, b_one, w_two, kept, pushed_ref, proj_ref = refs[-6:]
+    total = begun[...]
     for part in parts:
         total += part[...].astype(F32)
     pre = jnp.dot(total.astype(BF16), w_one[...], preferred_element_type=F32) + b_one[...]
@@ -202,24 +211,29 @@
     )
 
 
-def layer_two_kernel(n_col, dense_ref, first_ref, own_ref, near_ref, *refs):
-    blocks, outputs, scratch = refs[: -n_col - 1], refs[-n_col - 1 : -1], refs[-1]
-    block, half = near_ref.shape[1], scratch.shape[1]
-    rest = lanes([own_ref, *blocks], scratch)
-    total = first_ref[...] + dot_nt(rest, dense_ref[:, :half])
-    total += dot_nt(near_ref[...], dense_ref[:, dense_ref.shape[1] - block :])
-    for k, out in enumerate(outputs):
-        out[...] = total[:, k * block : (k + 1) * block].astype(BF16)
-
-
-def logits_kernel(n_col, pieces, *refs):
-    parts = refs[:n_col]
-    proj, bias, out_hbm, staged, sems = refs[n_col:]
+def layer_two_kernel(slots, dense_ref, first_ref, near_ref, rest_ref, *refs):
+    outputs = refs[-len(slots) :]
+    block, half = near_ref.shape[1], rest_ref.shape[1]
+    at = slice(slots[0] * block, (slots[-1] + 1) * block)
+    total = first_ref[:, at] + dot_nt(rest_ref[...], dense_ref[at, :half])
+    total += dot_nt(near_ref[...], dense_ref[at, dense_ref.shape[1] - block :])
+    for i, out in enumerate(outputs):
+        out[...] = total[:, i * block : (i + 1) * block].astype(BF16)
+
+
+def farthest_two_kernel(slot, dense_ref, first_ref, own_ref, near_ref, *refs):
+    blocks, (out, rest) = refs[:-2], refs[-2:]
+    lanes([own_ref, *blocks], rest)
+    layer_two_kernel([slot], dense_ref, first_ref, near_ref, rest, out)
+
+
+def logits_kernel(pieces, begun, *refs):
+    parts, (out_hbm, staged, sems) = refs[:-3], refs[-3:]
     step = -(-staged.shape[0] // pieces // 16) * 16
     copies = []
     for i in range(pieces):
         rows = slice(i * step, (i + 1) * step if i < pieces - 1 else staged.shape[0])
-        total = proj[rows, :].astype(F32) + bias[rows, :]
+        total = begun[rows, :]
         for part in parts:
             total += part[rows, :].astype(F32)
         staged[rows, 0, :] = total
@@ -311,11 +325,19 @@
         other_one = fetch_core(mine_one, "row", n_row)
         kept, bias_cols = prepare(mine_one)
         half_one = call(half_one_kernel, shape((n_col * block, f_in), F32), (dense, mine_one))
-        parts_one = call(
-            layer_one_kernel,
-            [shape((block, f_in), BF16)] * n_col,
+        far, others = n_col - 1, range(1, n_col - 1)
+        far_one = call(
+            functools.partial(layer_one_kernel, [far]),
+            [shape((block, f_in), BF16)],
             (dense, half_one, other_one),
         )
+        near_one = call(
+            functools.partial(layer_one_kernel, range(far)),
+            [shape((block, f_in), BF16)] * far,
+            (dense, half_one, other_one, *far_one),
+            specs=[vmem] * 3 + [anywhere],
+        )
+        parts_one = [*near_one, *far_one]
     else:
         kept, bias_cols = prepare()
         summed = call(
@@ -330,10 +352,13 @@
 
     arrived_one = send_across(parts_one, n_row, n_col)
     kept = fetch_core(kept, "row", n_row)
+    begun_one = call(
+        begin_kernel, shape((block, f_in), F32), (other_one, arrived_one[0])
+    )
     pushed, proj = call(
-        functools.partial(hidden_kernel, n_col),
+        hidden_kernel,
         (shape((block, hid), BF16), shape((classes, block), BF16)),
-        (*arrived_one, other_one, weight_one, bias_one[None], w_two_t, kept),
+        (begun_one, *arrived_one[1:], weight_one, bias_one[None], w_two_t, kept),
     )
     chips_two = [proj, *fetch_chips(proj, "row", n_row)]
     if dense_form:
@@ -357,12 +382,23 @@
         pushed = call(
             late_kernel, shape((block, hid), BF16), (pushed, half_two), specs=[vmem, anywhere]
         )
-        parts_two = call(
-            functools.partial(layer_two_kernel, n_col),
-            [shape((classes, block), BF16)] * n_col,
+        far_two, rest = call(
+            functools.partial(farthest_two_kernel, far),
+            [shape((classes, block), BF16), shape((classes, len(late) * block), BF16)],
             (dense, half_two, late[0], near, *late[1:]),
-            scratch=[pltpu.VMEM((classes, len(late) * block), BF16)],
-        )
+        )
+        middle_two = call(
+            functools.partial(layer_two_kernel, others),
+            [shape((classes, block), BF16)] * len(others),
+            (dense, half_two, near, rest),
+        )
+        own_two = call(
+            functools.partial(layer_two_kernel, [0]),
+            [shape((classes, block), BF16)],
+            (dense, half_two, near, rest, middle_two[0]),
+            specs=[vmem] * 4 + [anywhere],
+        )
+        parts_two = [*own_two, *middle_two, far_two]
     else:
         other_slots = jnp.arange(n_row) ^ 1
         summed = call(
@@ -377,10 +413,15 @@
     arrived_two = send_each(parts_two, "col", n_col)
     pushed = call(write_kernel, shape((block, hid), BF16), (fetch_core(pushed, "row", n_row),))
     pieces = 4
+    begun_two = call(
+        begin_kernel,
+        shape((classes, block), F32),
+        (bias_cols, own_proj, parts_two[0], arrived_two[0]),
+    )
     scores = call(
-        functools.partial(logits_kernel, n_col, pieces),
+        functools.partial(logits_kernel, pieces),
         shape((classes, 1, block), F32),
-        (parts_two[0], *arrived_two, own_proj, bias_cols),
+        (begun_two, *arrived_two[1:]),
         scratch=[pltpu.VMEM((classes, 1, block), F32), pltpu.SemaphoreType.DMA((pieces,))],
         out_specs=pl.BlockSpec(memory_space=pl.ANY),
     )

time: 34.6 us -> 34.7 us (level)
  Pallas kernels: 4.62 us -> 5.23 us
  waiting for transfers between devices: 7.77 us -> 7.31 us
    ppermute x4, waiting for transfers between devices: 2.8 us -> 3.54 us  [send_across(): arrived.append(lax.ppermute(blocks[slot], ('row', 'col'), pairs))]
    ppermute x9, waiting for transfers between devices: 3.11 us -> 2.49 us  [permuted(): lax.ppermute(block, axis, [(i, partner(i, slot)) for i in range(size)])]
    pallas_call x11 -> x16, Pallas kernels: 4.62 us -> 5.23 us  [call(): pl.pallas_call(kernel, out_shape=out_shape, in_specs=specs or [vmem] * le...]
    ppermute x7, waiting for transfers between devices: 1.86 us -> 1.28 us  [fetched(): lax.ppermute(block, axis, [(partner(i, seen(slot, i)), i) for i in range(...]
  transfers between devices with their start and end apart: 20 -> 20, of which waited for: 9 -> 8; matrix products, arithmetic and copies ran while one was open for 0% -> 0% of each run, Pallas kernels for 10% -> 12%
where the time goes in v1:
time: 34.7 us; the launch traced here: 34.4 us
  starting transfers between devices  20.3 us (59%)
  waiting for transfers between devices  7.31 us (21%)
  Pallas kernels  5.23 us (15%)
  between operations  1.52 us (4%)
    ppermute x7, starting transfers between devices, fetched(): lax.ppermute(block, axis, [(partner(i, seen(slot, i)), i) for i in range(...  8.62 us
    ppermute x9, starting transfers between devices, permuted(): lax.ppermute(block, axis, [(i, partner(i, slot)) for i in range(size)])  7.33 us
    pallas_call x16, Pallas kernels, call(): pl.pallas_call(kernel, out_shape=out_shape, in_specs=specs or [vmem] * le...  5.23 us
    ppermute x4, starting transfers between devices, send_across(): arrived.append(lax.ppermute(blocks[slot], ('row', 'col'), pairs))  4.37 us
    ppermute x4, waiting for transfers between devices, send_across(): arrived.append(lax.ppermute(blocks[slot], ('row', 'col'), pairs))  3.54 us
    ppermute x9, waiting for transfers between devices, permuted(): lax.ppermute(block, axis, [(i, partner(i, slot)) for i in range(size)])  2.49 us
    ppermute x7, waiting for transfers between devices, fetched(): lax.ppermute(block, axis, [(partner(i, seen(slot, i)), i) for i in range(...  1.28 us
  transfers between devices with their start and end apart: 20, of which 8 were waited for; matrix products, arithmetic and copies ran while one was open for 0% of the time, Pallas kernels for 12%

profile of v1, /device:TPU:0, one launch (start us, length us, event | category | flops | bytes accessed | tf_op | source)
XLA Modules:
  0.0 34.4 jit_solution(17323022706207344615)
XLA Ops:
  0.7 3.4 %collective-permute-start.2 = (bf16[128,128]{1,0:T(8,128)(2,1)}, bf16[128,128]{1,0:T(8,128)(2,1)S(1)}, u32[]{:S(2)}, u32[]{:S(2)}) collective-permute-start(bf16[128,128]{1,0:T(8,128)(2,1)} %bitcast.18), channel_id=1, source_target_pairs={{28,0},{24,4},{20,8},{16,12},{12,16},{8,20},{4,24},{0,28},{29,1},{... | collective-permute-start | bytes 98312 | tf_op jit(solution)/shard_map/ppermute | solution.py:40
  4.1 0.8 %collective-permute-start.1 = (bf16[128,128]{1,0:T(8,128)(2,1)}, bf16[128,128]{1,0:T(8,128)(2,1)S(1)}, u32[]{:S(2)}, u32[]{:S(2)}) collective-permute-start(bf16[128,128]{1,0:T(8,128)(2,1)} %bitcast.19), channel_id=1, source_target_pairs={{12,0},{16,4},{4,8},{24,12},{28,16},{0,20},{20,24},{8,28},{13,1},{... | collective-permute-start | bytes 98312 | tf_op jit(solution)/shard_map/ppermute | solution.py:40
  4.9 1.0 %collective-permute-start = (bf16[128,128]{1,0:T(8,128)(2,1)}, bf16[128,128]{1,0:T(8,128)(2,1)S(1)}, u32[]{:S(2)}, u32[]{:S(2)}) collective-permute-start(bf16[128,128]{1,0:T(8,128)(2,1)} %bitcast.20), channel_id=1, source_target_pairs={{20,0},{8,4},{28,8},{0,12},{4,16},{24,20},{12,24},{16,28},{21,1},{... | collective-permute-start | bytes 98312 | tf_op jit(solution)/shard_map/ppermute | solution.py:40
  6.5 1.6 %shard_map.113.refs_4_.dense_ref = bf16[512,1024]{1,0:T(8,128)(2,1)S(1)} custom-call(s32[1,1]{1,0:T(1,128)S(6)} %copy.13.count, s32[2,128]{1,0:T(2,128)} %bitcast.28, bf16[128,128,128]{2,1,0:T(8,128)(2,1)} %bitcast.25), custom_call_target="tpu_custom_call" | custom-call | flops 2097152 | bytes 4194304 | tf_op jit(solution)/shard_map/pallas_call | solution.py:74
  8.2 0.5 %collective-permute-done.refs_1_ = bf16[128,128]{1,0:T(8,128)(2,1)S(1)} collective-permute-done((bf16[128,128]{1,0:T(8,128)(2,1)}, bf16[128,128]{1,0:T(8,128)(2,1)S(1)}, u32[]{:S(2)}, u32[]{:S(2)}) %collective-permute-start) | collective-permute-done | bytes 32800 | tf_op jit(solution)/shard_map/ppermute | solution.py:40
  9.0 0.5 %collective-permute-start.8 = (bf16[128,256]{1,0:T(8,128)(2,1)S(1)}, bf16[128,256]{1,0:T(8,128)(2,1)S(1)}, u32[]{:S(2)}, u32[]{:S(2)}) collective-permute-start(bf16[128,256]{1,0:T(8,128)(2,1)S(1)} %get-tuple-element.16), channel_id=1, source_target_pairs={{0,4},{4,0},{8,12},{12,8},{16,20},{20,16},{24,28},{28,24},{1,5},{5... | collective-permute-start | bytes 196616 | tf_op jit(solution)/shard_map/ppermute | solution.py:36
  9.8 0.3 %collective-permute-done.3.other_ref.base = bf16[512,128]{1,0:T(8,128)(2,1)S(1)} collective-permute-done((bf16[512,128]{1,0:T(8,128)(2,1)S(1)}, bf16[512,128]{1,0:T(8,128)(2,1)S(1)}, u32[]{:S(2)}, u32[]{:S(2)}) %collective-permute-start.3) | collective-permute-done | bytes 131104 | tf_op jit(solution)/shard_map/ppermute | solution.py:36
  10.3 3.6 %collective-permute-start.4 = (bf16[128,128]{1,0:T(8,128)(2,1)S(1)}, bf16[128,128]{1,0:T(8,128)(2,1)S(1)}, u32[]{:S(2)}, u32[]{:S(2)}) collective-permute-start(bf16[128,128]{1,0:T(8,128)(2,1)S(1)} %shard_map.116.refs_0_), channel_id=1, source_target_pairs={{0,7},{1,6},{2,5},{3,4},{4,3},{5,2},{6,1},{7,0},{8,15},{9,14},{10,... | collective-permute-start | bytes 98312 | tf_op jit(solution)/shard_map/ppermute | solution.py:64
  14.6 0.3 %collective-permute-start.7 = (bf16[128,128]{1,0:T(8,128)(2,1)S(1)}, bf16[128,128]{1,0:T(8,128)(2,1)S(1)}, u32[]{:S(2)}, u32[]{:S(2)}) collective-permute-start(bf16[128,128]{1,0:T(8,128)(2,1)S(1)} %get-tuple-element.15), channel_id=1, source_target_pairs={{0,4},{1,5},{2,6},{3,7},{4,0},{5,1},{6,2},{7,3},{8,12},{9,13},{10,... | collective-permute-start | bytes 98312 | tf_op jit(solution)/shard_map/ppermute | solution.py:64
  14.9 0.7 %collective-permute-done.4.refs_0_ = bf16[128,128]{1,0:T(8,128)(2,1)S(1)} collective-permute-done((bf16[128,128]{1,0:T(8,128)(2,1)S(1)}, bf16[128,128]{1,0:T(8,128)(2,1)S(1)}, u32[]{:S(2)}, u32[]{:S(2)}) %collective-permute-start.4) | collective-permute-done | bytes 32800 | tf_op jit(solution)/shard_map/ppermute | solution.py:64
  15.7 2.8 %collective-permute-done.5.refs_0_ = bf16[128,128]{1,0:T(8,128)(2,1)S(1)} collective-permute-done((bf16[128,128]{1,0:T(8,128)(2,1)S(1)}, bf16[128,128]{1,0:T(8,128)(2,1)S(1)}, u32[]{:S(2)}, u32[]{:S(2)}) %collective-permute-start.5) | collective-permute-done | bytes 32800 | tf_op jit(solution)/shard_map/ppermute | solution.py:64
  18.9 1.1 %collective-permute-start.10 = (bf16[172,128]{1,0:T(8,128)(2,1)S(1)}, bf16[172,128]{1,0:T(8,128)(2,1)S(1)}, u32[]{:S(2)}, u32[]{:S(2)}) collective-permute-start(bf16[172,128]{1,0:T(8,128)(2,1)S(1)} %get-tuple-element.18.refs_0_), channel_id=1, source_target_pairs={{28,0},{24,4},{20,8},{16,12},{12,16},{8,20},{4,24},{0,28},{29,1},{... | collective-permute-start | bytes 132104 | tf_op jit(solution)/shard_map/ppermute | solution.py:40
  20.0 0.8 %collective-permute-start.9 = (bf16[172,128]{1,0:T(8,128)(2,1)S(1)}, bf16[172,128]{1,0:T(8,128)(2,1)S(1)}, u32[]{:S(2)}, u32[]{:S(2)}) collective-permute-start(bf16[172,128]{1,0:T(8,128)(2,1)S(1)} %get-tuple-element.18.refs_0_), channel_id=1, source_target_pairs={{12,0},{16,4},{4,8},{24,12},{28,16},{0,20},{20,24},{8,28},{13,1},{... | collective-permute-start | bytes 132104 | tf_op jit(solution)/shard_map/ppermute | solution.py:40
  20.8 1.3 %collective-permute-start.16 = (bf16[172,128]{1,0:T(8,128)(2,1)S(1)}, bf16[172,128]{1,0:T(8,128)(2,1)S(1)}, u32[]{:S(2)}, u32[]{:S(2)}) collective-permute-start(bf16[172,128]{1,0:T(8,128)(2,1)S(1)} %get-tuple-element.18.refs_0_), channel_id=1, source_target_pairs={{8,0},{20,4},{0,8},{28,12},{24,16},{4,20},{16,24},{12,28},{9,1},{2... | collective-permute-start | bytes 132104 | tf_op jit(solution)/shard_map/ppermute | solution.py:40
  22.3 1.0 %collective-permute-start.12 = (bf16[172,128]{1,0:T(8,128)(2,1)S(1)}, bf16[172,128]{1,0:T(8,128)(2,1)S(1)}, u32[]{:S(2)}, u32[]{:S(2)}) collective-permute-start(bf16[172,128]{1,0:T(8,128)(2,1)S(1)} %get-tuple-element.18.refs_0_), channel_id=1, source_target_pairs={{0,4},{4,0},{8,12},{12,8},{16,20},{20,16},{24,28},{28,24},{1,5},{5... | collective-permute-start | bytes 132104 | tf_op jit(solution)/shard_map/ppermute | solution.py:36
  23.4 0.5 %collective-permute-start.14 = (bf16[172,128]{1,0:T(8,128)(2,1)S(1)}, bf16[172,128]{1,0:T(8,128)(2,1)S(1)}, u32[]{:S(2)}, u32[]{:S(2)}) collective-permute-start(bf16[172,128]{1,0:T(8,128)(2,1)S(1)} %collective-permute-done.10.refs_2_), channel_id=1, source_target_pairs={{0,4},{4,0},{8,12},{12,8},{16,20},{20,16},{24,28},{28,24},{1,5},{5... | collective-permute-start | bytes 132104 | tf_op jit(solution)/shard_map/ppermute | solution.py:36
  23.9 0.6 %collective-permute-start.15 = (bf16[172,128]{1,0:T(8,128)(2,1)S(1)}, bf16[172,128]{1,0:T(8,128)(2,1)S(1)}, u32[]{:S(2)}, u32[]{:S(2)}) collective-permute-start(bf16[172,128]{1,0:T(8,128)(2,1)S(1)} %collective-permute-done.9.refs_1_), channel_id=1, source_target_pairs={{0,4},{4,0},{8,12},{12,8},{16,20},{20,16},{24,28},{28,24},{1,5},{5... | collective-permute-start | bytes 132104 | tf_op jit(solution)/shard_map/ppermute | solution.py:36
  25.0 0.7 %collective-permute-done.13.near_ref = bf16[172,128]{1,0:T(8,128)(2,1)S(1)} collective-permute-done((bf16[172,128]{1,0:T(8,128)(2,1)S(1)}, bf16[172,128]{1,0:T(8,128)(2,1)S(1)}, u32[]{:S(2)}, u32[]{:S(2)}) %collective-permute-start.13) | collective-permute-done | bytes 44064 | tf_op jit(solution)/shard_map/ppermute | solution.py:40
  25.9 2.1 %collective-permute-start.17 = (bf16[172,128]{1,0:T(8,128)(2,1)S(1)}, bf16[172,128]{1,0:T(8,128)(2,1)S(1)}, u32[]{:S(2)}, u32[]{:S(2)}) collective-permute-start(bf16[172,128]{1,0:T(8,128)(2,1)S(1)} %get-tuple-element.22), channel_id=1, source_target_pairs={{0,3},{1,2},{2,1},{3,0},{4,7},{5,6},{6,5},{7,4},{8,11},{9,10},{10,... | collective-permute-start | bytes 132104 | tf_op jit(solution)/shard_map/ppermute | solution.py:36
  28.3 2.4 %collective-permute-start.19 = (bf16[172,128]{1,0:T(8,128)(2,1)S(1)}, bf16[172,128]{1,0:T(8,128)(2,1)S(1)}, u32[]{:S(2)}, u32[]{:S(2)}) collective-permute-start(bf16[172,128]{1,0:T(8,128)(2,1)S(1)} %get-tuple-element.21.refs_0_), channel_id=1, source_target_pairs={{0,1},{1,0},{2,3},{3,2},{4,5},{5,4},{6,7},{7,6},{8,9},{9,8},{10,11... | collective-permute-start | bytes 132104 | tf_op jit(solution)/shard_map/ppermute | solution.py:36
  30.9 0.6 %shard_map.123 = bf16[128,256]{1,0:T(8,128)(2,1)} custom-call(bf16[128,256]{1,0:T(8,128)(2,1)S(1)} %collective-permute-done.11.value), custom_call_target="tpu_custom_call" | custom-call | tf_op jit(solution)/shard_map/pallas_call | solution.py:74
  31.6 0.5 %collective-permute-done.17.refs_2_ = bf16[172,128]{1,0:T(8,128)(2,1)S(1)} collective-permute-done((bf16[172,128]{1,0:T(8,128)(2,1)S(1)}, bf16[172,128]{1,0:T(8,128)(2,1)S(1)}, u32[]{:S(2)}, u32[]{:S(2)}) %collective-permute-start.17) | collective-permute-done | bytes 44064 | tf_op jit(solution)/shard_map/ppermute | solution.py:36
  32.1 1.6 %collective-permute-done.18.refs_0_ = bf16[172,128]{1,0:T(8,128)(2,1)S(1)} collective-permute-done((bf16[172,128]{1,0:T(8,128)(2,1)S(1)}, bf16[172,128]{1,0:T(8,128)(2,1)S(1)}, u32[]{:S(2)}, u32[]{:S(2)}) %collective-permute-start.18) | collective-permute-done | bytes 44064 | tf_op jit(solution)/shard_map/ppermute | solution.py:36
  33.7 0.7 %shard_map.128 = f32[172,1,128]{2,1,0:T(1,128)} custom-call(f32[172,128]{1,0:T(8,128)S(1)} %shard_map.127.begun, bf16[172,128]{1,0:T(8,128)(2,1)S(1)} %collective-permute-done.18.refs_0_, bf16[172,128]{1,0:T(8,128)(2,1)S(1)} %collective-permute-done.19.refs_1_), custom_call_target="tpu_custom_call" | custom-call | tf_op jit(solution)/shard_map/pallas_call | solution.py:74
  (46 shorter events, 3.3 us)
Async XLA Ops:
  0.6 8.3 %copy-start.4 = (f32[172]{0:T(256)S(1)}, f32[172]{0:T(256)}, u32[]{:S(2)}) copy-start(f32[172]{0:T(256)} %param.19) | copy-start | bytes 2068
  0.7 7.5 %collective-permute-start.2 = (bf16[128,128]{1,0:T(8,128)(2,1)}, bf16[128,128]{1,0:T(8,128)(2,1)S(1)}, u32[]{:S(2)}, u32[]{:S(2)}) collective-permute-start(bf16[128,128]{1,0:T(8,128)(2,1)} %bitcast.18), channel_id=1, source_target_pairs={{28,0},{24,4},{20,8},{16,12},{12,16},{8,20},{4,24},{0,28},{29,1},{... | collective-permute-start | bytes 98312 | tf_op jit(solution)/shard_map/ppermute | solution.py:40
  4.1 4.1 %collective-permute-start.1 = (bf16[128,128]{1,0:T(8,128)(2,1)}, bf16[128,128]{1,0:T(8,128)(2,1)S(1)}, u32[]{:S(2)}, u32[]{:S(2)}) collective-permute-start(bf16[128,128]{1,0:T(8,128)(2,1)} %bitcast.19), channel_id=1, source_target_pairs={{12,0},{16,4},{4,8},{24,12},{28,16},{0,20},{20,24},{8,28},{13,1},{... | collective-permute-start | bytes 98312 | tf_op jit(solution)/shard_map/ppermute | solution.py:40
  4.9 3.8 %collective-permute-start = (bf16[128,128]{1,0:T(8,128)(2,1)}, bf16[128,128]{1,0:T(8,128)(2,1)S(1)}, u32[]{:S(2)}, u32[]{:S(2)}) collective-permute-start(bf16[128,128]{1,0:T(8,128)(2,1)} %bitcast.20), channel_id=1, source_target_pairs={{20,0},{8,4},{28,8},{0,12},{4,16},{24,20},{12,24},{16,28},{21,1},{... | collective-permute-start | bytes 98312 | tf_op jit(solution)/shard_map/ppermute | solution.py:40
  8.1 10.4 %copy-start = (bf16[256,172]{0,1:T(8,128)(2,1)S(1)}, bf16[256,172]{0,1:T(8,128)(2,1)}, u32[]{:S(2)}) copy-start(bf16[256,172]{0,1:T(8,128)(2,1)} %param.18) | copy-start | bytes 264196
  8.1 10.4 %copy-start.2 = (bf16[128,256]{1,0:T(8,128)(2,1)S(1)}, bf16[128,256]{1,0:T(8,128)(2,1)}, u32[]{:S(2)}) copy-start(bf16[128,256]{1,0:T(8,128)(2,1)} %refs_3_.1) | copy-start | bytes 196612
  8.2 10.4 %copy-start.5 = (f32[256]{0:T(256)S(1)}, f32[256]{0:T(256)}, u32[]{:S(2)}) copy-start(f32[256]{0:T(256)} %param.17) | copy-start | bytes 3076
  8.7 1.4 %collective-permute-start.3 = (bf16[512,128]{1,0:T(8,128)(2,1)S(1)}, bf16[512,128]{1,0:T(8,128)(2,1)S(1)}, u32[]{:S(2)}, u32[]{:S(2)}) collective-permute-start(bf16[512,128]{1,0:T(8,128)(2,1)S(1)} %shard_map.114.mine_ref.refs_0_), channel_id=1, source_target_pairs={{0,4},{4,0},{8,12},{12,8},{16,20},{20,16},{24,28},{28,24},{1,5},{5... | collective-permute-start | bytes 393224 | tf_op jit(solution)/shard_map/ppermute | solution.py:36
  9.0 6.7 %collective-permute-start.8 = (bf16[128,256]{1,0:T(8,128)(2,1)S(1)}, bf16[128,256]{1,0:T(8,128)(2,1)S(1)}, u32[]{:S(2)}, u32[]{:S(2)}) collective-permute-start(bf16[128,256]{1,0:T(8,128)(2,1)S(1)} %get-tuple-element.16), channel_id=1, source_target_pairs={{0,4},{4,0},{8,12},{12,8},{16,20},{20,16},{24,28},{28,24},{1,5},{5... | collective-permute-start | bytes 196616 | tf_op jit(solution)/shard_map/ppermute | solution.py:36
  10.3 5.4 %collective-permute-start.4 = (bf16[128,128]{1,0:T(8,128)(2,1)S(1)}, bf16[128,128]{1,0:T(8,128)(2,1)S(1)}, u32[]{:S(2)}, u32[]{:S(2)}) collective-permute-start(bf16[128,128]{1,0:T(8,128)(2,1)S(1)} %shard_map.116.refs_0_), channel_id=1, source_target_pairs={{0,7},{1,6},{2,5},{3,4},{4,3},{5,2},{6,1},{7,0},{8,15},{9,14},{10,... | collective-permute-start | bytes 98312 | tf_op jit(solution)/shard_map/ppermute | solution.py:64
  14.2 4.3 %collective-permute-start.5 = (bf16[128,128]{1,0:T(8,128)(2,1)S(1)}, bf16[128,128]{1,0:T(8,128)(2,1)S(1)}, u32[]{:S(2)}, u32[]{:S(2)}) collective-permute-start(bf16[128,128]{1,0:T(8,128)(2,1)S(1)} %get-tuple-element.13), channel_id=1, source_target_pairs={{0,6},{1,7},{2,4},{3,5},{4,2},{5,3},{6,0},{7,1},{8,14},{9,15},{10,... | collective-permute-start | bytes 98312 | tf_op jit(solution)/shard_map/ppermute | solution.py:64
  14.3 4.2 %collective-permute-start.6 = (bf16[128,128]{1,0:T(8,128)(2,1)S(1)}, bf16[128,128]{1,0:T(8,128)(2,1)S(1)}, u32[]{:S(2)}, u32[]{:S(2)}) collective-permute-start(bf16[128,128]{1,0:T(8,128)(2,1)S(1)} %get-tuple-element.14), channel_id=1, source_target_pairs={{0,5},{1,4},{2,7},{3,6},{4,1},{5,0},{6,3},{7,2},{8,13},{9,12},{10,... | collective-permute-start | bytes 98312 | tf_op jit(solution)/shard_map/ppermute | solution.py:64
  14.6 3.9 %collective-permute-start.7 = (bf16[128,128]{1,0:T(8,128)(2,1)S(1)}, bf16[128,128]{1,0:T(8,128)(2,1)S(1)}, u32[]{:S(2)}, u32[]{:S(2)}) collective-permute-start(bf16[128,128]{1,0:T(8,128)(2,1)S(1)} %get-tuple-element.15), channel_id=1, source_target_pairs={{0,4},{1,5},{2,6},{3,7},{4,0},{5,1},{6,2},{7,3},{8,12},{9,13},{10,... | collective-permute-start | bytes 98312 | tf_op jit(solution)/shard_map/ppermute | solution.py:64
  18.9 4.6 %collective-permute-start.10 = (bf16[172,128]{1,0:T(8,128)(2,1)S(1)}, bf16[172,128]{1,0:T(8,128)(2,1)S(1)}, u32[]{:S(2)}, u32[]{:S(2)}) collective-permute-start(bf16[172,128]{1,0:T(8,128)(2,1)S(1)} %get-tuple-element.18.refs_0_), channel_id=1, source_target_pairs={{28,0},{24,4},{20,8},{16,12},{12,16},{8,20},{4,24},{0,28},{29,1},{... | collective-permute-start | bytes 132104 | tf_op jit(solution)/shard_map/ppermute | solution.py:40
  20.0 3.9 %collective-permute-start.9 = (bf16[172,128]{1,0:T(8,128)(2,1)S(1)}, bf16[172,128]{1,0:T(8,128)(2,1)S(1)}, u32[]{:S(2)}, u32[]{:S(2)}) collective-permute-start(bf16[172,128]{1,0:T(8,128)(2,1)S(1)} %get-tuple-element.18.refs_0_), channel_id=1, source_target_pairs={{12,0},{16,4},{4,8},{24,12},{28,16},{0,20},{20,24},{8,28},{13,1},{... | collective-permute-start | bytes 132104 | tf_op jit(solution)/shard_map/ppermute | solution.py:40
  20.8 4.0 %collective-permute-start.16 = (bf16[172,128]{1,0:T(8,128)(2,1)S(1)}, bf16[172,128]{1,0:T(8,128)(2,1)S(1)}, u32[]{:S(2)}, u32[]{:S(2)}) collective-permute-start(bf16[172,128]{1,0:T(8,128)(2,1)S(1)} %get-tuple-element.18.refs_0_), channel_id=1, source_target_pairs={{8,0},{20,4},{0,8},{28,12},{24,16},{4,20},{16,24},{12,28},{9,1},{2... | collective-permute-start | bytes 132104 | tf_op jit(solution)/shard_map/ppermute | solution.py:40
  22.1 3.5 %collective-permute-start.13 = (bf16[172,128]{1,0:T(8,128)(2,1)S(1)}, bf16[172,128]{1,0:T(8,128)(2,1)S(1)}, u32[]{:S(2)}, u32[]{:S(2)}) collective-permute-start(bf16[172,128]{1,0:T(8,128)(2,1)S(1)} %get-tuple-element.18.refs_0_), channel_id=1, source_target_pairs={{20,0},{8,4},{28,8},{0,12},{4,16},{24,20},{12,24},{16,28},{21,1},{... | collective-permute-start | bytes 132104 | tf_op jit(solution)/shard_map/ppermute | solution.py:40
  22.3 3.3 %collective-permute-start.12 = (bf16[172,128]{1,0:T(8,128)(2,1)S(1)}, bf16[172,128]{1,0:T(8,128)(2,1)S(1)}, u32[]{:S(2)}, u32[]{:S(2)}) collective-permute-start(bf16[172,128]{1,0:T(8,128)(2,1)S(1)} %get-tuple-element.18.refs_0_), channel_id=1, source_target_pairs={{0,4},{4,0},{8,12},{12,8},{16,20},{20,16},{24,28},{28,24},{1,5},{5... | collective-permute-start | bytes 132104 | tf_op jit(solution)/shard_map/ppermute | solution.py:36
  23.4 2.2 %collective-permute-start.14 = (bf16[172,128]{1,0:T(8,128)(2,1)S(1)}, bf16[172,128]{1,0:T(8,128)(2,1)S(1)}, u32[]{:S(2)}, u32[]{:S(2)}) collective-permute-start(bf16[172,128]{1,0:T(8,128)(2,1)S(1)} %collective-permute-done.10.refs_2_), channel_id=1, source_target_pairs={{0,4},{4,0},{8,12},{12,8},{16,20},{20,16},{24,28},{28,24},{1,5},{5... | collective-permute-start | bytes 132104 | tf_op jit(solution)/shard_map/ppermute | solution.py:36
  23.9 1.7 %collective-permute-start.15 = (bf16[172,128]{1,0:T(8,128)(2,1)S(1)}, bf16[172,128]{1,0:T(8,128)(2,1)S(1)}, u32[]{:S(2)}, u32[]{:S(2)}) collective-permute-start(bf16[172,128]{1,0:T(8,128)(2,1)S(1)} %collective-permute-done.9.refs_1_), channel_id=1, source_target_pairs={{0,4},{4,0},{8,12},{12,8},{16,20},{20,16},{24,28},{28,24},{1,5},{5... | collective-permute-start | bytes 132104 | tf_op jit(solution)/shard_map/ppermute | solution.py:36
  24.9 6.0 %collective-permute-start.11 = (bf16[128,256]{1,0:T(8,128)(2,1)S(1)}, bf16[128,256]{1,0:T(8,128)(2,1)S(1)}, u32[]{:S(2)}, u32[]{:S(2)}) collective-permute-start(bf16[128,256]{1,0:T(8,128)(2,1)S(1)} %shard_map.122), channel_id=1, source_target_pairs={{0,4},{4,0},{8,12},{12,8},{16,20},{20,16},{24,28},{28,24},{1,5},{5... | collective-permute-start | bytes 196616 | tf_op jit(solution)/shard_map/ppermute | solution.py:36
  25.9 6.2 %collective-permute-start.17 = (bf16[172,128]{1,0:T(8,128)(2,1)S(1)}, bf16[172,128]{1,0:T(8,128)(2,1)S(1)}, u32[]{:S(2)}, u32[]{:S(2)}) collective-permute-start(bf16[172,128]{1,0:T(8,128)(2,1)S(1)} %get-tuple-element.22), channel_id=1, source_target_pairs={{0,3},{1,2},{2,1},{3,0},{4,7},{5,6},{6,5},{7,4},{8,11},{9,10},{10,... | collective-permute-start | bytes 132104 | tf_op jit(solution)/shard_map/ppermute | solution.py:36
  28.2 5.5 %collective-permute-start.18 = (bf16[172,128]{1,0:T(8,128)(2,1)S(1)}, bf16[172,128]{1,0:T(8,128)(2,1)S(1)}, u32[]{:S(2)}, u32[]{:S(2)}) collective-permute-start(bf16[172,128]{1,0:T(8,128)(2,1)S(1)} %get-tuple-element.23), channel_id=1, source_target_pairs={{0,2},{1,3},{2,0},{3,1},{4,6},{5,7},{6,4},{7,5},{8,10},{9,11},{10,... | collective-permute-start | bytes 132104 | tf_op jit(solution)/shard_map/ppermute | solution.py:36
  28.3 5.4 %collective-permute-start.19 = (bf16[172,128]{1,0:T(8,128)(2,1)S(1)}, bf16[172,128]{1,0:T(8,128)(2,1)S(1)}, u32[]{:S(2)}, u32[]{:S(2)}) collective-permute-start(bf16[172,128]{1,0:T(8,128)(2,1)S(1)} %get-tuple-element.21.refs_0_), channel_id=1, source_target_pairs={{0,1},{1,0},{2,3},{3,2},{4,5},{5,4},{6,7},{7,6},{8,9},{9,8},{10,11... | collective-permute-start | bytes 132104 | tf_op jit(solution)/shard_map/ppermute | solution.py:36
  (3 other events, 24.5 us)

commit v2 on v0

--- a/solution.py
+++ b/solution.py
@@ -66,7 +66,8 @@
 
 
 def send_each(blocks, axis, size):
-    return [permuted(blocks[slot], axis, size, slot) for slot in reversed(range(1, size))]
+    slots = [size - 1, *range(1, size - 1)]
+    return [permuted(blocks[slot], axis, size, slot) for slot in slots]
 
 
 def call(kernel, out_shape, operands, specs=None, scratch=(), cost=None, out_specs=None):

time: 34.6 us -> 34.8 us (level)
    ppermute x7, waiting for transfers between devices: 1.86 us -> 1.11 us  [fetched(): lax.ppermute(block, axis, [(partner(i, seen(slot, i)), i) for i in range(...]
    ppermute x4, waiting for transfers between devices: 2.8 us -> 3.37 us  [send_across(): arrived.append(lax.ppermute(blocks[slot], ('row', 'col'), pairs))]
    ppermute x9, starting transfers between devices: 7.21 us -> 7.59 us  [permuted(): lax.ppermute(block, axis, [(i, partner(i, slot)) for i in range(size)])]
  transfers between devices with their start and end apart: 20 -> 20, of which waited for: 9 -> 9; matrix products, arithmetic and copies ran while one was open for 0% -> 0% of each run, Pallas kernels for 10% -> 11%
where the time goes in v2:
time: 34.8 us; the launch traced here: 34.5 us
  starting transfers between devices  20.5 us (59%)
  waiting for transfers between devices  7.55 us (22%)
  Pallas kernels  4.92 us (14%)
  between operations  1.46 us (4%)
    ppermute x7, starting transfers between devices, fetched(): lax.ppermute(block, axis, [(partner(i, seen(slot, i)), i) for i in range(...  8.65 us
    ppermute x9, starting transfers between devices, permuted(): lax.ppermute(block, axis, [(i, partner(i, slot)) for i in range(size)])  7.59 us
    pallas_call x11, Pallas kernels, call(): pl.pallas_call(kernel, out_shape=out_shape, in_specs=specs or [vmem] * le...  4.92 us
    ppermute x4, starting transfers between devices, send_across(): arrived.append(lax.ppermute(blocks[slot], ('row', 'col'), pairs))  4.3 us
    ppermute x4, waiting for transfers between devices, send_across(): arrived.append(lax.ppermute(blocks[slot], ('row', 'col'), pairs))  3.37 us
    ppermute x9, waiting for transfers between devices, permuted(): lax.ppermute(block, axis, [(i, partner(i, slot)) for i in range(size)])  3.08 us
    ppermute x7, waiting for transfers between devices, fetched(): lax.ppermute(block, axis, [(partner(i, seen(slot, i)), i) for i in range(...  1.11 us
  transfers between devices with their start and end apart: 20, of which 9 were waited for; matrix products, arithmetic and copies ran while one was open for 0% of the time, Pallas kernels for 11%

profile of v2, /device:TPU:0, one launch (start us, length us, event | category | flops | bytes accessed | tf_op | source)
XLA Modules:
  0.0 34.5 jit_solution(9375619022913393504)
XLA Ops:
  0.7 3.4 %collective-permute-start.2 = (bf16[128,128]{1,0:T(8,128)(2,1)}, bf16[128,128]{1,0:T(8,128)(2,1)S(1)}, u32[]{:S(2)}, u32[]{:S(2)}) collective-permute-start(bf16[128,128]{1,0:T(8,128)(2,1)} %bitcast.18), channel_id=1, source_target_pairs={{28,0},{24,4},{20,8},{16,12},{12,16},{8,20},{4,24},{0,28},{29,1},{... | collective-permute-start | bytes 98312 | tf_op jit(solution)/shard_map/ppermute | solution.py:40
  4.1 0.8 %collective-permute-start.1 = (bf16[128,128]{1,0:T(8,128)(2,1)}, bf16[128,128]{1,0:T(8,128)(2,1)S(1)}, u32[]{:S(2)}, u32[]{:S(2)}) collective-permute-start(bf16[128,128]{1,0:T(8,128)(2,1)} %bitcast.19), channel_id=1, source_target_pairs={{12,0},{16,4},{4,8},{24,12},{28,16},{0,20},{20,24},{8,28},{13,1},{... | collective-permute-start | bytes 98312 | tf_op jit(solution)/shard_map/ppermute | solution.py:40
  4.9 1.0 %collective-permute-start = (bf16[128,128]{1,0:T(8,128)(2,1)}, bf16[128,128]{1,0:T(8,128)(2,1)S(1)}, u32[]{:S(2)}, u32[]{:S(2)}) collective-permute-start(bf16[128,128]{1,0:T(8,128)(2,1)} %bitcast.20), channel_id=1, source_target_pairs={{20,0},{8,4},{28,8},{0,12},{4,16},{24,20},{12,24},{16,28},{21,1},{... | collective-permute-start | bytes 98312 | tf_op jit(solution)/shard_map/ppermute | solution.py:40
  6.5 1.9 %shard_map.113.refs_4_.dense_ref = bf16[512,1024]{1,0:T(8,128)(2,1)S(1)} custom-call(s32[1,1]{1,0:T(1,128)S(6)} %copy.13.count, s32[2,128]{1,0:T(2,128)} %bitcast.28, bf16[128,128,128]{2,1,0:T(8,128)(2,1)} %bitcast.25), custom_call_target="tpu_custom_call" | custom-call | flops 2097152 | bytes 4194304 | tf_op jit(solution)/shard_map/pallas_call | solution.py:75
  8.7 0.9 %collective-permute-start.3 = (bf16[512,128]{1,0:T(8,128)(2,1)S(1)}, bf16[512,128]{1,0:T(8,128)(2,1)S(1)}, u32[]{:S(2)}, u32[]{:S(2)}) collective-permute-start(bf16[512,128]{1,0:T(8,128)(2,1)S(1)} %shard_map.114.mine_ref.refs_0_), channel_id=1, source_target_pairs={{0,4},{4,0},{8,12},{12,8},{16,20},{20,16},{24,28},{28,24},{1,5},{5... | collective-permute-start | bytes 393224 | tf_op jit(solution)/shard_map/ppermute | solution.py:36
  10.9 3.4 %collective-permute-start.4 = (bf16[128,128]{1,0:T(8,128)(2,1)S(1)}, bf16[128,128]{1,0:T(8,128)(2,1)S(1)}, u32[]{:S(2)}, u32[]{:S(2)}) collective-permute-start(bf16[128,128]{1,0:T(8,128)(2,1)S(1)} %get-tuple-element.14), channel_id=1, source_target_pairs={{0,7},{1,6},{2,5},{3,4},{4,3},{5,2},{6,1},{7,0},{8,15},{9,14},{10,... | collective-permute-start | bytes 98312 | tf_op jit(solution)/shard_map/ppermute | solution.py:64
  14.3 0.7 %collective-permute-start.6 = (bf16[128,128]{1,0:T(8,128)(2,1)S(1)}, bf16[128,128]{1,0:T(8,128)(2,1)S(1)}, u32[]{:S(2)}, u32[]{:S(2)}) collective-permute-start(bf16[128,128]{1,0:T(8,128)(2,1)S(1)} %get-tuple-element.16), channel_id=1, source_target_pairs={{0,5},{1,4},{2,7},{3,6},{4,1},{5,0},{6,3},{7,2},{8,13},{9,12},{10,... | collective-permute-start | bytes 98312 | tf_op jit(solution)/shard_map/ppermute | solution.py:64
  15.2 0.9 %collective-permute-done.4.refs_0_ = bf16[128,128]{1,0:T(8,128)(2,1)S(1)} collective-permute-done((bf16[128,128]{1,0:T(8,128)(2,1)S(1)}, bf16[128,128]{1,0:T(8,128)(2,1)S(1)}, u32[]{:S(2)}, u32[]{:S(2)}) %collective-permute-start.4) | collective-permute-done | bytes 32800 | tf_op jit(solution)/shard_map/ppermute | solution.py:64
  16.1 2.5 %collective-permute-done.5.refs_1_ = bf16[128,128]{1,0:T(8,128)(2,1)S(1)} collective-permute-done((bf16[128,128]{1,0:T(8,128)(2,1)S(1)}, bf16[128,128]{1,0:T(8,128)(2,1)S(1)}, u32[]{:S(2)}, u32[]{:S(2)}) %collective-permute-start.5) | collective-permute-done | bytes 32800 | tf_op jit(solution)/shard_map/ppermute | solution.py:64
  18.9 0.9 %collective-permute-start.10 = (bf16[172,128]{1,0:T(8,128)(2,1)S(1)}, bf16[172,128]{1,0:T(8,128)(2,1)S(1)}, u32[]{:S(2)}, u32[]{:S(2)}) collective-permute-start(bf16[172,128]{1,0:T(8,128)(2,1)S(1)} %get-tuple-element.20.refs_0_), channel_id=1, source_target_pairs={{28,0},{24,4},{20,8},{16,12},{12,16},{8,20},{4,24},{0,28},{29,1},{... | collective-permute-start | bytes 132104 | tf_op jit(solution)/shard_map/ppermute | solution.py:40
  19.8 1.1 %collective-permute-start.9 = (bf16[172,128]{1,0:T(8,128)(2,1)S(1)}, bf16[172,128]{1,0:T(8,128)(2,1)S(1)}, u32[]{:S(2)}, u32[]{:S(2)}) collective-permute-start(bf16[172,128]{1,0:T(8,128)(2,1)S(1)} %get-tuple-element.20.refs_0_), channel_id=1, source_target_pairs={{12,0},{16,4},{4,8},{24,12},{28,16},{0,20},{20,24},{8,28},{13,1},{... | collective-permute-start | bytes 132104 | tf_op jit(solution)/shard_map/ppermute | solution.py:40
  20.9 1.3 %collective-permute-start.16 = (bf16[172,128]{1,0:T(8,128)(2,1)S(1)}, bf16[172,128]{1,0:T(8,128)(2,1)S(1)}, u32[]{:S(2)}, u32[]{:S(2)}) collective-permute-start(bf16[172,128]{1,0:T(8,128)(2,1)S(1)} %get-tuple-element.20.refs_0_), channel_id=1, source_target_pairs={{8,0},{20,4},{0,8},{28,12},{24,16},{4,20},{16,24},{12,28},{9,1},{2... | collective-permute-start | bytes 132104 | tf_op jit(solution)/shard_map/ppermute | solution.py:40
  22.4 0.7 %collective-permute-start.12 = (bf16[172,128]{1,0:T(8,128)(2,1)S(1)}, bf16[172,128]{1,0:T(8,128)(2,1)S(1)}, u32[]{:S(2)}, u32[]{:S(2)}) collective-permute-start(bf16[172,128]{1,0:T(8,128)(2,1)S(1)} %get-tuple-element.20.refs_0_), channel_id=1, source_target_pairs={{0,4},{4,0},{8,12},{12,8},{16,20},{20,16},{24,28},{28,24},{1,5},{5... | collective-permute-start | bytes 132104 | tf_op jit(solution)/shard_map/ppermute | solution.py:36
  23.4 0.8 %collective-permute-start.14 = (bf16[172,128]{1,0:T(8,128)(2,1)S(1)}, bf16[172,128]{1,0:T(8,128)(2,1)S(1)}, u32[]{:S(2)}, u32[]{:S(2)}) collective-permute-start(bf16[172,128]{1,0:T(8,128)(2,1)S(1)} %collective-permute-done.10.refs_2_), channel_id=1, source_target_pairs={{0,4},{4,0},{8,12},{12,8},{16,20},{20,16},{24,28},{28,24},{1,5},{5... | collective-permute-start | bytes 132104 | tf_op jit(solution)/shard_map/ppermute | solution.py:36
  24.2 0.5 %collective-permute-start.15 = (bf16[172,128]{1,0:T(8,128)(2,1)S(1)}, bf16[172,128]{1,0:T(8,128)(2,1)S(1)}, u32[]{:S(2)}, u32[]{:S(2)}) collective-permute-start(bf16[172,128]{1,0:T(8,128)(2,1)S(1)} %collective-permute-done.9.refs_1_), channel_id=1, source_target_pairs={{0,4},{4,0},{8,12},{12,8},{16,20},{20,16},{24,28},{28,24},{1,5},{5... | collective-permute-start | bytes 132104 | tf_op jit(solution)/shard_map/ppermute | solution.py:36
  25.1 0.6 %collective-permute-done.13.near_ref = bf16[172,128]{1,0:T(8,128)(2,1)S(1)} collective-permute-done((bf16[172,128]{1,0:T(8,128)(2,1)S(1)}, bf16[172,128]{1,0:T(8,128)(2,1)S(1)}, u32[]{:S(2)}, u32[]{:S(2)}) %collective-permute-start.13) | collective-permute-done | bytes 44064 | tf_op jit(solution)/shard_map/ppermute | solution.py:40
  26.1 2.0 %collective-permute-start.17 = (bf16[172,128]{1,0:T(8,128)(2,1)S(1)}, bf16[172,128]{1,0:T(8,128)(2,1)S(1)}, u32[]{:S(2)}, u32[]{:S(2)}) collective-permute-start(bf16[172,128]{1,0:T(8,128)(2,1)S(1)} %get-tuple-element.22), channel_id=1, source_target_pairs={{0,3},{1,2},{2,1},{3,0},{4,7},{5,6},{6,5},{7,4},{8,11},{9,10},{10,... | collective-permute-start | bytes 132104 | tf_op jit(solution)/shard_map/ppermute | solution.py:36
  28.1 0.6 %collective-permute-start.18 = (bf16[172,128]{1,0:T(8,128)(2,1)S(1)}, bf16[172,128]{1,0:T(8,128)(2,1)S(1)}, u32[]{:S(2)}, u32[]{:S(2)}) collective-permute-start(bf16[172,128]{1,0:T(8,128)(2,1)S(1)} %get-tuple-element.23), channel_id=1, source_target_pairs={{0,1},{1,0},{2,3},{3,2},{4,5},{5,4},{6,7},{7,6},{8,9},{9,8},{10,11... | collective-permute-start | bytes 132104 | tf_op jit(solution)/shard_map/ppermute | solution.py:36
  28.7 1.8 %collective-permute-start.19 = (bf16[172,128]{1,0:T(8,128)(2,1)S(1)}, bf16[172,128]{1,0:T(8,128)(2,1)S(1)}, u32[]{:S(2)}, u32[]{:S(2)}) collective-permute-start(bf16[172,128]{1,0:T(8,128)(2,1)S(1)} %get-tuple-element.24), channel_id=1, source_target_pairs={{0,2},{1,3},{2,0},{3,1},{4,6},{5,7},{6,4},{7,5},{8,10},{9,11},{10,... | collective-permute-start | bytes 132104 | tf_op jit(solution)/shard_map/ppermute | solution.py:36
  30.6 0.6 %shard_map.121 = bf16[128,256]{1,0:T(8,128)(2,1)} custom-call(bf16[128,256]{1,0:T(8,128)(2,1)S(1)} %collective-permute-done.11.value), custom_call_target="tpu_custom_call" | custom-call | tf_op jit(solution)/shard_map/pallas_call | solution.py:75
  31.2 1.0 %collective-permute-done.17.refs_1_ = bf16[172,128]{1,0:T(8,128)(2,1)S(1)} collective-permute-done((bf16[172,128]{1,0:T(8,128)(2,1)S(1)}, bf16[172,128]{1,0:T(8,128)(2,1)S(1)}, u32[]{:S(2)}, u32[]{:S(2)}) %collective-permute-start.17) | collective-permute-done | bytes 44064 | tf_op jit(solution)/shard_map/ppermute | solution.py:36
  32.2 0.9 %collective-permute-done.18.refs_2_ = bf16[172,128]{1,0:T(8,128)(2,1)S(1)} collective-permute-done((bf16[172,128]{1,0:T(8,128)(2,1)S(1)}, bf16[172,128]{1,0:T(8,128)(2,1)S(1)}, u32[]{:S(2)}, u32[]{:S(2)}) %collective-permute-start.18) | collective-permute-done | bytes 44064 | tf_op jit(solution)/shard_map/ppermute | solution.py:36
  33.2 0.6 %collective-permute-done.19.refs_3_ = bf16[172,128]{1,0:T(8,128)(2,1)S(1)} collective-permute-done((bf16[172,128]{1,0:T(8,128)(2,1)S(1)}, bf16[172,128]{1,0:T(8,128)(2,1)S(1)}, u32[]{:S(2)}, u32[]{:S(2)}) %collective-permute-start.19) | collective-permute-done | bytes 44064 | tf_op jit(solution)/shard_map/ppermute | solution.py:36
  33.8 0.7 %shard_map.123 = f32[172,1,128]{2,1,0:T(1,128)} custom-call(bf16[172,128]{1,0:T(8,128)(2,1)S(1)} %get-tuple-element.21.refs_0_, bf16[172,128]{1,0:T(8,128)(2,1)S(1)} %collective-permute-done.17.refs_1_, bf16[172,128]{1,0:T(8,128)(2,1)S(1)} %collective-permute-done.18.refs_2_, bf16[172,128]{1,0:T(8,128)(2,1)S(1)} %collective-permute-done.19.refs_3_, ...), custom_call_target="tpu_custom_call" | custom-call | tf_op jit(solution)/shard_map/pallas_call | solution.py:75
  (41 shorter events, 3.4 us)
Async XLA Ops:
  0.6 9.0 %copy-start.4 = (f32[172]{0:T(256)S(1)}, f32[172]{0:T(256)}, u32[]{:S(2)}) copy-start(f32[172]{0:T(256)} %param.19) | copy-start | bytes 2068
  0.7 7.7 %collective-permute-start.2 = (bf16[128,128]{1,0:T(8,128)(2,1)}, bf16[128,128]{1,0:T(8,128)(2,1)S(1)}, u32[]{:S(2)}, u32[]{:S(2)}) collective-permute-start(bf16[128,128]{1,0:T(8,128)(2,1)} %bitcast.18), channel_id=1, source_target_pairs={{28,0},{24,4},{20,8},{16,12},{12,16},{8,20},{4,24},{0,28},{29,1},{... | collective-permute-start | bytes 98312 | tf_op jit(solution)/shard_map/ppermute | solution.py:40
  4.1 4.3 %collective-permute-start.1 = (bf16[128,128]{1,0:T(8,128)(2,1)}, bf16[128,128]{1,0:T(8,128)(2,1)S(1)}, u32[]{:S(2)}, u32[]{:S(2)}) collective-permute-start(bf16[128,128]{1,0:T(8,128)(2,1)} %bitcast.19), channel_id=1, source_target_pairs={{12,0},{16,4},{4,8},{24,12},{28,16},{0,20},{20,24},{8,28},{13,1},{... | collective-permute-start | bytes 98312 | tf_op jit(solution)/shard_map/ppermute | solution.py:40
  4.9 3.8 %collective-permute-start = (bf16[128,128]{1,0:T(8,128)(2,1)}, bf16[128,128]{1,0:T(8,128)(2,1)S(1)}, u32[]{:S(2)}, u32[]{:S(2)}) collective-permute-start(bf16[128,128]{1,0:T(8,128)(2,1)} %bitcast.20), channel_id=1, source_target_pairs={{20,0},{8,4},{28,8},{0,12},{4,16},{24,20},{12,24},{16,28},{21,1},{... | collective-permute-start | bytes 98312 | tf_op jit(solution)/shard_map/ppermute | solution.py:40
  6.5 12.1 %copy-start = (bf16[256,172]{0,1:T(8,128)(2,1)S(1)}, bf16[256,172]{0,1:T(8,128)(2,1)}, u32[]{:S(2)}) copy-start(bf16[256,172]{0,1:T(8,128)(2,1)} %param.18) | copy-start | bytes 264196
  6.5 12.1 %copy-start.2 = (bf16[128,256]{1,0:T(8,128)(2,1)S(1)}, bf16[128,256]{1,0:T(8,128)(2,1)}, u32[]{:S(2)}) copy-start(bf16[128,256]{1,0:T(8,128)(2,1)} %refs_5_.1) | copy-start | bytes 196612
  6.5 12.1 %copy-start.5 = (f32[256]{0:T(256)S(1)}, f32[256]{0:T(256)}, u32[]{:S(2)}) copy-start(f32[256]{0:T(256)} %param.17) | copy-start | bytes 3076
  8.7 1.9 %collective-permute-start.3 = (bf16[512,128]{1,0:T(8,128)(2,1)S(1)}, bf16[512,128]{1,0:T(8,128)(2,1)S(1)}, u32[]{:S(2)}, u32[]{:S(2)}) collective-permute-start(bf16[512,128]{1,0:T(8,128)(2,1)S(1)} %shard_map.114.mine_ref.refs_0_), channel_id=1, source_target_pairs={{0,4},{4,0},{8,12},{12,8},{16,20},{20,16},{24,28},{28,24},{1,5},{5... | collective-permute-start | bytes 393224 | tf_op jit(solution)/shard_map/ppermute | solution.py:36
  9.7 5.5 %collective-permute-start.8 = (bf16[128,256]{1,0:T(8,128)(2,1)S(1)}, bf16[128,256]{1,0:T(8,128)(2,1)S(1)}, u32[]{:S(2)}, u32[]{:S(2)}) collective-permute-start(bf16[128,256]{1,0:T(8,128)(2,1)S(1)} %get-tuple-element.18), channel_id=1, source_target_pairs={{0,4},{4,0},{8,12},{12,8},{16,20},{20,16},{24,28},{28,24},{1,5},{5... | collective-permute-start | bytes 196616 | tf_op jit(solution)/shard_map/ppermute | solution.py:36
  10.9 5.2 %collective-permute-start.4 = (bf16[128,128]{1,0:T(8,128)(2,1)S(1)}, bf16[128,128]{1,0:T(8,128)(2,1)S(1)}, u32[]{:S(2)}, u32[]{:S(2)}) collective-permute-start(bf16[128,128]{1,0:T(8,128)(2,1)S(1)} %get-tuple-element.14), channel_id=1, source_target_pairs={{0,7},{1,6},{2,5},{3,4},{4,3},{5,2},{6,1},{7,0},{8,15},{9,14},{10,... | collective-permute-start | bytes 98312 | tf_op jit(solution)/shard_map/ppermute | solution.py:64
  14.3 4.3 %collective-permute-start.5 = (bf16[128,128]{1,0:T(8,128)(2,1)S(1)}, bf16[128,128]{1,0:T(8,128)(2,1)S(1)}, u32[]{:S(2)}, u32[]{:S(2)}) collective-permute-start(bf16[128,128]{1,0:T(8,128)(2,1)S(1)} %get-tuple-element.15), channel_id=1, source_target_pairs={{0,6},{1,7},{2,4},{3,5},{4,2},{5,3},{6,0},{7,1},{8,14},{9,15},{10,... | collective-permute-start | bytes 98312 | tf_op jit(solution)/shard_map/ppermute | solution.py:64
  14.3 4.3 %collective-permute-start.6 = (bf16[128,128]{1,0:T(8,128)(2,1)S(1)}, bf16[128,128]{1,0:T(8,128)(2,1)S(1)}, u32[]{:S(2)}, u32[]{:S(2)}) collective-permute-start(bf16[128,128]{1,0:T(8,128)(2,1)S(1)} %get-tuple-element.16), channel_id=1, source_target_pairs={{0,5},{1,4},{2,7},{3,6},{4,1},{5,0},{6,3},{7,2},{8,13},{9,12},{10,... | collective-permute-start | bytes 98312 | tf_op jit(solution)/shard_map/ppermute | solution.py:64
  15.0 3.5 %collective-permute-start.7 = (bf16[128,128]{1,0:T(8,128)(2,1)S(1)}, bf16[128,128]{1,0:T(8,128)(2,1)S(1)}, u32[]{:S(2)}, u32[]{:S(2)}) collective-permute-start(bf16[128,128]{1,0:T(8,128)(2,1)S(1)} %get-tuple-element.17), channel_id=1, source_target_pairs={{0,4},{1,5},{2,6},{3,7},{4,0},{5,1},{6,2},{7,3},{8,12},{9,13},{10,... | collective-permute-start | bytes 98312 | tf_op jit(solution)/shard_map/ppermute | solution.py:64
  18.9 4.5 %collective-permute-start.10 = (bf16[172,128]{1,0:T(8,128)(2,1)S(1)}, bf16[172,128]{1,0:T(8,128)(2,1)S(1)}, u32[]{:S(2)}, u32[]{:S(2)}) collective-permute-start(bf16[172,128]{1,0:T(8,128)(2,1)S(1)} %get-tuple-element.20.refs_0_), channel_id=1, source_target_pairs={{28,0},{24,4},{20,8},{16,12},{12,16},{8,20},{4,24},{0,28},{29,1},{... | collective-permute-start | bytes 132104 | tf_op jit(solution)/shard_map/ppermute | solution.py:40
  19.8 4.4 %collective-permute-start.9 = (bf16[172,128]{1,0:T(8,128)(2,1)S(1)}, bf16[172,128]{1,0:T(8,128)(2,1)S(1)}, u32[]{:S(2)}, u32[]{:S(2)}) collective-permute-start(bf16[172,128]{1,0:T(8,128)(2,1)S(1)} %get-tuple-element.20.refs_0_), channel_id=1, source_target_pairs={{12,0},{16,4},{4,8},{24,12},{28,16},{0,20},{20,24},{8,28},{13,1},{... | collective-permute-start | bytes 132104 | tf_op jit(solution)/shard_map/ppermute | solution.py:40
  20.9 4.1 %collective-permute-start.16 = (bf16[172,128]{1,0:T(8,128)(2,1)S(1)}, bf16[172,128]{1,0:T(8,128)(2,1)S(1)}, u32[]{:S(2)}, u32[]{:S(2)}) collective-permute-start(bf16[172,128]{1,0:T(8,128)(2,1)S(1)} %get-tuple-element.20.refs_0_), channel_id=1, source_target_pairs={{8,0},{20,4},{0,8},{28,12},{24,16},{4,20},{16,24},{12,28},{9,1},{2... | collective-permute-start | bytes 132104 | tf_op jit(solution)/shard_map/ppermute | solution.py:40
  22.2 3.5 %collective-permute-start.13 = (bf16[172,128]{1,0:T(8,128)(2,1)S(1)}, bf16[172,128]{1,0:T(8,128)(2,1)S(1)}, u32[]{:S(2)}, u32[]{:S(2)}) collective-permute-start(bf16[172,128]{1,0:T(8,128)(2,1)S(1)} %get-tuple-element.20.refs_0_), channel_id=1, source_target_pairs={{20,0},{8,4},{28,8},{0,12},{4,16},{24,20},{12,24},{16,28},{21,1},{... | collective-permute-start | bytes 132104 | tf_op jit(solution)/shard_map/ppermute | solution.py:40
  22.4 3.2 %collective-permute-start.12 = (bf16[172,128]{1,0:T(8,128)(2,1)S(1)}, bf16[172,128]{1,0:T(8,128)(2,1)S(1)}, u32[]{:S(2)}, u32[]{:S(2)}) collective-permute-start(bf16[172,128]{1,0:T(8,128)(2,1)S(1)} %get-tuple-element.20.refs_0_), channel_id=1, source_target_pairs={{0,4},{4,0},{8,12},{12,8},{16,20},{20,16},{24,28},{28,24},{1,5},{5... | collective-permute-start | bytes 132104 | tf_op jit(solution)/shard_map/ppermute | solution.py:36
  23.4 2.3 %collective-permute-start.14 = (bf16[172,128]{1,0:T(8,128)(2,1)S(1)}, bf16[172,128]{1,0:T(8,128)(2,1)S(1)}, u32[]{:S(2)}, u32[]{:S(2)}) collective-permute-start(bf16[172,128]{1,0:T(8,128)(2,1)S(1)} %collective-permute-done.10.refs_2_), channel_id=1, source_target_pairs={{0,4},{4,0},{8,12},{12,8},{16,20},{20,16},{24,28},{28,24},{1,5},{5... | collective-permute-start | bytes 132104 | tf_op jit(solution)/shard_map/ppermute | solution.py:36
  24.2 1.5 %collective-permute-start.15 = (bf16[172,128]{1,0:T(8,128)(2,1)S(1)}, bf16[172,128]{1,0:T(8,128)(2,1)S(1)}, u32[]{:S(2)}, u32[]{:S(2)}) collective-permute-start(bf16[172,128]{1,0:T(8,128)(2,1)S(1)} %collective-permute-done.9.refs_1_), channel_id=1, source_target_pairs={{0,4},{4,0},{8,12},{12,8},{16,20},{20,16},{24,28},{28,24},{1,5},{5... | collective-permute-start | bytes 132104 | tf_op jit(solution)/shard_map/ppermute | solution.py:36
  25.0 5.6 %collective-permute-start.11 = (bf16[128,256]{1,0:T(8,128)(2,1)S(1)}, bf16[128,256]{1,0:T(8,128)(2,1)S(1)}, u32[]{:S(2)}, u32[]{:S(2)}) collective-permute-start(bf16[128,256]{1,0:T(8,128)(2,1)S(1)} %shard_map.120), channel_id=1, source_target_pairs={{0,4},{4,0},{8,12},{12,8},{16,20},{20,16},{24,28},{28,24},{1,5},{5... | collective-permute-start | bytes 196616 | tf_op jit(solution)/shard_map/ppermute | solution.py:36
  26.1 6.1 %collective-permute-start.17 = (bf16[172,128]{1,0:T(8,128)(2,1)S(1)}, bf16[172,128]{1,0:T(8,128)(2,1)S(1)}, u32[]{:S(2)}, u32[]{:S(2)}) collective-permute-start(bf16[172,128]{1,0:T(8,128)(2,1)S(1)} %get-tuple-element.22), channel_id=1, source_target_pairs={{0,3},{1,2},{2,1},{3,0},{4,7},{5,6},{6,5},{7,4},{8,11},{9,10},{10,... | collective-permute-start | bytes 132104 | tf_op jit(solution)/shard_map/ppermute | solution.py:36
  28.1 5.1 %collective-permute-start.18 = (bf16[172,128]{1,0:T(8,128)(2,1)S(1)}, bf16[172,128]{1,0:T(8,128)(2,1)S(1)}, u32[]{:S(2)}, u32[]{:S(2)}) collective-permute-start(bf16[172,128]{1,0:T(8,128)(2,1)S(1)} %get-tuple-element.23), channel_id=1, source_target_pairs={{0,1},{1,0},{2,3},{3,2},{4,5},{5,4},{6,7},{7,6},{8,9},{9,8},{10,11... | collective-permute-start | bytes 132104 | tf_op jit(solution)/shard_map/ppermute | solution.py:36
  28.7 5.1 %collective-permute-start.19 = (bf16[172,128]{1,0:T(8,128)(2,1)S(1)}, bf16[172,128]{1,0:T(8,128)(2,1)S(1)}, u32[]{:S(2)}, u32[]{:S(2)}) collective-permute-start(bf16[172,128]{1,0:T(8,128)(2,1)S(1)} %get-tuple-element.24), channel_id=1, source_target_pairs={{0,2},{1,3},{2,0},{3,1},{4,6},{5,7},{6,4},{7,5},{8,10},{9,11},{10,... | collective-permute-start | bytes 132104 | tf_op jit(solution)/shard_map/ppermute | solution.py:36
  (3 other events, 26.0 us)

commit v3 on v0

--- a/solution.py
+++ b/solution.py
@@ -65,8 +65,27 @@
     return arrived
 
 
-def send_each(blocks, axis, size):
-    return [permuted(blocks[slot], axis, size, slot) for slot in reversed(range(1, size))]
+def send_plan(size):
+    far = size - 1
+    return list(zip([far, *reversed(range(1, far))], [far, *range(1, far)]))
+
+
+def by_core(pair, pick):
+    if pair[0] == pair[1]:
+        return pick(pair[0])
+    return jnp.where((lax.axis_index("row") & 1) == 0, pick(pair[0]), pick(pair[1]))
+
+
+def send_each(blocks, n_row, n_col):
+    arrived = []
+    for block, slots in zip(blocks, send_plan(n_col)):
+        pairs = [
+            (row * n_col + col, row * n_col + partner(col, slots[row & 1]))
+            for row in range(n_row)
+            for col in range(n_col)
+        ]
+        arrived.append(lax.ppermute(block, ("row", "col"), pairs))
+    return arrived
 
 
 def call(kernel, out_shape, operands, specs=None, scratch=(), cost=None, out_specs=None):
@@ -208,8 +227,8 @@
     rest = lanes([own_ref, *blocks], scratch)
     total = first_ref[...] + dot_nt(rest, dense_ref[:, :half])
     total += dot_nt(near_ref[...], dense_ref[:, dense_ref.shape[1] - block :])
-    for k, out in enumerate(outputs):
-        out[...] = total[:, k * block : (k + 1) * block].astype(BF16)
+    for pair, out in zip([(0, 0), *send_plan(n_col)], outputs):
+        out[...] = by_core(pair, lambda k: total[:, k * block : (k + 1) * block]).astype(BF16)
 
 
 def logits_kernel(n_col, pieces, *refs):
@@ -372,9 +391,9 @@
             specs=[smem, smem, vmem, vmem],
             scratch=[pltpu.VMEM((n_col, classes, block), F32)],
         )
-        parts_two = [summed[k] for k in range(n_col)]
-
-    arrived_two = send_each(parts_two, "col", n_col)
+        parts_two = [summed[0], *[by_core(p, lambda k: summed[k]) for p in send_plan(n_col)]]
+
+    arrived_two = send_each(parts_two[1:], n_row, n_col)
     pushed = call(write_kernel, shape((block, hid), BF16), (fetch_core(pushed, "row", n_row),))
     pieces = 4
     scores = call(

time: 34.6 us -> 34.7 us (level)
  starting transfers between devices: 20.4 us -> 19.7 us
  Pallas kernels: 4.62 us -> 5.08 us
    ppermute x9 -> x6, starting transfers between devices: 7.21 us -> 2.17 us  [permuted(): lax.ppermute(block, axis, [(i, partner(i, slot)) for i in range(size)])]
    ppermute x0 -> x3, starting transfers between devices: none -> 4.45 us  [send_each(): arrived.append(lax.ppermute(block, ('row', 'col'), pairs))]
    ppermute x0 -> x3, waiting for transfers between devices: none -> 2.86 us  [send_each(): arrived.append(lax.ppermute(block, ('row', 'col'), pairs))]
    ppermute x9 -> x6, waiting for transfers between devices: 3.11 us -> 0.36 us  [permuted(): lax.ppermute(block, axis, [(i, partner(i, slot)) for i in range(size)])]
    ppermute x4, waiting for transfers between devices: 2.8 us -> 3.38 us  [send_across(): arrived.append(lax.ppermute(blocks[slot], ('row', 'col'), pairs))]
    ppermute x7, waiting for transfers between devices: 1.86 us -> 1.37 us  [fetched(): lax.ppermute(block, axis, [(partner(i, seen(slot, i)), i) for i in range(...]
    pallas_call x11, Pallas kernels: 4.62 us -> 5.08 us  [call(): pl.pallas_call(kernel, out_shape=out_shape, in_specs=specs or [vmem] * le...]
  transfers between devices with their start and end apart: 20 -> 20, of which waited for: 9 -> 9; matrix products, arithmetic and copies ran while one was open for 0% -> 0% of each run, Pallas kernels for 10% -> 12%
where the time goes in v3:
time: 34.7 us; the launch traced here: 34.3 us
  starting transfers between devices  19.7 us (57%)
  waiting for transfers between devices  7.97 us (23%)
  Pallas kernels  5.08 us (15%)
  between operations  1.46 us (4%)
    ppermute x7, starting transfers between devices, fetched(): lax.ppermute(block, axis, [(partner(i, seen(slot, i)), i) for i in range(...  8.83 us
    pallas_call x11, Pallas kernels, call(): pl.pallas_call(kernel, out_shape=out_shape, in_specs=specs or [vmem] * le...  5.08 us
    ppermute x3, starting transfers between devices, send_each(): arrived.append(lax.ppermute(block, ('row', 'col'), pairs))  4.45 us
    ppermute x4, starting transfers between devices, send_across(): arrived.append(lax.ppermute(blocks[slot], ('row', 'col'), pairs))  4.29 us
    ppermute x4, waiting for transfers between devices, send_across(): arrived.append(lax.ppermute(blocks[slot], ('row', 'col'), pairs))  3.38 us
    ppermute x3, waiting for transfers between devices, send_each(): arrived.append(lax.ppermute(block, ('row', 'col'), pairs))  2.86 us
    ppermute x6, starting transfers between devices, permuted(): lax.ppermute(block, axis, [(i, partner(i, slot)) for i in range(size)])  2.17 us
    ppermute x7, waiting for transfers between devices, fetched(): lax.ppermute(block, axis, [(partner(i, seen(slot, i)), i) for i in range(...  1.37 us
  transfers between devices with their start and end apart: 20, of which 9 were waited for; matrix products, arithmetic and copies ran while one was open for 0% of the time, Pallas kernels for 12%

profile of v3, /device:TPU:0, one launch (start us, length us, event | category | flops | bytes accessed | tf_op | source)
XLA Modules:
  0.0 34.3 jit_solution(816225563367717329)
XLA Ops:
  0.7 3.4 %collective-permute-start.2 = (bf16[128,128]{1,0:T(8,128)(2,1)}, bf16[128,128]{1,0:T(8,128)(2,1)S(1)}, u32[]{:S(2)}, u32[]{:S(2)}) collective-permute-start(bf16[128,128]{1,0:T(8,128)(2,1)} %bitcast.18), channel_id=1, source_target_pairs={{28,0},{24,4},{20,8},{16,12},{12,16},{8,20},{4,24},{0,28},{29,1},{... | collective-permute-start | bytes 98312 | tf_op jit(solution)/shard_map/ppermute | solution.py:40
  4.1 0.8 %collective-permute-start.1 = (bf16[128,128]{1,0:T(8,128)(2,1)}, bf16[128,128]{1,0:T(8,128)(2,1)S(1)}, u32[]{:S(2)}, u32[]{:S(2)}) collective-permute-start(bf16[128,128]{1,0:T(8,128)(2,1)} %bitcast.19), channel_id=1, source_target_pairs={{12,0},{16,4},{4,8},{24,12},{28,16},{0,20},{20,24},{8,28},{13,1},{... | collective-permute-start | bytes 98312 | tf_op jit(solution)/shard_map/ppermute | solution.py:40
  4.9 1.0 %collective-permute-start = (bf16[128,128]{1,0:T(8,128)(2,1)}, bf16[128,128]{1,0:T(8,128)(2,1)S(1)}, u32[]{:S(2)}, u32[]{:S(2)}) collective-permute-start(bf16[128,128]{1,0:T(8,128)(2,1)} %bitcast.20), channel_id=1, source_target_pairs={{20,0},{8,4},{28,8},{0,12},{4,16},{24,20},{12,24},{16,28},{21,1},{... | collective-permute-start | bytes 98312 | tf_op jit(solution)/shard_map/ppermute | solution.py:40
  6.5 2.0 %shard_map.113.refs_4_.dense_ref = bf16[512,1024]{1,0:T(8,128)(2,1)S(1)} custom-call(s32[1,1]{1,0:T(1,128)S(6)} %copy.13.count, s32[2,128]{1,0:T(2,128)} %bitcast.28, bf16[128,128,128]{2,1,0:T(8,128)(2,1)} %bitcast.25), custom_call_target="tpu_custom_call" | custom-call | flops 2097152 | bytes 4194304 | tf_op jit(solution)/shard_map/pallas_call | solution.py:93
  9.0 0.5 %collective-permute-start.8 = (bf16[128,256]{1,0:T(8,128)(2,1)S(1)}, bf16[128,256]{1,0:T(8,128)(2,1)S(1)}, u32[]{:S(2)}, u32[]{:S(2)}) collective-permute-start(bf16[128,256]{1,0:T(8,128)(2,1)S(1)} %get-tuple-element.18), channel_id=1, source_target_pairs={{0,4},{4,0},{8,12},{12,8},{16,20},{20,16},{24,28},{28,24},{1,5},{5... | collective-permute-start | bytes 196616 | tf_op jit(solution)/shard_map/ppermute | solution.py:36
  10.4 3.4 %collective-permute-start.4 = (bf16[128,128]{1,0:T(8,128)(2,1)S(1)}, bf16[128,128]{1,0:T(8,128)(2,1)S(1)}, u32[]{:S(2)}, u32[]{:S(2)}) collective-permute-start(bf16[128,128]{1,0:T(8,128)(2,1)S(1)} %get-tuple-element.14), channel_id=1, source_target_pairs={{0,7},{1,6},{2,5},{3,4},{4,3},{5,2},{6,1},{7,0},{8,15},{9,14},{10,... | collective-permute-start | bytes 98312 | tf_op jit(solution)/shard_map/ppermute | solution.py:64
  13.8 0.6 %collective-permute-start.6 = (bf16[128,128]{1,0:T(8,128)(2,1)S(1)}, bf16[128,128]{1,0:T(8,128)(2,1)S(1)}, u32[]{:S(2)}, u32[]{:S(2)}) collective-permute-start(bf16[128,128]{1,0:T(8,128)(2,1)S(1)} %get-tuple-element.16), channel_id=1, source_target_pairs={{0,5},{1,4},{2,7},{3,6},{4,1},{5,0},{6,3},{7,2},{8,13},{9,12},{10,... | collective-permute-start | bytes 98312 | tf_op jit(solution)/shard_map/ppermute | solution.py:64
  14.7 0.9 %collective-permute-done.4.refs_0_ = bf16[128,128]{1,0:T(8,128)(2,1)S(1)} collective-permute-done((bf16[128,128]{1,0:T(8,128)(2,1)S(1)}, bf16[128,128]{1,0:T(8,128)(2,1)S(1)}, u32[]{:S(2)}, u32[]{:S(2)}) %collective-permute-start.4) | collective-permute-done | bytes 32800 | tf_op jit(solution)/shard_map/ppermute | solution.py:64
  15.6 2.5 %collective-permute-done.5.refs_1_ = bf16[128,128]{1,0:T(8,128)(2,1)S(1)} collective-permute-done((bf16[128,128]{1,0:T(8,128)(2,1)S(1)}, bf16[128,128]{1,0:T(8,128)(2,1)S(1)}, u32[]{:S(2)}, u32[]{:S(2)}) %collective-permute-start.5) | collective-permute-done | bytes 32800 | tf_op jit(solution)/shard_map/ppermute | solution.py:64
  18.5 1.3 %collective-permute-start.10 = (bf16[172,128]{1,0:T(8,128)(2,1)S(1)}, bf16[172,128]{1,0:T(8,128)(2,1)S(1)}, u32[]{:S(2)}, u32[]{:S(2)}) collective-permute-start(bf16[172,128]{1,0:T(8,128)(2,1)S(1)} %get-tuple-element.20.refs_0_), channel_id=1, source_target_pairs={{28,0},{24,4},{20,8},{16,12},{12,16},{8,20},{4,24},{0,28},{29,1},{... | collective-permute-start | bytes 132104 | tf_op jit(solution)/shard_map/ppermute | solution.py:40
  19.8 0.8 %collective-permute-start.9 = (bf16[172,128]{1,0:T(8,128)(2,1)S(1)}, bf16[172,128]{1,0:T(8,128)(2,1)S(1)}, u32[]{:S(2)}, u32[]{:S(2)}) collective-permute-start(bf16[172,128]{1,0:T(8,128)(2,1)S(1)} %get-tuple-element.20.refs_0_), channel_id=1, source_target_pairs={{12,0},{16,4},{4,8},{24,12},{28,16},{0,20},{20,24},{8,28},{13,1},{... | collective-permute-start | bytes 132104 | tf_op jit(solution)/shard_map/ppermute | solution.py:40
  20.6 1.1 %collective-permute-start.16 = (bf16[172,128]{1,0:T(8,128)(2,1)S(1)}, bf16[172,128]{1,0:T(8,128)(2,1)S(1)}, u32[]{:S(2)}, u32[]{:S(2)}) collective-permute-start(bf16[172,128]{1,0:T(8,128)(2,1)S(1)} %get-tuple-element.20.refs_0_), channel_id=1, source_target_pairs={{8,0},{20,4},{0,8},{28,12},{24,16},{4,20},{16,24},{12,28},{9,1},{2... | collective-permute-start | bytes 132104 | tf_op jit(solution)/shard_map/ppermute | solution.py:40
  21.7 0.4 %collective-permute-start.13 = (bf16[172,128]{1,0:T(8,128)(2,1)S(1)}, bf16[172,128]{1,0:T(8,128)(2,1)S(1)}, u32[]{:S(2)}, u32[]{:S(2)}) collective-permute-start(bf16[172,128]{1,0:T(8,128)(2,1)S(1)} %get-tuple-element.20.refs_0_), channel_id=1, source_target_pairs={{20,0},{8,4},{28,8},{0,12},{4,16},{24,20},{12,24},{16,28},{21,1},{... | collective-permute-start | bytes 132104 | tf_op jit(solution)/shard_map/ppermute | solution.py:40
  22.1 0.9 %collective-permute-start.12 = (bf16[172,128]{1,0:T(8,128)(2,1)S(1)}, bf16[172,128]{1,0:T(8,128)(2,1)S(1)}, u32[]{:S(2)}, u32[]{:S(2)}) collective-permute-start(bf16[172,128]{1,0:T(8,128)(2,1)S(1)} %get-tuple-element.20.refs_0_), channel_id=1, source_target_pairs={{0,4},{4,0},{8,12},{12,8},{16,20},{20,16},{24,28},{28,24},{1,5},{5... | collective-permute-start | bytes 132104 | tf_op jit(solution)/shard_map/ppermute | solution.py:36
  23.1 0.5 %collective-permute-start.14 = (bf16[172,128]{1,0:T(8,128)(2,1)S(1)}, bf16[172,128]{1,0:T(8,128)(2,1)S(1)}, u32[]{:S(2)}, u32[]{:S(2)}) collective-permute-start(bf16[172,128]{1,0:T(8,128)(2,1)S(1)} %collective-permute-done.10.refs_2_), channel_id=1, source_target_pairs={{0,4},{4,0},{8,12},{12,8},{16,20},{20,16},{24,28},{28,24},{1,5},{5... | collective-permute-start | bytes 132104 | tf_op jit(solution)/shard_map/ppermute | solution.py:36
  24.1 0.6 %collective-permute-done.16.refs_2_ = bf16[172,128]{1,0:T(8,128)(2,1)S(1)} collective-permute-done((bf16[172,128]{1,0:T(8,128)(2,1)S(1)}, bf16[172,128]{1,0:T(8,128)(2,1)S(1)}, u32[]{:S(2)}, u32[]{:S(2)}) %collective-permute-start.16) | collective-permute-done | bytes 44064 | tf_op jit(solution)/shard_map/ppermute | solution.py:40
  24.7 0.5 %collective-permute-done.13.near_ref = bf16[172,128]{1,0:T(8,128)(2,1)S(1)} collective-permute-done((bf16[172,128]{1,0:T(8,128)(2,1)S(1)}, bf16[172,128]{1,0:T(8,128)(2,1)S(1)}, u32[]{:S(2)}, u32[]{:S(2)}) %collective-permute-start.13) | collective-permute-done | bytes 44064 | tf_op jit(solution)/shard_map/ppermute | solution.py:40
  25.2 0.4 %shard_map.122 = (bf16[172,128]{1,0:T(8,128)(2,1)S(1)}, bf16[172,128]{1,0:T(8,128)(2,1)S(1)}, bf16[172,128]{1,0:T(8,128)(2,1)S(1)}, bf16[172,128]{1,0:T(8,128)(2,1)S(1)}) custom-call(bf16[512,1024]{1,0:T(8,128)(2,1)S(1)} %shard_map.113.refs_4_.dense_ref, f32[172,512]{1,0:T(8,128)S(1)} %shard_map.119.after.first_ref, ...), custom_call_target="tpu_custom_call" | custom-call | tf_op jit(solution)/shard_map/pallas_call | solution.py:93
  25.6 2.0 %collective-permute-start.17 = (bf16[172,128]{1,0:T(8,128)(2,1)S(1)}, bf16[172,128]{1,0:T(8,128)(2,1)S(1)}, u32[]{:S(2)}, u32[]{:S(2)}) collective-permute-start(bf16[172,128]{1,0:T(8,128)(2,1)S(1)} %get-tuple-element.22), channel_id=1, source_target_pairs={{0,3},{1,2},{2,1},{3,0},{4,7},{5,6},{6,5},{7,4},{8,11},{9,10},{10,... | collective-permute-start | bytes 132104 | tf_op jit(solution)/shard_map/ppermute | solution.py:87
  27.9 2.2 %collective-permute-start.19 = (bf16[172,128]{1,0:T(8,128)(2,1)S(1)}, bf16[172,128]{1,0:T(8,128)(2,1)S(1)}, u32[]{:S(2)}, u32[]{:S(2)}) collective-permute-start(bf16[172,128]{1,0:T(8,128)(2,1)S(1)} %get-tuple-element.24), channel_id=1, source_target_pairs={{0,1},{1,0},{2,3},{3,2},{4,6},{5,7},{6,4},{7,5},{8,9},{9,8},{10,11... | collective-permute-start | bytes 132104 | tf_op jit(solution)/shard_map/ppermute | solution.py:87
  30.1 0.6 %shard_map.121 = bf16[128,256]{1,0:T(8,128)(2,1)} custom-call(bf16[128,256]{1,0:T(8,128)(2,1)S(1)} %collective-permute-done.11.value), custom_call_target="tpu_custom_call" | custom-call | tf_op jit(solution)/shard_map/pallas_call | solution.py:93
  30.7 1.0 %collective-permute-done.17.refs_1_ = bf16[172,128]{1,0:T(8,128)(2,1)S(1)} collective-permute-done((bf16[172,128]{1,0:T(8,128)(2,1)S(1)}, bf16[172,128]{1,0:T(8,128)(2,1)S(1)}, u32[]{:S(2)}, u32[]{:S(2)}) %collective-permute-start.17) | collective-permute-done | bytes 44064 | tf_op jit(solution)/shard_map/ppermute | solution.py:87
  31.7 1.9 %collective-permute-done.18.refs_2_ = bf16[172,128]{1,0:T(8,128)(2,1)S(1)} collective-permute-done((bf16[172,128]{1,0:T(8,128)(2,1)S(1)}, bf16[172,128]{1,0:T(8,128)(2,1)S(1)}, u32[]{:S(2)}, u32[]{:S(2)}) %collective-permute-start.18) | collective-permute-done | bytes 44064 | tf_op jit(solution)/shard_map/ppermute | solution.py:87
  33.6 0.7 %shard_map.123 = f32[172,1,128]{2,1,0:T(1,128)} custom-call(bf16[172,128]{1,0:T(8,128)(2,1)S(1)} %get-tuple-element.21.refs_0_, bf16[172,128]{1,0:T(8,128)(2,1)S(1)} %collective-permute-done.17.refs_1_, bf16[172,128]{1,0:T(8,128)(2,1)S(1)} %collective-permute-done.18.refs_2_, bf16[172,128]{1,0:T(8,128)(2,1)S(1)} %collective-permute-done.19.refs_3_, ...), custom_call_target="tpu_custom_call" | custom-call | tf_op jit(solution)/shard_map/pallas_call | solution.py:93
  (41 shorter events, 2.9 us)
Async XLA Ops:
  0.6 8.3 %copy-start.4 = (f32[172]{0:T(256)S(1)}, f32[172]{0:T(256)}, u32[]{:S(2)}) copy-start(f32[172]{0:T(256)} %param.19) | copy-start | bytes 2068
  0.7 7.8 %collective-permute-start.2 = (bf16[128,128]{1,0:T(8,128)(2,1)}, bf16[128,128]{1,0:T(8,128)(2,1)S(1)}, u32[]{:S(2)}, u32[]{:S(2)}) collective-permute-start(bf16[128,128]{1,0:T(8,128)(2,1)} %bitcast.18), channel_id=1, source_target_pairs={{28,0},{24,4},{20,8},{16,12},{12,16},{8,20},{4,24},{0,28},{29,1},{... | collective-permute-start | bytes 98312 | tf_op jit(solution)/shard_map/ppermute | solution.py:40
  4.1 4.5 %collective-permute-start.1 = (bf16[128,128]{1,0:T(8,128)(2,1)}, bf16[128,128]{1,0:T(8,128)(2,1)S(1)}, u32[]{:S(2)}, u32[]{:S(2)}) collective-permute-start(bf16[128,128]{1,0:T(8,128)(2,1)} %bitcast.19), channel_id=1, source_target_pairs={{12,0},{16,4},{4,8},{24,12},{28,16},{0,20},{20,24},{8,28},{13,1},{... | collective-permute-start | bytes 98312 | tf_op jit(solution)/shard_map/ppermute | solution.py:40
  4.9 3.8 %collective-permute-start = (bf16[128,128]{1,0:T(8,128)(2,1)}, bf16[128,128]{1,0:T(8,128)(2,1)S(1)}, u32[]{:S(2)}, u32[]{:S(2)}) collective-permute-start(bf16[128,128]{1,0:T(8,128)(2,1)} %bitcast.20), channel_id=1, source_target_pairs={{20,0},{8,4},{28,8},{0,12},{4,16},{24,20},{12,24},{16,28},{21,1},{... | collective-permute-start | bytes 98312 | tf_op jit(solution)/shard_map/ppermute | solution.py:40
  6.5 11.6 %copy-start = (bf16[256,172]{0,1:T(8,128)(2,1)S(1)}, bf16[256,172]{0,1:T(8,128)(2,1)}, u32[]{:S(2)}) copy-start(bf16[256,172]{0,1:T(8,128)(2,1)} %param.18) | copy-start | bytes 264196
  6.5 11.6 %copy-start.2 = (bf16[128,256]{1,0:T(8,128)(2,1)S(1)}, bf16[128,256]{1,0:T(8,128)(2,1)}, u32[]{:S(2)}) copy-start(bf16[128,256]{1,0:T(8,128)(2,1)} %refs_5_.1) | copy-start | bytes 196612
  6.5 11.6 %copy-start.5 = (f32[256]{0:T(256)S(1)}, f32[256]{0:T(256)}, u32[]{:S(2)}) copy-start(f32[256]{0:T(256)} %param.17) | copy-start | bytes 3076
  8.7 1.4 %collective-permute-start.3 = (bf16[512,128]{1,0:T(8,128)(2,1)S(1)}, bf16[512,128]{1,0:T(8,128)(2,1)S(1)}, u32[]{:S(2)}, u32[]{:S(2)}) collective-permute-start(bf16[512,128]{1,0:T(8,128)(2,1)S(1)} %shard_map.114.mine_ref.refs_0_), channel_id=1, source_target_pairs={{0,4},{4,0},{8,12},{12,8},{16,20},{20,16},{24,28},{28,24},{1,5},{5... | collective-permute-start | bytes 393224 | tf_op jit(solution)/shard_map/ppermute | solution.py:36
  9.0 5.7 %collective-permute-start.8 = (bf16[128,256]{1,0:T(8,128)(2,1)S(1)}, bf16[128,256]{1,0:T(8,128)(2,1)S(1)}, u32[]{:S(2)}, u32[]{:S(2)}) collective-permute-start(bf16[128,256]{1,0:T(8,128)(2,1)S(1)} %get-tuple-element.18), channel_id=1, source_target_pairs={{0,4},{4,0},{8,12},{12,8},{16,20},{20,16},{24,28},{28,24},{1,5},{5... | collective-permute-start | bytes 196616 | tf_op jit(solution)/shard_map/ppermute | solution.py:36
  10.4 5.2 %collective-permute-start.4 = (bf16[128,128]{1,0:T(8,128)(2,1)S(1)}, bf16[128,128]{1,0:T(8,128)(2,1)S(1)}, u32[]{:S(2)}, u32[]{:S(2)}) collective-permute-start(bf16[128,128]{1,0:T(8,128)(2,1)S(1)} %get-tuple-element.14), channel_id=1, source_target_pairs={{0,7},{1,6},{2,5},{3,4},{4,3},{5,2},{6,1},{7,0},{8,15},{9,14},{10,... | collective-permute-start | bytes 98312 | tf_op jit(solution)/shard_map/ppermute | solution.py:64
  13.8 4.3 %collective-permute-start.5 = (bf16[128,128]{1,0:T(8,128)(2,1)S(1)}, bf16[128,128]{1,0:T(8,128)(2,1)S(1)}, u32[]{:S(2)}, u32[]{:S(2)}) collective-permute-start(bf16[128,128]{1,0:T(8,128)(2,1)S(1)} %get-tuple-element.15), channel_id=1, source_target_pairs={{0,6},{1,7},{2,4},{3,5},{4,2},{5,3},{6,0},{7,1},{8,14},{9,15},{10,... | collective-permute-start | bytes 98312 | tf_op jit(solution)/shard_map/ppermute | solution.py:64
  13.8 4.3 %collective-permute-start.6 = (bf16[128,128]{1,0:T(8,128)(2,1)S(1)}, bf16[128,128]{1,0:T(8,128)(2,1)S(1)}, u32[]{:S(2)}, u32[]{:S(2)}) collective-permute-start(bf16[128,128]{1,0:T(8,128)(2,1)S(1)} %get-tuple-element.16), channel_id=1, source_target_pairs={{0,5},{1,4},{2,7},{3,6},{4,1},{5,0},{6,3},{7,2},{8,13},{9,12},{10,... | collective-permute-start | bytes 98312 | tf_op jit(solution)/shard_map/ppermute | solution.py:64
  14.4 3.6 %collective-permute-start.7 = (bf16[128,128]{1,0:T(8,128)(2,1)S(1)}, bf16[128,128]{1,0:T(8,128)(2,1)S(1)}, u32[]{:S(2)}, u32[]{:S(2)}) collective-permute-start(bf16[128,128]{1,0:T(8,128)(2,1)S(1)} %get-tuple-element.17), channel_id=1, source_target_pairs={{0,4},{1,5},{2,6},{3,7},{4,0},{5,1},{6,2},{7,3},{8,12},{9,13},{10,... | collective-permute-start | bytes 98312 | tf_op jit(solution)/shard_map/ppermute | solution.py:64
  18.5 4.6 %collective-permute-start.10 = (bf16[172,128]{1,0:T(8,128)(2,1)S(1)}, bf16[172,128]{1,0:T(8,128)(2,1)S(1)}, u32[]{:S(2)}, u32[]{:S(2)}) collective-permute-start(bf16[172,128]{1,0:T(8,128)(2,1)S(1)} %get-tuple-element.20.refs_0_), channel_id=1, source_target_pairs={{28,0},{24,4},{20,8},{16,12},{12,16},{8,20},{4,24},{0,28},{29,1},{... | collective-permute-start | bytes 132104 | tf_op jit(solution)/shard_map/ppermute | solution.py:40
  19.8 3.9 %collective-permute-start.9 = (bf16[172,128]{1,0:T(8,128)(2,1)S(1)}, bf16[172,128]{1,0:T(8,128)(2,1)S(1)}, u32[]{:S(2)}, u32[]{:S(2)}) collective-permute-start(bf16[172,128]{1,0:T(8,128)(2,1)S(1)} %get-tuple-element.20.refs_0_), channel_id=1, source_target_pairs={{12,0},{16,4},{4,8},{24,12},{28,16},{0,20},{20,24},{8,28},{13,1},{... | collective-permute-start | bytes 132104 | tf_op jit(solution)/shard_map/ppermute | solution.py:40
  20.6 4.0 %collective-permute-start.16 = (bf16[172,128]{1,0:T(8,128)(2,1)S(1)}, bf16[172,128]{1,0:T(8,128)(2,1)S(1)}, u32[]{:S(2)}, u32[]{:S(2)}) collective-permute-start(bf16[172,128]{1,0:T(8,128)(2,1)S(1)} %get-tuple-element.20.refs_0_), channel_id=1, source_target_pairs={{8,0},{20,4},{0,8},{28,12},{24,16},{4,20},{16,24},{12,28},{9,1},{2... | collective-permute-start | bytes 132104 | tf_op jit(solution)/shard_map/ppermute | solution.py:40
  21.7 3.5 %collective-permute-start.13 = (bf16[172,128]{1,0:T(8,128)(2,1)S(1)}, bf16[172,128]{1,0:T(8,128)(2,1)S(1)}, u32[]{:S(2)}, u32[]{:S(2)}) collective-permute-start(bf16[172,128]{1,0:T(8,128)(2,1)S(1)} %get-tuple-element.20.refs_0_), channel_id=1, source_target_pairs={{20,0},{8,4},{28,8},{0,12},{4,16},{24,20},{12,24},{16,28},{21,1},{... | collective-permute-start | bytes 132104 | tf_op jit(solution)/shard_map/ppermute | solution.py:40
  22.1 3.1 %collective-permute-start.12 = (bf16[172,128]{1,0:T(8,128)(2,1)S(1)}, bf16[172,128]{1,0:T(8,128)(2,1)S(1)}, u32[]{:S(2)}, u32[]{:S(2)}) collective-permute-start(bf16[172,128]{1,0:T(8,128)(2,1)S(1)} %get-tuple-element.20.refs_0_), channel_id=1, source_target_pairs={{0,4},{4,0},{8,12},{12,8},{16,20},{20,16},{24,28},{28,24},{1,5},{5... | collective-permute-start | bytes 132104 | tf_op jit(solution)/shard_map/ppermute | solution.py:36
  23.1 2.1 %collective-permute-start.14 = (bf16[172,128]{1,0:T(8,128)(2,1)S(1)}, bf16[172,128]{1,0:T(8,128)(2,1)S(1)}, u32[]{:S(2)}, u32[]{:S(2)}) collective-permute-start(bf16[172,128]{1,0:T(8,128)(2,1)S(1)} %collective-permute-done.10.refs_2_), channel_id=1, source_target_pairs={{0,4},{4,0},{8,12},{12,8},{16,20},{20,16},{24,28},{28,24},{1,5},{5... | collective-permute-start | bytes 132104 | tf_op jit(solution)/shard_map/ppermute | solution.py:36
  23.7 1.5 %collective-permute-start.15 = (bf16[172,128]{1,0:T(8,128)(2,1)S(1)}, bf16[172,128]{1,0:T(8,128)(2,1)S(1)}, u32[]{:S(2)}, u32[]{:S(2)}) collective-permute-start(bf16[172,128]{1,0:T(8,128)(2,1)S(1)} %collective-permute-done.9.refs_1_), channel_id=1, source_target_pairs={{0,4},{4,0},{8,12},{12,8},{16,20},{20,16},{24,28},{28,24},{1,5},{5... | collective-permute-start | bytes 132104 | tf_op jit(solution)/shard_map/ppermute | solution.py:36
  24.7 5.4 %collective-permute-start.11 = (bf16[128,256]{1,0:T(8,128)(2,1)S(1)}, bf16[128,256]{1,0:T(8,128)(2,1)S(1)}, u32[]{:S(2)}, u32[]{:S(2)}) collective-permute-start(bf16[128,256]{1,0:T(8,128)(2,1)S(1)} %shard_map.120), channel_id=1, source_target_pairs={{0,4},{4,0},{8,12},{12,8},{16,20},{20,16},{24,28},{28,24},{1,5},{5... | collective-permute-start | bytes 196616 | tf_op jit(solution)/shard_map/ppermute | solution.py:36
  25.6 6.1 %collective-permute-start.17 = (bf16[172,128]{1,0:T(8,128)(2,1)S(1)}, bf16[172,128]{1,0:T(8,128)(2,1)S(1)}, u32[]{:S(2)}, u32[]{:S(2)}) collective-permute-start(bf16[172,128]{1,0:T(8,128)(2,1)S(1)} %get-tuple-element.22), channel_id=1, source_target_pairs={{0,3},{1,2},{2,1},{3,0},{4,7},{5,6},{6,5},{7,4},{8,11},{9,10},{10,... | collective-permute-start | bytes 132104 | tf_op jit(solution)/shard_map/ppermute | solution.py:87
  27.6 6.0 %collective-permute-start.18 = (bf16[172,128]{1,0:T(8,128)(2,1)S(1)}, bf16[172,128]{1,0:T(8,128)(2,1)S(1)}, u32[]{:S(2)}, u32[]{:S(2)}) collective-permute-start(bf16[172,128]{1,0:T(8,128)(2,1)S(1)} %get-tuple-element.23), channel_id=1, source_target_pairs={{0,2},{1,3},{2,0},{3,1},{4,5},{5,4},{6,7},{7,6},{8,10},{9,11},{10,... | collective-permute-start | bytes 132104 | tf_op jit(solution)/shard_map/ppermute | solution.py:87
  27.9 5.7 %collective-permute-start.19 = (bf16[172,128]{1,0:T(8,128)(2,1)S(1)}, bf16[172,128]{1,0:T(8,128)(2,1)S(1)}, u32[]{:S(2)}, u32[]{:S(2)}) collective-permute-start(bf16[172,128]{1,0:T(8,128)(2,1)S(1)} %get-tuple-element.24), channel_id=1, source_target_pairs={{0,1},{1,0},{2,3},{3,2},{4,6},{5,7},{6,4},{7,5},{8,9},{9,8},{10,11... | collective-permute-start | bytes 132104 | tf_op jit(solution)/shard_map/ppermute | solution.py:87
  (3 other events, 24.5 us)

commit v4 on v0

--- a/solution.py
+++ b/solution.py
@@ -202,24 +202,37 @@
     )
 
 
-def layer_two_kernel(n_col, dense_ref, first_ref, own_ref, near_ref, *refs):
-    blocks, outputs, scratch = refs[: -n_col - 1], refs[-n_col - 1 : -1], refs[-1]
-    block, half = near_ref.shape[1], scratch.shape[1]
-    rest = lanes([own_ref, *blocks], scratch)
-    total = first_ref[...] + dot_nt(rest, dense_ref[:, :half])
-    total += dot_nt(near_ref[...], dense_ref[:, dense_ref.shape[1] - block :])
-    for k, out in enumerate(outputs):
-        out[...] = total[:, k * block : (k + 1) * block].astype(BF16)
-
-
-def logits_kernel(n_col, pieces, *refs):
-    parts = refs[:n_col]
-    proj, bias, out_hbm, staged, sems = refs[n_col:]
+def layer_two_kernel(slots, dense_ref, first_ref, near_ref, rest_ref, *refs):
+    outputs = refs[-len(slots) :]
+    block, half = near_ref.shape[1], rest_ref.shape[1]
+    at = slice(slots[0] * block, (slots[-1] + 1) * block)
+    total = first_ref[:, at] + dot_nt(rest_ref[...], dense_ref[at, :half])
+    total += dot_nt(near_ref[...], dense_ref[at, dense_ref.shape[1] - block :])
+    for i, out in enumerate(outputs):
+        out[...] = total[:, i * block : (i + 1) * block].astype(BF16)
+
+
+def sent_two_kernel(slots, dense_ref, first_ref, own_ref, near_ref, *refs):
+    rest = refs[-1]
+    blocks, outputs = refs[: -len(slots) - 1], refs[-len(slots) - 1 : -1]
+    lanes([own_ref, *blocks], rest)
+    layer_two_kernel(slots, dense_ref, first_ref, near_ref, rest, *outputs)
+
+
+def begin_kernel(*refs):
+    total = refs[0][...].astype(F32)
+    for ref in refs[1:-1]:
+        total += ref[...].astype(F32)
+    refs[-1][...] = total
+
+
+def logits_kernel(pieces, begun, *refs):
+    parts, (out_hbm, staged, sems) = refs[:-3], refs[-3:]
     step = -(-staged.shape[0] // pieces // 16) * 16
     copies = []
     for i in range(pieces):
         rows = slice(i * step, (i + 1) * step if i < pieces - 1 else staged.shape[0])
-        total = proj[rows, :].astype(F32) + bias[rows, :]
+        total = begun[rows, :]
         for part in parts:
             total += part[rows, :].astype(F32)
         staged[rows, 0, :] = total
@@ -357,12 +370,20 @@
         pushed = call(
             late_kernel, shape((block, hid), BF16), (pushed, half_two), specs=[vmem, anywhere]
         )
-        parts_two = call(
-            functools.partial(layer_two_kernel, n_col),
-            [shape((classes, block), BF16)] * n_col,
+        sent = range(1, n_col)
+        *sent_two, rest = call(
+            functools.partial(sent_two_kernel, sent),
+            [shape((classes, block), BF16)] * len(sent)
+            + [shape((classes, len(late) * block), BF16)],
             (dense, half_two, late[0], near, *late[1:]),
-            scratch=[pltpu.VMEM((classes, len(late) * block), BF16)],
-        )
+        )
+        own_two = call(
+            functools.partial(layer_two_kernel, [0]),
+            [shape((classes, block), BF16)],
+            (dense, half_two, near, rest, sent_two[0]),
+            specs=[vmem] * 4 + [anywhere],
+        )
+        parts_two = [*own_two, *sent_two]
     else:
         other_slots = jnp.arange(n_row) ^ 1
         summed = call(
@@ -377,10 +398,15 @@
     arrived_two = send_each(parts_two, "col", n_col)
     pushed = call(write_kernel, shape((block, hid), BF16), (fetch_core(pushed, "row", n_row),))
     pieces = 4
+    begun_two = call(
+        begin_kernel,
+        shape((classes, block), F32),
+        (bias_cols, own_proj, parts_two[0], arrived_two[0]),
+    )
     scores = call(
-        functools.partial(logits_kernel, n_col, pieces),
+        functools.partial(logits_kernel, pieces),
         shape((classes, 1, block), F32),
-        (parts_two[0], *arrived_two, own_proj, bias_cols),
+        (begun_two, *arrived_two[1:]),
         scratch=[pltpu.VMEM((classes, 1, block), F32), pltpu.SemaphoreType.DMA((pieces,))],
         out_specs=pl.BlockSpec(memory_space=pl.ANY),
     )

time: 34.6 us -> 34.4 us (level)
  Pallas kernels: 4.62 us -> 5.27 us
  waiting for transfers between devices: 7.77 us -> 7.27 us
    ppermute x7, waiting for transfers between devices: 1.86 us -> 1.08 us  [fetched(): lax.ppermute(block, axis, [(partner(i, seen(slot, i)), i) for i in range(...]
    ppermute x4, waiting for transfers between devices: 2.8 us -> 3.49 us  [send_across(): arrived.append(lax.ppermute(blocks[slot], ('row', 'col'), pairs))]
    pallas_call x11 -> x13, Pallas kernels: 4.62 us -> 5.27 us  [call(): pl.pallas_call(kernel, out_shape=out_shape, in_specs=specs or [vmem] * le...]
    ppermute x9, waiting for transfers between devices: 3.11 us -> 2.71 us  [permuted(): lax.ppermute(block, axis, [(i, partner(i, slot)) for i in range(size)])]
  transfers between devices with their start and end apart: 20 -> 20, of which waited for: 9 -> 8; matrix products, arithmetic and copies ran while one was open for 0% -> 0% of each run, Pallas kernels for 10% -> 12%
where the time goes in v4:
time: 34.4 us; the launch traced here: 34.2 us
  starting transfers between devices  20.2 us (59%)
  waiting for transfers between devices  7.27 us (21%)
  Pallas kernels  5.27 us (15%)
  between operations  1.49 us (4%)
    ppermute x7, starting transfers between devices, fetched(): lax.ppermute(block, axis, [(partner(i, seen(slot, i)), i) for i in range(...  8.6 us
    ppermute x9, starting transfers between devices, permuted(): lax.ppermute(block, axis, [(i, partner(i, slot)) for i in range(size)])  7.14 us
    pallas_call x13, Pallas kernels, call(): pl.pallas_call(kernel, out_shape=out_shape, in_specs=specs or [vmem] * le...  5.27 us
    ppermute x4, starting transfers between devices, send_across(): arrived.append(lax.ppermute(blocks[slot], ('row', 'col'), pairs))  4.42 us
    ppermute x4, waiting for transfers between devices, send_across(): arrived.append(lax.ppermute(blocks[slot], ('row', 'col'), pairs))  3.49 us
    ppermute x9, waiting for transfers between devices, permuted(): lax.ppermute(block, axis, [(i, partner(i, slot)) for i in range(size)])  2.71 us
    ppermute x7, waiting for transfers between devices, fetched(): lax.ppermute(block, axis, [(partner(i, seen(slot, i)), i) for i in range(...  1.08 us
  transfers between devices with their start and end apart: 20, of which 8 were waited for; matrix products, arithmetic and copies ran while one was open for 0% of the time, Pallas kernels for 12%

profile of v4, /device:TPU:0, one launch (start us, length us, event | category | flops | bytes accessed | tf_op | source)
XLA Modules:
  0.0 34.2 jit_solution(17707387212565070855)
XLA Ops:
  0.7 3.4 %collective-permute-start.2 = (bf16[128,128]{1,0:T(8,128)(2,1)}, bf16[128,128]{1,0:T(8,128)(2,1)S(1)}, u32[]{:S(2)}, u32[]{:S(2)}) collective-permute-start(bf16[128,128]{1,0:T(8,128)(2,1)} %bitcast.18), channel_id=1, source_target_pairs={{28,0},{24,4},{20,8},{16,12},{12,16},{8,20},{4,24},{0,28},{29,1},{... | collective-permute-start | bytes 98312 | tf_op jit(solution)/shard_map/ppermute | solution.py:40
  4.1 0.8 %collective-permute-start.1 = (bf16[128,128]{1,0:T(8,128)(2,1)}, bf16[128,128]{1,0:T(8,128)(2,1)S(1)}, u32[]{:S(2)}, u32[]{:S(2)}) collective-permute-start(bf16[128,128]{1,0:T(8,128)(2,1)} %bitcast.19), channel_id=1, source_target_pairs={{12,0},{16,4},{4,8},{24,12},{28,16},{0,20},{20,24},{8,28},{13,1},{... | collective-permute-start | bytes 98312 | tf_op jit(solution)/shard_map/ppermute | solution.py:40
  4.9 1.0 %collective-permute-start = (bf16[128,128]{1,0:T(8,128)(2,1)}, bf16[128,128]{1,0:T(8,128)(2,1)S(1)}, u32[]{:S(2)}, u32[]{:S(2)}) collective-permute-start(bf16[128,128]{1,0:T(8,128)(2,1)} %bitcast.20), channel_id=1, source_target_pairs={{20,0},{8,4},{28,8},{0,12},{4,16},{24,20},{12,24},{16,28},{21,1},{... | collective-permute-start | bytes 98312 | tf_op jit(solution)/shard_map/ppermute | solution.py:40
  6.5 2.0 %shard_map.113.refs_4_.dense_ref = bf16[512,1024]{1,0:T(8,128)(2,1)S(1)} custom-call(s32[1,1]{1,0:T(1,128)S(6)} %copy.13.count, s32[2,128]{1,0:T(2,128)} %bitcast.28, bf16[128,128,128]{2,1,0:T(8,128)(2,1)} %bitcast.25), custom_call_target="tpu_custom_call" | custom-call | flops 2097152 | bytes 4194304 | tf_op jit(solution)/shard_map/pallas_call | solution.py:74
  9.1 0.3 collective-permute-start.8
  9.8 0.3 %collective-permute-done.3.other_ref.refs_4_ = bf16[512,128]{1,0:T(8,128)(2,1)S(1)} collective-permute-done((bf16[512,128]{1,0:T(8,128)(2,1)S(1)}, bf16[512,128]{1,0:T(8,128)(2,1)S(1)}, u32[]{:S(2)}, u32[]{:S(2)}) %collective-permute-start.3) | collective-permute-done | bytes 131104 | tf_op jit(solution)/shard_map/ppermute | solution.py:36
  10.4 3.7 %collective-permute-start.4 = (bf16[128,128]{1,0:T(8,128)(2,1)S(1)}, bf16[128,128]{1,0:T(8,128)(2,1)S(1)}, u32[]{:S(2)}, u32[]{:S(2)}) collective-permute-start(bf16[128,128]{1,0:T(8,128)(2,1)S(1)} %get-tuple-element.14), channel_id=1, source_target_pairs={{0,7},{1,6},{2,5},{3,4},{4,3},{5,2},{6,1},{7,0},{8,15},{9,14},{10,... | collective-permute-start | bytes 98312 | tf_op jit(solution)/shard_map/ppermute | solution.py:64
  14.1 0.4 %collective-permute-start.6 = (bf16[128,128]{1,0:T(8,128)(2,1)S(1)}, bf16[128,128]{1,0:T(8,128)(2,1)S(1)}, u32[]{:S(2)}, u32[]{:S(2)}) collective-permute-start(bf16[128,128]{1,0:T(8,128)(2,1)S(1)} %get-tuple-element.16), channel_id=1, source_target_pairs={{0,5},{1,4},{2,7},{3,6},{4,1},{5,0},{6,3},{7,2},{8,13},{9,12},{10,... | collective-permute-start | bytes 98312 | tf_op jit(solution)/shard_map/ppermute | solution.py:64
  14.5 0.3 %collective-permute-start.7 = (bf16[128,128]{1,0:T(8,128)(2,1)S(1)}, bf16[128,128]{1,0:T(8,128)(2,1)S(1)}, u32[]{:S(2)}, u32[]{:S(2)}) collective-permute-start(bf16[128,128]{1,0:T(8,128)(2,1)S(1)} %get-tuple-element.17), channel_id=1, source_target_pairs={{0,4},{1,5},{2,6},{3,7},{4,0},{5,1},{6,2},{7,3},{8,12},{9,13},{10,... | collective-permute-start | bytes 98312 | tf_op jit(solution)/shard_map/ppermute | solution.py:64
  14.8 1.0 %collective-permute-done.4.refs_0_ = bf16[128,128]{1,0:T(8,128)(2,1)S(1)} collective-permute-done((bf16[128,128]{1,0:T(8,128)(2,1)S(1)}, bf16[128,128]{1,0:T(8,128)(2,1)S(1)}, u32[]{:S(2)}, u32[]{:S(2)}) %collective-permute-start.4) | collective-permute-done | bytes 32800 | tf_op jit(solution)/shard_map/ppermute | solution.py:64
  15.8 2.5 %collective-permute-done.5.refs_1_ = bf16[128,128]{1,0:T(8,128)(2,1)S(1)} collective-permute-done((bf16[128,128]{1,0:T(8,128)(2,1)S(1)}, bf16[128,128]{1,0:T(8,128)(2,1)S(1)}, u32[]{:S(2)}, u32[]{:S(2)}) %collective-permute-start.5) | collective-permute-done | bytes 32800 | tf_op jit(solution)/shard_map/ppermute | solution.py:64
  18.7 1.1 %collective-permute-start.10 = (bf16[172,128]{1,0:T(8,128)(2,1)S(1)}, bf16[172,128]{1,0:T(8,128)(2,1)S(1)}, u32[]{:S(2)}, u32[]{:S(2)}) collective-permute-start(bf16[172,128]{1,0:T(8,128)(2,1)S(1)} %get-tuple-element.20.refs_0_), channel_id=1, source_target_pairs={{28,0},{24,4},{20,8},{16,12},{12,16},{8,20},{4,24},{0,28},{29,1},{... | collective-permute-start | bytes 132104 | tf_op jit(solution)/shard_map/ppermute | solution.py:40
  19.8 0.8 %collective-permute-start.9 = (bf16[172,128]{1,0:T(8,128)(2,1)S(1)}, bf16[172,128]{1,0:T(8,128)(2,1)S(1)}, u32[]{:S(2)}, u32[]{:S(2)}) collective-permute-start(bf16[172,128]{1,0:T(8,128)(2,1)S(1)} %get-tuple-element.20.refs_0_), channel_id=1, source_target_pairs={{12,0},{16,4},{4,8},{24,12},{28,16},{0,20},{20,24},{8,28},{13,1},{... | collective-permute-start | bytes 132104 | tf_op jit(solution)/shard_map/ppermute | solution.py:40
  20.6 1.3 %collective-permute-start.16 = (bf16[172,128]{1,0:T(8,128)(2,1)S(1)}, bf16[172,128]{1,0:T(8,128)(2,1)S(1)}, u32[]{:S(2)}, u32[]{:S(2)}) collective-permute-start(bf16[172,128]{1,0:T(8,128)(2,1)S(1)} %get-tuple-element.20.refs_0_), channel_id=1, source_target_pairs={{8,0},{20,4},{0,8},{28,12},{24,16},{4,20},{16,24},{12,28},{9,1},{2... | collective-permute-start | bytes 132104 | tf_op jit(solution)/shard_map/ppermute | solution.py:40
  22.1 0.9 %collective-permute-start.12 = (bf16[172,128]{1,0:T(8,128)(2,1)S(1)}, bf16[172,128]{1,0:T(8,128)(2,1)S(1)}, u32[]{:S(2)}, u32[]{:S(2)}) collective-permute-start(bf16[172,128]{1,0:T(8,128)(2,1)S(1)} %get-tuple-element.20.refs_0_), channel_id=1, source_target_pairs={{0,4},{4,0},{8,12},{12,8},{16,20},{20,16},{24,28},{28,24},{1,5},{5... | collective-permute-start | bytes 132104 | tf_op jit(solution)/shard_map/ppermute | solution.py:36
  23.7 0.7 %collective-permute-start.15 = (bf16[172,128]{1,0:T(8,128)(2,1)S(1)}, bf16[172,128]{1,0:T(8,128)(2,1)S(1)}, u32[]{:S(2)}, u32[]{:S(2)}) collective-permute-start(bf16[172,128]{1,0:T(8,128)(2,1)S(1)} %collective-permute-done.9.refs_1_), channel_id=1, source_target_pairs={{0,4},{4,0},{8,12},{12,8},{16,20},{20,16},{24,28},{28,24},{1,5},{5... | collective-permute-start | bytes 132104 | tf_op jit(solution)/shard_map/ppermute | solution.py:36
  24.8 0.6 %collective-permute-done.13.near_ref = bf16[172,128]{1,0:T(8,128)(2,1)S(1)} collective-permute-done((bf16[172,128]{1,0:T(8,128)(2,1)S(1)}, bf16[172,128]{1,0:T(8,128)(2,1)S(1)}, u32[]{:S(2)}, u32[]{:S(2)}) %collective-permute-start.13) | collective-permute-done | bytes 44064 | tf_op jit(solution)/shard_map/ppermute | solution.py:40
  25.4 0.3 shard_map.122
  25.8 2.0 %collective-permute-start.17 = (bf16[172,128]{1,0:T(8,128)(2,1)S(1)}, bf16[172,128]{1,0:T(8,128)(2,1)S(1)}, u32[]{:S(2)}, u32[]{:S(2)}) collective-permute-start(bf16[172,128]{1,0:T(8,128)(2,1)S(1)} %get-tuple-element.24), channel_id=1, source_target_pairs={{0,3},{1,2},{2,1},{3,0},{4,7},{5,6},{6,5},{7,4},{8,11},{9,10},{10,... | collective-permute-start | bytes 132104 | tf_op jit(solution)/shard_map/ppermute | solution.py:36
  27.8 2.4 %collective-permute-start.19 = (bf16[172,128]{1,0:T(8,128)(2,1)S(1)}, bf16[172,128]{1,0:T(8,128)(2,1)S(1)}, u32[]{:S(2)}, u32[]{:S(2)}) collective-permute-start(bf16[172,128]{1,0:T(8,128)(2,1)S(1)} %get-tuple-element.23.refs_0_), channel_id=1, source_target_pairs={{0,1},{1,0},{2,3},{3,2},{4,5},{5,4},{6,7},{7,6},{8,9},{9,8},{10,11... | collective-permute-start | bytes 132104 | tf_op jit(solution)/shard_map/ppermute | solution.py:36
  30.5 0.6 %shard_map.121 = bf16[128,256]{1,0:T(8,128)(2,1)} custom-call(bf16[128,256]{1,0:T(8,128)(2,1)S(1)} %collective-permute-done.11.value), custom_call_target="tpu_custom_call" | custom-call | tf_op jit(solution)/shard_map/pallas_call | solution.py:74
  31.1 1.0 %collective-permute-done.17.refs_3_ = bf16[172,128]{1,0:T(8,128)(2,1)S(1)} collective-permute-done((bf16[172,128]{1,0:T(8,128)(2,1)S(1)}, bf16[172,128]{1,0:T(8,128)(2,1)S(1)}, u32[]{:S(2)}, u32[]{:S(2)}) %collective-permute-start.17) | collective-permute-done | bytes 44064 | tf_op jit(solution)/shard_map/ppermute | solution.py:36
  32.2 1.3 %collective-permute-done.18.refs_0_ = bf16[172,128]{1,0:T(8,128)(2,1)S(1)} collective-permute-done((bf16[172,128]{1,0:T(8,128)(2,1)S(1)}, bf16[172,128]{1,0:T(8,128)(2,1)S(1)}, u32[]{:S(2)}, u32[]{:S(2)}) %collective-permute-start.18) | collective-permute-done | bytes 44064 | tf_op jit(solution)/shard_map/ppermute | solution.py:36
  33.5 0.7 %shard_map.125 = f32[172,1,128]{2,1,0:T(1,128)} custom-call(f32[172,128]{1,0:T(8,128)S(1)} %shard_map.124.begun, bf16[172,128]{1,0:T(8,128)(2,1)S(1)} %collective-permute-done.18.refs_0_, bf16[172,128]{1,0:T(8,128)(2,1)S(1)} %collective-permute-done.19.refs_1_), custom_call_target="tpu_custom_call" | custom-call | tf_op jit(solution)/shard_map/pallas_call | solution.py:74
  (43 shorter events, 3.0 us)
Async XLA Ops:
  0.6 8.4 %copy-start.4 = (f32[172]{0:T(256)S(1)}, f32[172]{0:T(256)}, u32[]{:S(2)}) copy-start(f32[172]{0:T(256)} %param.19) | copy-start | bytes 2068
  0.7 7.8 %collective-permute-start.2 = (bf16[128,128]{1,0:T(8,128)(2,1)}, bf16[128,128]{1,0:T(8,128)(2,1)S(1)}, u32[]{:S(2)}, u32[]{:S(2)}) collective-permute-start(bf16[128,128]{1,0:T(8,128)(2,1)} %bitcast.18), channel_id=1, source_target_pairs={{28,0},{24,4},{20,8},{16,12},{12,16},{8,20},{4,24},{0,28},{29,1},{... | collective-permute-start | bytes 98312 | tf_op jit(solution)/shard_map/ppermute | solution.py:40
  4.1 4.5 %collective-permute-start.1 = (bf16[128,128]{1,0:T(8,128)(2,1)}, bf16[128,128]{1,0:T(8,128)(2,1)S(1)}, u32[]{:S(2)}, u32[]{:S(2)}) collective-permute-start(bf16[128,128]{1,0:T(8,128)(2,1)} %bitcast.19), channel_id=1, source_target_pairs={{12,0},{16,4},{4,8},{24,12},{28,16},{0,20},{20,24},{8,28},{13,1},{... | collective-permute-start | bytes 98312 | tf_op jit(solution)/shard_map/ppermute | solution.py:40
  4.9 3.8 %collective-permute-start = (bf16[128,128]{1,0:T(8,128)(2,1)}, bf16[128,128]{1,0:T(8,128)(2,1)S(1)}, u32[]{:S(2)}, u32[]{:S(2)}) collective-permute-start(bf16[128,128]{1,0:T(8,128)(2,1)} %bitcast.20), channel_id=1, source_target_pairs={{20,0},{8,4},{28,8},{0,12},{4,16},{24,20},{12,24},{16,28},{21,1},{... | collective-permute-start | bytes 98312 | tf_op jit(solution)/shard_map/ppermute | solution.py:40
  6.5 11.9 %copy-start = (bf16[256,172]{0,1:T(8,128)(2,1)S(1)}, bf16[256,172]{0,1:T(8,128)(2,1)}, u32[]{:S(2)}) copy-start(bf16[256,172]{0,1:T(8,128)(2,1)} %param.18) | copy-start | bytes 264196
  6.5 11.9 %copy-start.2 = (bf16[128,256]{1,0:T(8,128)(2,1)S(1)}, bf16[128,256]{1,0:T(8,128)(2,1)}, u32[]{:S(2)}) copy-start(bf16[128,256]{1,0:T(8,128)(2,1)} %refs_5_.1) | copy-start | bytes 196612
  6.5 11.9 %copy-start.5 = (f32[256]{0:T(256)S(1)}, f32[256]{0:T(256)}, u32[]{:S(2)}) copy-start(f32[256]{0:T(256)} %param.17) | copy-start | bytes 3076
  8.7 1.4 %collective-permute-start.3 = (bf16[512,128]{1,0:T(8,128)(2,1)S(1)}, bf16[512,128]{1,0:T(8,128)(2,1)S(1)}, u32[]{:S(2)}, u32[]{:S(2)}) collective-permute-start(bf16[512,128]{1,0:T(8,128)(2,1)S(1)} %shard_map.114.mine_ref.refs_0_), channel_id=1, source_target_pairs={{0,4},{4,0},{8,12},{12,8},{16,20},{20,16},{24,28},{28,24},{1,5},{5... | collective-permute-start | bytes 393224 | tf_op jit(solution)/shard_map/ppermute | solution.py:36
  9.1 5.7 %collective-permute-start.8 = (bf16[128,256]{1,0:T(8,128)(2,1)S(1)}, bf16[128,256]{1,0:T(8,128)(2,1)S(1)}, u32[]{:S(2)}, u32[]{:S(2)}) collective-permute-start(bf16[128,256]{1,0:T(8,128)(2,1)S(1)} %get-tuple-element.18), channel_id=1, source_target_pairs={{0,4},{4,0},{8,12},{12,8},{16,20},{20,16},{24,28},{28,24},{1,5},{5... | collective-permute-start | bytes 196616 | tf_op jit(solution)/shard_map/ppermute | solution.py:36
  10.4 5.4 %collective-permute-start.4 = (bf16[128,128]{1,0:T(8,128)(2,1)S(1)}, bf16[128,128]{1,0:T(8,128)(2,1)S(1)}, u32[]{:S(2)}, u32[]{:S(2)}) collective-permute-start(bf16[128,128]{1,0:T(8,128)(2,1)S(1)} %get-tuple-element.14), channel_id=1, source_target_pairs={{0,7},{1,6},{2,5},{3,4},{4,3},{5,2},{6,1},{7,0},{8,15},{9,14},{10,... | collective-permute-start | bytes 98312 | tf_op jit(solution)/shard_map/ppermute | solution.py:64
  14.1 4.2 %collective-permute-start.5 = (bf16[128,128]{1,0:T(8,128)(2,1)S(1)}, bf16[128,128]{1,0:T(8,128)(2,1)S(1)}, u32[]{:S(2)}, u32[]{:S(2)}) collective-permute-start(bf16[128,128]{1,0:T(8,128)(2,1)S(1)} %get-tuple-element.15), channel_id=1, source_target_pairs={{0,6},{1,7},{2,4},{3,5},{4,2},{5,3},{6,0},{7,1},{8,14},{9,15},{10,... | collective-permute-start | bytes 98312 | tf_op jit(solution)/shard_map/ppermute | solution.py:64
  14.1 4.2 %collective-permute-start.6 = (bf16[128,128]{1,0:T(8,128)(2,1)S(1)}, bf16[128,128]{1,0:T(8,128)(2,1)S(1)}, u32[]{:S(2)}, u32[]{:S(2)}) collective-permute-start(bf16[128,128]{1,0:T(8,128)(2,1)S(1)} %get-tuple-element.16), channel_id=1, source_target_pairs={{0,5},{1,4},{2,7},{3,6},{4,1},{5,0},{6,3},{7,2},{8,13},{9,12},{10,... | collective-permute-start | bytes 98312 | tf_op jit(solution)/shard_map/ppermute | solution.py:64
  14.5 3.8 %collective-permute-start.7 = (bf16[128,128]{1,0:T(8,128)(2,1)S(1)}, bf16[128,128]{1,0:T(8,128)(2,1)S(1)}, u32[]{:S(2)}, u32[]{:S(2)}) collective-permute-start(bf16[128,128]{1,0:T(8,128)(2,1)S(1)} %get-tuple-element.17), channel_id=1, source_target_pairs={{0,4},{1,5},{2,6},{3,7},{4,0},{5,1},{6,2},{7,3},{8,12},{9,13},{10,... | collective-permute-start | bytes 98312 | tf_op jit(solution)/shard_map/ppermute | solution.py:64
  18.7 4.7 %collective-permute-start.10 = (bf16[172,128]{1,0:T(8,128)(2,1)S(1)}, bf16[172,128]{1,0:T(8,128)(2,1)S(1)}, u32[]{:S(2)}, u32[]{:S(2)}) collective-permute-start(bf16[172,128]{1,0:T(8,128)(2,1)S(1)} %get-tuple-element.20.refs_0_), channel_id=1, source_target_pairs={{28,0},{24,4},{20,8},{16,12},{12,16},{8,20},{4,24},{0,28},{29,1},{... | collective-permute-start | bytes 132104 | tf_op jit(solution)/shard_map/ppermute | solution.py:40
  19.8 3.9 %collective-permute-start.9 = (bf16[172,128]{1,0:T(8,128)(2,1)S(1)}, bf16[172,128]{1,0:T(8,128)(2,1)S(1)}, u32[]{:S(2)}, u32[]{:S(2)}) collective-permute-start(bf16[172,128]{1,0:T(8,128)(2,1)S(1)} %get-tuple-element.20.refs_0_), channel_id=1, source_target_pairs={{12,0},{16,4},{4,8},{24,12},{28,16},{0,20},{20,24},{8,28},{13,1},{... | collective-permute-start | bytes 132104 | tf_op jit(solution)/shard_map/ppermute | solution.py:40
  20.6 4.1 %collective-permute-start.16 = (bf16[172,128]{1,0:T(8,128)(2,1)S(1)}, bf16[172,128]{1,0:T(8,128)(2,1)S(1)}, u32[]{:S(2)}, u32[]{:S(2)}) collective-permute-start(bf16[172,128]{1,0:T(8,128)(2,1)S(1)} %get-tuple-element.20.refs_0_), channel_id=1, source_target_pairs={{8,0},{20,4},{0,8},{28,12},{24,16},{4,20},{16,24},{12,28},{9,1},{2... | collective-permute-start | bytes 132104 | tf_op jit(solution)/shard_map/ppermute | solution.py:40
  22.0 3.5 %collective-permute-start.13 = (bf16[172,128]{1,0:T(8,128)(2,1)S(1)}, bf16[172,128]{1,0:T(8,128)(2,1)S(1)}, u32[]{:S(2)}, u32[]{:S(2)}) collective-permute-start(bf16[172,128]{1,0:T(8,128)(2,1)S(1)} %get-tuple-element.20.refs_0_), channel_id=1, source_target_pairs={{20,0},{8,4},{28,8},{0,12},{4,16},{24,20},{12,24},{16,28},{21,1},{... | collective-permute-start | bytes 132104 | tf_op jit(solution)/shard_map/ppermute | solution.py:40
  22.1 3.3 %collective-permute-start.12 = (bf16[172,128]{1,0:T(8,128)(2,1)S(1)}, bf16[172,128]{1,0:T(8,128)(2,1)S(1)}, u32[]{:S(2)}, u32[]{:S(2)}) collective-permute-start(bf16[172,128]{1,0:T(8,128)(2,1)S(1)} %get-tuple-element.20.refs_0_), channel_id=1, source_target_pairs={{0,4},{4,0},{8,12},{12,8},{16,20},{20,16},{24,28},{28,24},{1,5},{5... | collective-permute-start | bytes 132104 | tf_op jit(solution)/shard_map/ppermute | solution.py:36
  23.4 2.1 %collective-permute-start.14 = (bf16[172,128]{1,0:T(8,128)(2,1)S(1)}, bf16[172,128]{1,0:T(8,128)(2,1)S(1)}, u32[]{:S(2)}, u32[]{:S(2)}) collective-permute-start(bf16[172,128]{1,0:T(8,128)(2,1)S(1)} %collective-permute-done.10.refs_2_), channel_id=1, source_target_pairs={{0,4},{4,0},{8,12},{12,8},{16,20},{20,16},{24,28},{28,24},{1,5},{5... | collective-permute-start | bytes 132104 | tf_op jit(solution)/shard_map/ppermute | solution.py:36
  23.7 1.8 %collective-permute-start.15 = (bf16[172,128]{1,0:T(8,128)(2,1)S(1)}, bf16[172,128]{1,0:T(8,128)(2,1)S(1)}, u32[]{:S(2)}, u32[]{:S(2)}) collective-permute-start(bf16[172,128]{1,0:T(8,128)(2,1)S(1)} %collective-permute-done.9.refs_1_), channel_id=1, source_target_pairs={{0,4},{4,0},{8,12},{12,8},{16,20},{20,16},{24,28},{28,24},{1,5},{5... | collective-permute-start | bytes 132104 | tf_op jit(solution)/shard_map/ppermute | solution.py:36
  24.7 5.8 %collective-permute-start.11 = (bf16[128,256]{1,0:T(8,128)(2,1)S(1)}, bf16[128,256]{1,0:T(8,128)(2,1)S(1)}, u32[]{:S(2)}, u32[]{:S(2)}) collective-permute-start(bf16[128,256]{1,0:T(8,128)(2,1)S(1)} %shard_map.120), channel_id=1, source_target_pairs={{0,4},{4,0},{8,12},{12,8},{16,20},{20,16},{24,28},{28,24},{1,5},{5... | collective-permute-start | bytes 196616 | tf_op jit(solution)/shard_map/ppermute | solution.py:36
  25.8 6.4 %collective-permute-start.17 = (bf16[172,128]{1,0:T(8,128)(2,1)S(1)}, bf16[172,128]{1,0:T(8,128)(2,1)S(1)}, u32[]{:S(2)}, u32[]{:S(2)}) collective-permute-start(bf16[172,128]{1,0:T(8,128)(2,1)S(1)} %get-tuple-element.24), channel_id=1, source_target_pairs={{0,3},{1,2},{2,1},{3,0},{4,7},{5,6},{6,5},{7,4},{8,11},{9,10},{10,... | collective-permute-start | bytes 132104 | tf_op jit(solution)/shard_map/ppermute | solution.py:36
  27.8 5.7 %collective-permute-start.18 = (bf16[172,128]{1,0:T(8,128)(2,1)S(1)}, bf16[172,128]{1,0:T(8,128)(2,1)S(1)}, u32[]{:S(2)}, u32[]{:S(2)}) collective-permute-start(bf16[172,128]{1,0:T(8,128)(2,1)S(1)} %get-tuple-element.25), channel_id=1, source_target_pairs={{0,2},{1,3},{2,0},{3,1},{4,6},{5,7},{6,4},{7,5},{8,10},{9,11},{10,... | collective-permute-start | bytes 132104 | tf_op jit(solution)/shard_map/ppermute | solution.py:36
  27.8 5.7 %collective-permute-start.19 = (bf16[172,128]{1,0:T(8,128)(2,1)S(1)}, bf16[172,128]{1,0:T(8,128)(2,1)S(1)}, u32[]{:S(2)}, u32[]{:S(2)}) collective-permute-start(bf16[172,128]{1,0:T(8,128)(2,1)S(1)} %get-tuple-element.23.refs_0_), channel_id=1, source_target_pairs={{0,1},{1,0},{2,3},{3,2},{4,5},{5,4},{6,7},{7,6},{8,9},{9,8},{10,11... | collective-permute-start | bytes 132104 | tf_op jit(solution)/shard_map/ppermute | solution.py:36
  (3 other events, 24.8 us)

commit v5 on v4

--- a/solution.py
+++ b/solution.py
@@ -66,7 +66,8 @@
 
 
 def send_each(blocks, axis, size):
-    return [permuted(blocks[slot], axis, size, slot) for slot in reversed(range(1, size))]
+    slots = [size - 1, *range(1, size - 1)]
+    return [permuted(blocks[slot], axis, size, slot) for slot in slots]
 
 
 def call(kernel, out_shape, operands, specs=None, scratch=(), cost=None, out_specs=None):

time: 34.4 us -> 34.2 us (level)
  Pallas kernels: 5.27 us -> 5.88 us
  starting transfers between devices: 20.2 us -> 19.7 us
    pallas_call x13, Pallas kernels: 5.27 us -> 5.88 us  [call(): pl.pallas_call(kernel, out_shape=out_shape, in_specs=specs or [vmem] * le...]
    ppermute x4, waiting for transfers between devices: 3.49 us -> 2.89 us  [send_across(): arrived.append(lax.ppermute(blocks[slot], ('row', 'col'), pairs))]
    ppermute x9, starting transfers between devices: 7.14 us -> 6.58 us  [permuted(): lax.ppermute(block, axis, [(i, partner(i, slot)) for i in range(size)])]
  transfers between devices with their start and end apart: 20 -> 20, of which waited for: 8 -> 8; matrix products, arithmetic and copies ran while one was open for 0% -> 0% of each run, Pallas kernels for 12% -> 14%
where the time goes in v5:
time: 34.2 us; the launch traced here: 34.1 us
  starting transfers between devices  19.7 us (58%)
  waiting for transfers between devices  6.93 us (20%)
  Pallas kernels  5.88 us (17%)
  between operations  1.52 us (4%)
    ppermute x7, starting transfers between devices, fetched(): lax.ppermute(block, axis, [(partner(i, seen(slot, i)), i) for i in range(...  8.84 us
    ppermute x9, starting transfers between devices, permuted(): lax.ppermute(block, axis, [(i, partner(i, slot)) for i in range(size)])  6.58 us
    pallas_call x13, Pallas kernels, call(): pl.pallas_call(kernel, out_shape=out_shape, in_specs=specs or [vmem] * le...  5.88 us
    ppermute x4, starting transfers between devices, send_across(): arrived.append(lax.ppermute(blocks[slot], ('row', 'col'), pairs))  4.29 us
    ppermute x4, waiting for transfers between devices, send_across(): arrived.append(lax.ppermute(blocks[slot], ('row', 'col'), pairs))  2.89 us
    ppermute x9, waiting for transfers between devices, permuted(): lax.ppermute(block, axis, [(i, partner(i, slot)) for i in range(size)])  2.81 us
    ppermute x7, waiting for transfers between devices, fetched(): lax.ppermute(block, axis, [(partner(i, seen(slot, i)), i) for i in range(...  1.22 us
  transfers between devices with their start and end apart: 20, of which 8 were waited for; matrix products, arithmetic and copies ran while one was open for 0% of the time, Pallas kernels for 14%

profile of v5, /device:TPU:0, one launch (start us, length us, event | category | flops | bytes accessed | tf_op | source)
XLA Modules:
  0.0 34.1 jit_solution(7938919899652907288)
XLA Ops:
  0.7 3.4 %collective-permute-start.2 = (bf16[128,128]{1,0:T(8,128)(2,1)}, bf16[128,128]{1,0:T(8,128)(2,1)S(1)}, u32[]{:S(2)}, u32[]{:S(2)}) collective-permute-start(bf16[128,128]{1,0:T(8,128)(2,1)} %bitcast.18), channel_id=1, source_target_pairs={{28,0},{24,4},{20,8},{16,12},{12,16},{8,20},{4,24},{0,28},{29,1},{... | collective-permute-start | bytes 98312 | tf_op jit(solution)/shard_map/ppermute | solution.py:40
  4.1 0.8 %collective-permute-start.1 = (bf16[128,128]{1,0:T(8,128)(2,1)}, bf16[128,128]{1,0:T(8,128)(2,1)S(1)}, u32[]{:S(2)}, u32[]{:S(2)}) collective-permute-start(bf16[128,128]{1,0:T(8,128)(2,1)} %bitcast.19), channel_id=1, source_target_pairs={{12,0},{16,4},{4,8},{24,12},{28,16},{0,20},{20,24},{8,28},{13,1},{... | collective-permute-start | bytes 98312 | tf_op jit(solution)/shard_map/ppermute | solution.py:40
  4.9 1.0 %collective-permute-start = (bf16[128,128]{1,0:T(8,128)(2,1)}, bf16[128,128]{1,0:T(8,128)(2,1)S(1)}, u32[]{:S(2)}, u32[]{:S(2)}) collective-permute-start(bf16[128,128]{1,0:T(8,128)(2,1)} %bitcast.20), channel_id=1, source_target_pairs={{20,0},{8,4},{28,8},{0,12},{4,16},{24,20},{12,24},{16,28},{21,1},{... | collective-permute-start | bytes 98312 | tf_op jit(solution)/shard_map/ppermute | solution.py:40
  6.5 2.6 %shard_map.113.refs_4_.dense_ref = bf16[512,1024]{1,0:T(8,128)(2,1)S(1)} custom-call(s32[1,1]{1,0:T(1,128)S(6)} %copy.13.count, s32[2,128]{1,0:T(2,128)} %bitcast.28, bf16[128,128,128]{2,1,0:T(8,128)(2,1)} %bitcast.25), custom_call_target="tpu_custom_call" | custom-call | flops 2097152 | bytes 4194304 | tf_op jit(solution)/shard_map/pallas_call | solution.py:75
  9.4 0.5 %collective-permute-start.8 = (bf16[128,256]{1,0:T(8,128)(2,1)S(1)}, bf16[128,256]{1,0:T(8,128)(2,1)S(1)}, u32[]{:S(2)}, u32[]{:S(2)}) collective-permute-start(bf16[128,256]{1,0:T(8,128)(2,1)S(1)} %get-tuple-element.18), channel_id=1, source_target_pairs={{0,4},{4,0},{8,12},{12,8},{16,20},{20,16},{24,28},{28,24},{1,5},{5... | collective-permute-start | bytes 196616 | tf_op jit(solution)/shard_map/ppermute | solution.py:36
  10.9 2.9 %collective-permute-start.4 = (bf16[128,128]{1,0:T(8,128)(2,1)S(1)}, bf16[128,128]{1,0:T(8,128)(2,1)S(1)}, u32[]{:S(2)}, u32[]{:S(2)}) collective-permute-start(bf16[128,128]{1,0:T(8,128)(2,1)S(1)} %get-tuple-element.14), channel_id=1, source_target_pairs={{0,7},{1,6},{2,5},{3,4},{4,3},{5,2},{6,1},{7,0},{8,15},{9,14},{10,... | collective-permute-start | bytes 98312 | tf_op jit(solution)/shard_map/ppermute | solution.py:64
  13.8 1.0 %collective-permute-start.6 = (bf16[128,128]{1,0:T(8,128)(2,1)S(1)}, bf16[128,128]{1,0:T(8,128)(2,1)S(1)}, u32[]{:S(2)}, u32[]{:S(2)}) collective-permute-start(bf16[128,128]{1,0:T(8,128)(2,1)S(1)} %get-tuple-element.16), channel_id=1, source_target_pairs={{0,5},{1,4},{2,7},{3,6},{4,1},{5,0},{6,3},{7,2},{8,13},{9,12},{10,... | collective-permute-start | bytes 98312 | tf_op jit(solution)/shard_map/ppermute | solution.py:64
  14.9 0.3 %collective-permute-start.7 = (bf16[128,128]{1,0:T(8,128)(2,1)S(1)}, bf16[128,128]{1,0:T(8,128)(2,1)S(1)}, u32[]{:S(2)}, u32[]{:S(2)}) collective-permute-start(bf16[128,128]{1,0:T(8,128)(2,1)S(1)} %get-tuple-element.17), channel_id=1, source_target_pairs={{0,4},{1,5},{2,6},{3,7},{4,0},{5,1},{6,2},{7,3},{8,12},{9,13},{10,... | collective-permute-start | bytes 98312 | tf_op jit(solution)/shard_map/ppermute | solution.py:64
  15.2 1.0 %collective-permute-done.4.refs_0_ = bf16[128,128]{1,0:T(8,128)(2,1)S(1)} collective-permute-done((bf16[128,128]{1,0:T(8,128)(2,1)S(1)}, bf16[128,128]{1,0:T(8,128)(2,1)S(1)}, u32[]{:S(2)}, u32[]{:S(2)}) %collective-permute-start.4) | collective-permute-done | bytes 32800 | tf_op jit(solution)/shard_map/ppermute | solution.py:64
  16.2 1.9 %collective-permute-done.5.refs_1_ = bf16[128,128]{1,0:T(8,128)(2,1)S(1)} collective-permute-done((bf16[128,128]{1,0:T(8,128)(2,1)S(1)}, bf16[128,128]{1,0:T(8,128)(2,1)S(1)}, u32[]{:S(2)}, u32[]{:S(2)}) %collective-permute-start.5) | collective-permute-done | bytes 32800 | tf_op jit(solution)/shard_map/ppermute | solution.py:64
  18.5 1.3 %collective-permute-start.10 = (bf16[172,128]{1,0:T(8,128)(2,1)S(1)}, bf16[172,128]{1,0:T(8,128)(2,1)S(1)}, u32[]{:S(2)}, u32[]{:S(2)}) collective-permute-start(bf16[172,128]{1,0:T(8,128)(2,1)S(1)} %get-tuple-element.20.refs_0_), channel_id=1, source_target_pairs={{28,0},{24,4},{20,8},{16,12},{12,16},{8,20},{4,24},{0,28},{29,1},{... | collective-permute-start | bytes 132104 | tf_op jit(solution)/shard_map/ppermute | solution.py:40
  19.8 0.8 %collective-permute-start.9 = (bf16[172,128]{1,0:T(8,128)(2,1)S(1)}, bf16[172,128]{1,0:T(8,128)(2,1)S(1)}, u32[]{:S(2)}, u32[]{:S(2)}) collective-permute-start(bf16[172,128]{1,0:T(8,128)(2,1)S(1)} %get-tuple-element.20.refs_0_), channel_id=1, source_target_pairs={{12,0},{16,4},{4,8},{24,12},{28,16},{0,20},{20,24},{8,28},{13,1},{... | collective-permute-start | bytes 132104 | tf_op jit(solution)/shard_map/ppermute | solution.py:40
  20.6 1.1 %collective-permute-start.16 = (bf16[172,128]{1,0:T(8,128)(2,1)S(1)}, bf16[172,128]{1,0:T(8,128)(2,1)S(1)}, u32[]{:S(2)}, u32[]{:S(2)}) collective-permute-start(bf16[172,128]{1,0:T(8,128)(2,1)S(1)} %get-tuple-element.20.refs_0_), channel_id=1, source_target_pairs={{8,0},{20,4},{0,8},{28,12},{24,16},{4,20},{16,24},{12,28},{9,1},{2... | collective-permute-start | bytes 132104 | tf_op jit(solution)/shard_map/ppermute | solution.py:40
  21.7 0.4 %collective-permute-start.13 = (bf16[172,128]{1,0:T(8,128)(2,1)S(1)}, bf16[172,128]{1,0:T(8,128)(2,1)S(1)}, u32[]{:S(2)}, u32[]{:S(2)}) collective-permute-start(bf16[172,128]{1,0:T(8,128)(2,1)S(1)} %get-tuple-element.20.refs_0_), channel_id=1, source_target_pairs={{20,0},{8,4},{28,8},{0,12},{4,16},{24,20},{12,24},{16,28},{21,1},{... | collective-permute-start | bytes 132104 | tf_op jit(solution)/shard_map/ppermute | solution.py:40
  22.1 0.9 %collective-permute-start.12 = (bf16[172,128]{1,0:T(8,128)(2,1)S(1)}, bf16[172,128]{1,0:T(8,128)(2,1)S(1)}, u32[]{:S(2)}, u32[]{:S(2)}) collective-permute-start(bf16[172,128]{1,0:T(8,128)(2,1)S(1)} %get-tuple-element.20.refs_0_), channel_id=1, source_target_pairs={{0,4},{4,0},{8,12},{12,8},{16,20},{20,16},{24,28},{28,24},{1,5},{5... | collective-permute-start | bytes 132104 | tf_op jit(solution)/shard_map/ppermute | solution.py:36
  23.1 0.5 %collective-permute-start.14 = (bf16[172,128]{1,0:T(8,128)(2,1)S(1)}, bf16[172,128]{1,0:T(8,128)(2,1)S(1)}, u32[]{:S(2)}, u32[]{:S(2)}) collective-permute-start(bf16[172,128]{1,0:T(8,128)(2,1)S(1)} %collective-permute-done.10.refs_2_), channel_id=1, source_target_pairs={{0,4},{4,0},{8,12},{12,8},{16,20},{20,16},{24,28},{28,24},{1,5},{5... | collective-permute-start | bytes 132104 | tf_op jit(solution)/shard_map/ppermute | solution.py:36
  24.1 0.6 %collective-permute-done.16.refs_2_ = bf16[172,128]{1,0:T(8,128)(2,1)S(1)} collective-permute-done((bf16[172,128]{1,0:T(8,128)(2,1)S(1)}, bf16[172,128]{1,0:T(8,128)(2,1)S(1)}, u32[]{:S(2)}, u32[]{:S(2)}) %collective-permute-start.16) | collective-permute-done | bytes 44064 | tf_op jit(solution)/shard_map/ppermute | solution.py:40
  24.7 0.5 %collective-permute-done.13.near_ref = bf16[172,128]{1,0:T(8,128)(2,1)S(1)} collective-permute-done((bf16[172,128]{1,0:T(8,128)(2,1)S(1)}, bf16[172,128]{1,0:T(8,128)(2,1)S(1)}, u32[]{:S(2)}, u32[]{:S(2)}) %collective-permute-start.13) | collective-permute-done | bytes 44064 | tf_op jit(solution)/shard_map/ppermute | solution.py:40
  25.6 2.1 %collective-permute-start.17 = (bf16[172,128]{1,0:T(8,128)(2,1)S(1)}, bf16[172,128]{1,0:T(8,128)(2,1)S(1)}, u32[]{:S(2)}, u32[]{:S(2)}) collective-permute-start(bf16[172,128]{1,0:T(8,128)(2,1)S(1)} %get-tuple-element.24), channel_id=1, source_target_pairs={{0,3},{1,2},{2,1},{3,0},{4,7},{5,6},{6,5},{7,4},{8,11},{9,10},{10,... | collective-permute-start | bytes 132104 | tf_op jit(solution)/shard_map/ppermute | solution.py:36
  27.8 2.2 %collective-permute-start.18 = (bf16[172,128]{1,0:T(8,128)(2,1)S(1)}, bf16[172,128]{1,0:T(8,128)(2,1)S(1)}, u32[]{:S(2)}, u32[]{:S(2)}) collective-permute-start(bf16[172,128]{1,0:T(8,128)(2,1)S(1)} %get-tuple-element.23.refs_0_), channel_id=1, source_target_pairs={{0,1},{1,0},{2,3},{3,2},{4,5},{5,4},{6,7},{7,6},{8,9},{9,8},{10,11... | collective-permute-start | bytes 132104 | tf_op jit(solution)/shard_map/ppermute | solution.py:36
  30.3 0.6 %shard_map.121 = bf16[128,256]{1,0:T(8,128)(2,1)} custom-call(bf16[128,256]{1,0:T(8,128)(2,1)S(1)} %collective-permute-done.11.value), custom_call_target="tpu_custom_call" | custom-call | tf_op jit(solution)/shard_map/pallas_call | solution.py:75
  30.9 1.1 %collective-permute-done.17.refs_3_ = bf16[172,128]{1,0:T(8,128)(2,1)S(1)} collective-permute-done((bf16[172,128]{1,0:T(8,128)(2,1)S(1)}, bf16[172,128]{1,0:T(8,128)(2,1)S(1)}, u32[]{:S(2)}, u32[]{:S(2)}) %collective-permute-start.17) | collective-permute-done | bytes 44064 | tf_op jit(solution)/shard_map/ppermute | solution.py:36
  32.0 1.3 %collective-permute-done.19.refs_1_ = bf16[172,128]{1,0:T(8,128)(2,1)S(1)} collective-permute-done((bf16[172,128]{1,0:T(8,128)(2,1)S(1)}, bf16[172,128]{1,0:T(8,128)(2,1)S(1)}, u32[]{:S(2)}, u32[]{:S(2)}) %collective-permute-start.19) | collective-permute-done | bytes 44064 | tf_op jit(solution)/shard_map/ppermute | solution.py:36
  33.4 0.7 %shard_map.125 = f32[172,1,128]{2,1,0:T(1,128)} custom-call(f32[172,128]{1,0:T(8,128)S(1)} %shard_map.124.begun, bf16[172,128]{1,0:T(8,128)(2,1)S(1)} %collective-permute-done.18.refs_0_, bf16[172,128]{1,0:T(8,128)(2,1)S(1)} %collective-permute-done.19.refs_1_), custom_call_target="tpu_custom_call" | custom-call | tf_op jit(solution)/shard_map/pallas_call | solution.py:75
  (43 shorter events, 2.8 us)
Async XLA Ops:
  0.6 8.6 %copy-start.4 = (f32[172]{0:T(256)S(1)}, f32[172]{0:T(256)}, u32[]{:S(2)}) copy-start(f32[172]{0:T(256)} %param.19) | copy-start | bytes 2068
  0.7 8.5 %collective-permute-start.2 = (bf16[128,128]{1,0:T(8,128)(2,1)}, bf16[128,128]{1,0:T(8,128)(2,1)S(1)}, u32[]{:S(2)}, u32[]{:S(2)}) collective-permute-start(bf16[128,128]{1,0:T(8,128)(2,1)} %bitcast.18), channel_id=1, source_target_pairs={{28,0},{24,4},{20,8},{16,12},{12,16},{8,20},{4,24},{0,28},{29,1},{... | collective-permute-start | bytes 98312 | tf_op jit(solution)/shard_map/ppermute | solution.py:40
  4.1 5.1 %collective-permute-start.1 = (bf16[128,128]{1,0:T(8,128)(2,1)}, bf16[128,128]{1,0:T(8,128)(2,1)S(1)}, u32[]{:S(2)}, u32[]{:S(2)}) collective-permute-start(bf16[128,128]{1,0:T(8,128)(2,1)} %bitcast.19), channel_id=1, source_target_pairs={{12,0},{16,4},{4,8},{24,12},{28,16},{0,20},{20,24},{8,28},{13,1},{... | collective-permute-start | bytes 98312 | tf_op jit(solution)/shard_map/ppermute | solution.py:40
  4.9 4.3 %collective-permute-start = (bf16[128,128]{1,0:T(8,128)(2,1)}, bf16[128,128]{1,0:T(8,128)(2,1)S(1)}, u32[]{:S(2)}, u32[]{:S(2)}) collective-permute-start(bf16[128,128]{1,0:T(8,128)(2,1)} %bitcast.20), channel_id=1, source_target_pairs={{20,0},{8,4},{28,8},{0,12},{4,16},{24,20},{12,24},{16,28},{21,1},{... | collective-permute-start | bytes 98312 | tf_op jit(solution)/shard_map/ppermute | solution.py:40
  6.5 11.6 %copy-start = (bf16[256,172]{0,1:T(8,128)(2,1)S(1)}, bf16[256,172]{0,1:T(8,128)(2,1)}, u32[]{:S(2)}) copy-start(bf16[256,172]{0,1:T(8,128)(2,1)} %param.18) | copy-start | bytes 264196
  6.5 11.6 %copy-start.2 = (bf16[128,256]{1,0:T(8,128)(2,1)S(1)}, bf16[128,256]{1,0:T(8,128)(2,1)}, u32[]{:S(2)}) copy-start(bf16[128,256]{1,0:T(8,128)(2,1)} %refs_5_.1) | copy-start | bytes 196612
  6.5 11.6 %copy-start.5 = (f32[256]{0:T(256)S(1)}, f32[256]{0:T(256)}, u32[]{:S(2)}) copy-start(f32[256]{0:T(256)} %param.17) | copy-start | bytes 3076
  9.2 1.4 %collective-permute-start.3 = (bf16[512,128]{1,0:T(8,128)(2,1)S(1)}, bf16[512,128]{1,0:T(8,128)(2,1)S(1)}, u32[]{:S(2)}, u32[]{:S(2)}) collective-permute-start(bf16[512,128]{1,0:T(8,128)(2,1)S(1)} %shard_map.114.mine_ref.refs_0_), channel_id=1, source_target_pairs={{0,4},{4,0},{8,12},{12,8},{16,20},{20,16},{24,28},{28,24},{1,5},{5... | collective-permute-start | bytes 393224 | tf_op jit(solution)/shard_map/ppermute | solution.py:36
  9.4 5.8 %collective-permute-start.8 = (bf16[128,256]{1,0:T(8,128)(2,1)S(1)}, bf16[128,256]{1,0:T(8,128)(2,1)S(1)}, u32[]{:S(2)}, u32[]{:S(2)}) collective-permute-start(bf16[128,256]{1,0:T(8,128)(2,1)S(1)} %get-tuple-element.18), channel_id=1, source_target_pairs={{0,4},{4,0},{8,12},{12,8},{16,20},{20,16},{24,28},{28,24},{1,5},{5... | collective-permute-start | bytes 196616 | tf_op jit(solution)/shard_map/ppermute | solution.py:36
  10.9 5.3 %collective-permute-start.4 = (bf16[128,128]{1,0:T(8,128)(2,1)S(1)}, bf16[128,128]{1,0:T(8,128)(2,1)S(1)}, u32[]{:S(2)}, u32[]{:S(2)}) collective-permute-start(bf16[128,128]{1,0:T(8,128)(2,1)S(1)} %get-tuple-element.14), channel_id=1, source_target_pairs={{0,7},{1,6},{2,5},{3,4},{4,3},{5,2},{6,1},{7,0},{8,15},{9,14},{10,... | collective-permute-start | bytes 98312 | tf_op jit(solution)/shard_map/ppermute | solution.py:64
  13.8 4.3 %collective-permute-start.5 = (bf16[128,128]{1,0:T(8,128)(2,1)S(1)}, bf16[128,128]{1,0:T(8,128)(2,1)S(1)}, u32[]{:S(2)}, u32[]{:S(2)}) collective-permute-start(bf16[128,128]{1,0:T(8,128)(2,1)S(1)} %get-tuple-element.15), channel_id=1, source_target_pairs={{0,6},{1,7},{2,4},{3,5},{4,2},{5,3},{6,0},{7,1},{8,14},{9,15},{10,... | collective-permute-start | bytes 98312 | tf_op jit(solution)/shard_map/ppermute | solution.py:64
  13.8 4.3 %collective-permute-start.6 = (bf16[128,128]{1,0:T(8,128)(2,1)S(1)}, bf16[128,128]{1,0:T(8,128)(2,1)S(1)}, u32[]{:S(2)}, u32[]{:S(2)}) collective-permute-start(bf16[128,128]{1,0:T(8,128)(2,1)S(1)} %get-tuple-element.16), channel_id=1, source_target_pairs={{0,5},{1,4},{2,7},{3,6},{4,1},{5,0},{6,3},{7,2},{8,13},{9,12},{10,... | collective-permute-start | bytes 98312 | tf_op jit(solution)/shard_map/ppermute | solution.py:64
  14.9 3.2 %collective-permute-start.7 = (bf16[128,128]{1,0:T(8,128)(2,1)S(1)}, bf16[128,128]{1,0:T(8,128)(2,1)S(1)}, u32[]{:S(2)}, u32[]{:S(2)}) collective-permute-start(bf16[128,128]{1,0:T(8,128)(2,1)S(1)} %get-tuple-element.17), channel_id=1, source_target_pairs={{0,4},{1,5},{2,6},{3,7},{4,0},{5,1},{6,2},{7,3},{8,12},{9,13},{10,... | collective-permute-start | bytes 98312 | tf_op jit(solution)/shard_map/ppermute | solution.py:64
  18.5 4.6 %collective-permute-start.10 = (bf16[172,128]{1,0:T(8,128)(2,1)S(1)}, bf16[172,128]{1,0:T(8,128)(2,1)S(1)}, u32[]{:S(2)}, u32[]{:S(2)}) collective-permute-start(bf16[172,128]{1,0:T(8,128)(2,1)S(1)} %get-tuple-element.20.refs_0_), channel_id=1, source_target_pairs={{28,0},{24,4},{20,8},{16,12},{12,16},{8,20},{4,24},{0,28},{29,1},{... | collective-permute-start | bytes 132104 | tf_op jit(solution)/shard_map/ppermute | solution.py:40
  19.8 3.9 %collective-permute-start.9 = (bf16[172,128]{1,0:T(8,128)(2,1)S(1)}, bf16[172,128]{1,0:T(8,128)(2,1)S(1)}, u32[]{:S(2)}, u32[]{:S(2)}) collective-permute-start(bf16[172,128]{1,0:T(8,128)(2,1)S(1)} %get-tuple-element.20.refs_0_), channel_id=1, source_target_pairs={{12,0},{16,4},{4,8},{24,12},{28,16},{0,20},{20,24},{8,28},{13,1},{... | collective-permute-start | bytes 132104 | tf_op jit(solution)/shard_map/ppermute | solution.py:40
  20.6 4.0 %collective-permute-start.16 = (bf16[172,128]{1,0:T(8,128)(2,1)S(1)}, bf16[172,128]{1,0:T(8,128)(2,1)S(1)}, u32[]{:S(2)}, u32[]{:S(2)}) collective-permute-start(bf16[172,128]{1,0:T(8,128)(2,1)S(1)} %get-tuple-element.20.refs_0_), channel_id=1, source_target_pairs={{8,0},{20,4},{0,8},{28,12},{24,16},{4,20},{16,24},{12,28},{9,1},{2... | collective-permute-start | bytes 132104 | tf_op jit(solution)/shard_map/ppermute | solution.py:40
  21.7 3.5 %collective-permute-start.13 = (bf16[172,128]{1,0:T(8,128)(2,1)S(1)}, bf16[172,128]{1,0:T(8,128)(2,1)S(1)}, u32[]{:S(2)}, u32[]{:S(2)}) collective-permute-start(bf16[172,128]{1,0:T(8,128)(2,1)S(1)} %get-tuple-element.20.refs_0_), channel_id=1, source_target_pairs={{20,0},{8,4},{28,8},{0,12},{4,16},{24,20},{12,24},{16,28},{21,1},{... | collective-permute-start | bytes 132104 | tf_op jit(solution)/shard_map/ppermute | solution.py:40
  22.1 3.1 %collective-permute-start.12 = (bf16[172,128]{1,0:T(8,128)(2,1)S(1)}, bf16[172,128]{1,0:T(8,128)(2,1)S(1)}, u32[]{:S(2)}, u32[]{:S(2)}) collective-permute-start(bf16[172,128]{1,0:T(8,128)(2,1)S(1)} %get-tuple-element.20.refs_0_), channel_id=1, source_target_pairs={{0,4},{4,0},{8,12},{12,8},{16,20},{20,16},{24,28},{28,24},{1,5},{5... | collective-permute-start | bytes 132104 | tf_op jit(solution)/shard_map/ppermute | solution.py:36
  23.1 2.1 %collective-permute-start.14 = (bf16[172,128]{1,0:T(8,128)(2,1)S(1)}, bf16[172,128]{1,0:T(8,128)(2,1)S(1)}, u32[]{:S(2)}, u32[]{:S(2)}) collective-permute-start(bf16[172,128]{1,0:T(8,128)(2,1)S(1)} %collective-permute-done.10.refs_2_), channel_id=1, source_target_pairs={{0,4},{4,0},{8,12},{12,8},{16,20},{20,16},{24,28},{28,24},{1,5},{5... | collective-permute-start | bytes 132104 | tf_op jit(solution)/shard_map/ppermute | solution.py:36
  23.7 1.5 %collective-permute-start.15 = (bf16[172,128]{1,0:T(8,128)(2,1)S(1)}, bf16[172,128]{1,0:T(8,128)(2,1)S(1)}, u32[]{:S(2)}, u32[]{:S(2)}) collective-permute-start(bf16[172,128]{1,0:T(8,128)(2,1)S(1)} %collective-permute-done.9.refs_1_), channel_id=1, source_target_pairs={{0,4},{4,0},{8,12},{12,8},{16,20},{20,16},{24,28},{28,24},{1,5},{5... | collective-permute-start | bytes 132104 | tf_op jit(solution)/shard_map/ppermute | solution.py:36
  24.7 5.6 %collective-permute-start.11 = (bf16[128,256]{1,0:T(8,128)(2,1)S(1)}, bf16[128,256]{1,0:T(8,128)(2,1)S(1)}, u32[]{:S(2)}, u32[]{:S(2)}) collective-permute-start(bf16[128,256]{1,0:T(8,128)(2,1)S(1)} %shard_map.120), channel_id=1, source_target_pairs={{0,4},{4,0},{8,12},{12,8},{16,20},{20,16},{24,28},{28,24},{1,5},{5... | collective-permute-start | bytes 196616 | tf_op jit(solution)/shard_map/ppermute | solution.py:36
  25.6 6.4 %collective-permute-start.17 = (bf16[172,128]{1,0:T(8,128)(2,1)S(1)}, bf16[172,128]{1,0:T(8,128)(2,1)S(1)}, u32[]{:S(2)}, u32[]{:S(2)}) collective-permute-start(bf16[172,128]{1,0:T(8,128)(2,1)S(1)} %get-tuple-element.24), channel_id=1, source_target_pairs={{0,3},{1,2},{2,1},{3,0},{4,7},{5,6},{6,5},{7,4},{8,11},{9,10},{10,... | collective-permute-start | bytes 132104 | tf_op jit(solution)/shard_map/ppermute | solution.py:36
  27.7 5.7 %collective-permute-start.19 = (bf16[172,128]{1,0:T(8,128)(2,1)S(1)}, bf16[172,128]{1,0:T(8,128)(2,1)S(1)}, u32[]{:S(2)}, u32[]{:S(2)}) collective-permute-start(bf16[172,128]{1,0:T(8,128)(2,1)S(1)} %get-tuple-element.25), channel_id=1, source_target_pairs={{0,2},{1,3},{2,0},{3,1},{4,6},{5,7},{6,4},{7,5},{8,10},{9,11},{10,... | collective-permute-start | bytes 132104 | tf_op jit(solution)/shard_map/ppermute | solution.py:36
  27.8 5.5 %collective-permute-start.18 = (bf16[172,128]{1,0:T(8,128)(2,1)S(1)}, bf16[172,128]{1,0:T(8,128)(2,1)S(1)}, u32[]{:S(2)}, u32[]{:S(2)}) collective-permute-start(bf16[172,128]{1,0:T(8,128)(2,1)S(1)} %get-tuple-element.23.refs_0_), channel_id=1, source_target_pairs={{0,1},{1,0},{2,3},{3,2},{4,5},{5,4},{6,7},{7,6},{8,9},{9,8},{10,11... | collective-permute-start | bytes 132104 | tf_op jit(solution)/shard_map/ppermute | solution.py:36
  (3 other events, 25.8 us)

commit v6 on v0

--- a/solution.py
+++ b/solution.py
@@ -276,7 +276,7 @@
 
     if dense_form:
         anywhere = pl.BlockSpec(memory_space=pl.ANY)
-        chunks = 8
+        chunks = 16
         dense = call(
             functools.partial(build_kernel, n_row, n_col, chunks),
             shape((n_col * block, n_row * block), BF16),

time: 34.6 us -> 34.6 us (level)
  waiting for transfers between devices: 7.77 us -> 8.4 us
    ppermute x4, waiting for transfers between devices: 2.8 us -> 3.48 us  [send_across(): arrived.append(lax.ppermute(blocks[slot], ('row', 'col'), pairs))]
    ppermute x4, starting transfers between devices: 4.3 us -> 4.87 us  [send_across(): arrived.append(lax.ppermute(blocks[slot], ('row', 'col'), pairs))]
    ppermute x7, starting transfers between devices: 8.9 us -> 8.42 us  [fetched(): lax.ppermute(block, axis, [(partner(i, seen(slot, i)), i) for i in range(...]
    ppermute x9, starting transfers between devices: 7.21 us -> 6.77 us  [permuted(): lax.ppermute(block, axis, [(i, partner(i, slot)) for i in range(size)])]
  transfers between devices with their start and end apart: 20 -> 20, of which waited for: 9 -> 8; matrix products, arithmetic and copies ran while one was open for 0% -> 0% of each run, Pallas kernels for 10% -> 10%
where the time goes in v6:
time: 34.6 us
  starting transfers between devices  20.1 us (58%)
  waiting for transfers between devices  8.4 us (24%)
  Pallas kernels  4.65 us (13%)
  between operations  1.47 us (4%)
    ppermute x7, starting transfers between devices, fetched(): lax.ppermute(block, axis, [(partner(i, seen(slot, i)), i) for i in range(...  8.42 us
    ppermute x9, starting transfers between devices, permuted(): lax.ppermute(block, axis, [(i, partner(i, slot)) for i in range(size)])  6.77 us
    ppermute x4, starting transfers between devices, send_across(): arrived.append(lax.ppermute(blocks[slot], ('row', 'col'), pairs))  4.87 us
    pallas_call x11, Pallas kernels, call(): pl.pallas_call(kernel, out_shape=out_shape, in_specs=specs or [vmem] * le...  4.65 us
    ppermute x4, waiting for transfers between devices, send_across(): arrived.append(lax.ppermute(blocks[slot], ('row', 'col'), pairs))  3.48 us
    ppermute x9, waiting for transfers between devices, permuted(): lax.ppermute(block, axis, [(i, partner(i, slot)) for i in range(size)])  2.86 us
    ppermute x7, waiting for transfers between devices, fetched(): lax.ppermute(block, axis, [(partner(i, seen(slot, i)), i) for i in range(...  2.05 us
  transfers between devices with their start and end apart: 20, of which 8 were waited for; matrix products, arithmetic and copies ran while one was open for 0% of the time, Pallas kernels for 10%

profile of v6, /device:TPU:0, one launch (start us, length us, event | category | flops | bytes accessed | tf_op | source)
XLA Modules:
  0.0 34.6 jit_solution(16192982283966545190)
XLA Ops:
  0.7 3.4 %collective-permute-start.2 = (bf16[128,128]{1,0:T(8,128)(2,1)}, bf16[128,128]{1,0:T(8,128)(2,1)S(1)}, u32[]{:S(2)}, u32[]{:S(2)}) collective-permute-start(bf16[128,128]{1,0:T(8,128)(2,1)} %bitcast.18), channel_id=1, source_target_pairs={{28,0},{24,4},{20,8},{16,12},{12,16},{8,20},{4,24},{0,28},{29,1},{... | collective-permute-start | bytes 98312 | tf_op jit(solution)/shard_map/ppermute | solution.py:40
  4.1 0.8 %collective-permute-start.1 = (bf16[128,128]{1,0:T(8,128)(2,1)}, bf16[128,128]{1,0:T(8,128)(2,1)S(1)}, u32[]{:S(2)}, u32[]{:S(2)}) collective-permute-start(bf16[128,128]{1,0:T(8,128)(2,1)} %bitcast.19), channel_id=1, source_target_pairs={{12,0},{16,4},{4,8},{24,12},{28,16},{0,20},{20,24},{8,28},{13,1},{... | collective-permute-start | bytes 98312 | tf_op jit(solution)/shard_map/ppermute | solution.py:40
  4.9 1.0 %collective-permute-start = (bf16[128,128]{1,0:T(8,128)(2,1)}, bf16[128,128]{1,0:T(8,128)(2,1)S(1)}, u32[]{:S(2)}, u32[]{:S(2)}) collective-permute-start(bf16[128,128]{1,0:T(8,128)(2,1)} %bitcast.20), channel_id=1, source_target_pairs={{20,0},{8,4},{28,8},{0,12},{4,16},{24,20},{12,24},{16,28},{21,1},{... | collective-permute-start | bytes 98312 | tf_op jit(solution)/shard_map/ppermute | solution.py:40
  6.5 1.6 %shard_map.113.refs_4_.dense_ref = bf16[512,1024]{1,0:T(8,128)(2,1)S(1)} custom-call(s32[1,1]{1,0:T(1,128)S(6)} %copy.13.count, s32[2,128]{1,0:T(2,128)} %bitcast.28, bf16[128,128,128]{2,1,0:T(8,128)(2,1)} %bitcast.25), custom_call_target="tpu_custom_call" | custom-call | flops 2097152 | bytes 4194304 | tf_op jit(solution)/shard_map/pallas_call | solution.py:74
  8.1 0.6 %collective-permute-done.refs_1_ = bf16[128,128]{1,0:T(8,128)(2,1)S(1)} collective-permute-done((bf16[128,128]{1,0:T(8,128)(2,1)}, bf16[128,128]{1,0:T(8,128)(2,1)S(1)}, u32[]{:S(2)}, u32[]{:S(2)}) %collective-permute-start) | collective-permute-done | bytes 32800 | tf_op jit(solution)/shard_map/ppermute | solution.py:40
  8.7 0.4 %collective-permute-start.3 = (bf16[512,128]{1,0:T(8,128)(2,1)S(1)}, bf16[512,128]{1,0:T(8,128)(2,1)S(1)}, u32[]{:S(2)}, u32[]{:S(2)}) collective-permute-start(bf16[512,128]{1,0:T(8,128)(2,1)S(1)} %shard_map.114.mine_ref.refs_0_), channel_id=1, source_target_pairs={{0,4},{4,0},{8,12},{12,8},{16,20},{20,16},{24,28},{28,24},{1,5},{5... | collective-permute-start | bytes 393224 | tf_op jit(solution)/shard_map/ppermute | solution.py:36
  10.4 4.1 %collective-permute-start.4 = (bf16[128,128]{1,0:T(8,128)(2,1)S(1)}, bf16[128,128]{1,0:T(8,128)(2,1)S(1)}, u32[]{:S(2)}, u32[]{:S(2)}) collective-permute-start(bf16[128,128]{1,0:T(8,128)(2,1)S(1)} %get-tuple-element.14), channel_id=1, source_target_pairs={{0,7},{1,6},{2,5},{3,4},{4,3},{5,2},{6,1},{7,0},{8,15},{9,14},{10,... | collective-permute-start | bytes 98312 | tf_op jit(solution)/shard_map/ppermute | solution.py:64
  14.5 0.4 %collective-permute-start.6 = (bf16[128,128]{1,0:T(8,128)(2,1)S(1)}, bf16[128,128]{1,0:T(8,128)(2,1)S(1)}, u32[]{:S(2)}, u32[]{:S(2)}) collective-permute-start(bf16[128,128]{1,0:T(8,128)(2,1)S(1)} %get-tuple-element.16), channel_id=1, source_target_pairs={{0,5},{1,4},{2,7},{3,6},{4,1},{5,0},{6,3},{7,2},{8,13},{9,12},{10,... | collective-permute-start | bytes 98312 | tf_op jit(solution)/shard_map/ppermute | solution.py:64
  15.3 0.9 %collective-permute-done.4.refs_0_ = bf16[128,128]{1,0:T(8,128)(2,1)S(1)} collective-permute-done((bf16[128,128]{1,0:T(8,128)(2,1)S(1)}, bf16[128,128]{1,0:T(8,128)(2,1)S(1)}, u32[]{:S(2)}, u32[]{:S(2)}) %collective-permute-start.4) | collective-permute-done | bytes 32800 | tf_op jit(solution)/shard_map/ppermute | solution.py:64
  16.2 2.5 %collective-permute-done.5.refs_1_ = bf16[128,128]{1,0:T(8,128)(2,1)S(1)} collective-permute-done((bf16[128,128]{1,0:T(8,128)(2,1)S(1)}, bf16[128,128]{1,0:T(8,128)(2,1)S(1)}, u32[]{:S(2)}, u32[]{:S(2)}) %collective-permute-start.5) | collective-permute-done | bytes 32800 | tf_op jit(solution)/shard_map/ppermute | solution.py:64
  19.1 0.7 %collective-permute-start.10 = (bf16[172,128]{1,0:T(8,128)(2,1)S(1)}, bf16[172,128]{1,0:T(8,128)(2,1)S(1)}, u32[]{:S(2)}, u32[]{:S(2)}) collective-permute-start(bf16[172,128]{1,0:T(8,128)(2,1)S(1)} %get-tuple-element.20.refs_0_), channel_id=1, source_target_pairs={{28,0},{24,4},{20,8},{16,12},{12,16},{8,20},{4,24},{0,28},{29,1},{... | collective-permute-start | bytes 132104 | tf_op jit(solution)/shard_map/ppermute | solution.py:40
  19.8 0.8 %collective-permute-start.9 = (bf16[172,128]{1,0:T(8,128)(2,1)S(1)}, bf16[172,128]{1,0:T(8,128)(2,1)S(1)}, u32[]{:S(2)}, u32[]{:S(2)}) collective-permute-start(bf16[172,128]{1,0:T(8,128)(2,1)S(1)} %get-tuple-element.20.refs_0_), channel_id=1, source_target_pairs={{12,0},{16,4},{4,8},{24,12},{28,16},{0,20},{20,24},{8,28},{13,1},{... | collective-permute-start | bytes 132104 | tf_op jit(solution)/shard_map/ppermute | solution.py:40
  20.6 1.8 %collective-permute-start.16 = (bf16[172,128]{1,0:T(8,128)(2,1)S(1)}, bf16[172,128]{1,0:T(8,128)(2,1)S(1)}, u32[]{:S(2)}, u32[]{:S(2)}) collective-permute-start(bf16[172,128]{1,0:T(8,128)(2,1)S(1)} %get-tuple-element.20.refs_0_), channel_id=1, source_target_pairs={{8,0},{20,4},{0,8},{28,12},{24,16},{4,20},{16,24},{12,28},{9,1},{2... | collective-permute-start | bytes 132104 | tf_op jit(solution)/shard_map/ppermute | solution.py:40
  22.4 0.7 %collective-permute-start.12 = (bf16[172,128]{1,0:T(8,128)(2,1)S(1)}, bf16[172,128]{1,0:T(8,128)(2,1)S(1)}, u32[]{:S(2)}, u32[]{:S(2)}) collective-permute-start(bf16[172,128]{1,0:T(8,128)(2,1)S(1)} %get-tuple-element.20.refs_0_), channel_id=1, source_target_pairs={{0,4},{4,0},{8,12},{12,8},{16,20},{20,16},{24,28},{28,24},{1,5},{5... | collective-permute-start | bytes 132104 | tf_op jit(solution)/shard_map/ppermute | solution.py:36
  23.1 0.8 %collective-permute-done.10.refs_2_ = bf16[172,128]{1,0:T(8,128)(2,1)S(1)} collective-permute-done((bf16[172,128]{1,0:T(8,128)(2,1)S(1)}, bf16[172,128]{1,0:T(8,128)(2,1)S(1)}, u32[]{:S(2)}, u32[]{:S(2)}) %collective-permute-start.10) | collective-permute-done | bytes 44064 | tf_op jit(solution)/shard_map/ppermute | solution.py:40
  24.1 0.7 %collective-permute-start.15 = (bf16[172,128]{1,0:T(8,128)(2,1)S(1)}, bf16[172,128]{1,0:T(8,128)(2,1)S(1)}, u32[]{:S(2)}, u32[]{:S(2)}) collective-permute-start(bf16[172,128]{1,0:T(8,128)(2,1)S(1)} %collective-permute-done.9.refs_1_), channel_id=1, source_target_pairs={{0,4},{4,0},{8,12},{12,8},{16,20},{20,16},{24,28},{28,24},{1,5},{5... | collective-permute-start | bytes 132104 | tf_op jit(solution)/shard_map/ppermute | solution.py:36
  25.2 0.7 %collective-permute-done.13.near_ref = bf16[172,128]{1,0:T(8,128)(2,1)S(1)} collective-permute-done((bf16[172,128]{1,0:T(8,128)(2,1)S(1)}, bf16[172,128]{1,0:T(8,128)(2,1)S(1)}, u32[]{:S(2)}, u32[]{:S(2)}) %collective-permute-start.13) | collective-permute-done | bytes 44064 | tf_op jit(solution)/shard_map/ppermute | solution.py:40
  25.9 0.4 %shard_map.122 = (bf16[172,128]{1,0:T(8,128)(2,1)S(1)}, bf16[172,128]{1,0:T(8,128)(2,1)S(1)}, bf16[172,128]{1,0:T(8,128)(2,1)S(1)}, bf16[172,128]{1,0:T(8,128)(2,1)S(1)}) custom-call(bf16[512,1024]{1,0:T(8,128)(2,1)S(1)} %shard_map.113.refs_4_.dense_ref, f32[172,512]{1,0:T(8,128)S(1)} %shard_map.119.after.first_ref, ...), custom_call_target="tpu_custom_call" | custom-call | tf_op jit(solution)/shard_map/pallas_call | solution.py:74
  26.3 2.1 %collective-permute-start.17 = (bf16[172,128]{1,0:T(8,128)(2,1)S(1)}, bf16[172,128]{1,0:T(8,128)(2,1)S(1)}, u32[]{:S(2)}, u32[]{:S(2)}) collective-permute-start(bf16[172,128]{1,0:T(8,128)(2,1)S(1)} %get-tuple-element.22), channel_id=1, source_target_pairs={{0,3},{1,2},{2,1},{3,0},{4,7},{5,6},{6,5},{7,4},{8,11},{9,10},{10,... | collective-permute-start | bytes 132104 | tf_op jit(solution)/shard_map/ppermute | solution.py:36
  28.4 2.4 %collective-permute-start.19 = (bf16[172,128]{1,0:T(8,128)(2,1)S(1)}, bf16[172,128]{1,0:T(8,128)(2,1)S(1)}, u32[]{:S(2)}, u32[]{:S(2)}) collective-permute-start(bf16[172,128]{1,0:T(8,128)(2,1)S(1)} %get-tuple-element.24), channel_id=1, source_target_pairs={{0,1},{1,0},{2,3},{3,2},{4,5},{5,4},{6,7},{7,6},{8,9},{9,8},{10,11... | collective-permute-start | bytes 132104 | tf_op jit(solution)/shard_map/ppermute | solution.py:36
  30.8 0.6 %shard_map.121 = bf16[128,256]{1,0:T(8,128)(2,1)} custom-call(bf16[128,256]{1,0:T(8,128)(2,1)S(1)} %collective-permute-done.11.value), custom_call_target="tpu_custom_call" | custom-call | tf_op jit(solution)/shard_map/pallas_call | solution.py:74
  31.4 1.1 %collective-permute-done.17.refs_1_ = bf16[172,128]{1,0:T(8,128)(2,1)S(1)} collective-permute-done((bf16[172,128]{1,0:T(8,128)(2,1)S(1)}, bf16[172,128]{1,0:T(8,128)(2,1)S(1)}, u32[]{:S(2)}, u32[]{:S(2)}) %collective-permute-start.17) | collective-permute-done | bytes 44064 | tf_op jit(solution)/shard_map/ppermute | solution.py:36
  32.5 1.4 %collective-permute-done.18.refs_2_ = bf16[172,128]{1,0:T(8,128)(2,1)S(1)} collective-permute-done((bf16[172,128]{1,0:T(8,128)(2,1)S(1)}, bf16[172,128]{1,0:T(8,128)(2,1)S(1)}, u32[]{:S(2)}, u32[]{:S(2)}) %collective-permute-start.18) | collective-permute-done | bytes 44064 | tf_op jit(solution)/shard_map/ppermute | solution.py:36
  33.9 0.7 %shard_map.123 = f32[172,1,128]{2,1,0:T(1,128)} custom-call(bf16[172,128]{1,0:T(8,128)(2,1)S(1)} %get-tuple-element.21.refs_0_, bf16[172,128]{1,0:T(8,128)(2,1)S(1)} %collective-permute-done.17.refs_1_, bf16[172,128]{1,0:T(8,128)(2,1)S(1)} %collective-permute-done.18.refs_2_, bf16[172,128]{1,0:T(8,128)(2,1)S(1)} %collective-permute-done.19.refs_3_, ...), custom_call_target="tpu_custom_call" | custom-call | tf_op jit(solution)/shard_map/pallas_call | solution.py:74
  (41 shorter events, 2.7 us)
Async XLA Ops:
  0.6 8.5 %copy-start.4 = (f32[172]{0:T(256)S(1)}, f32[172]{0:T(256)}, u32[]{:S(2)}) copy-start(f32[172]{0:T(256)} %param.19) | copy-start | bytes 2068
  0.7 7.4 %collective-permute-start.2 = (bf16[128,128]{1,0:T(8,128)(2,1)}, bf16[128,128]{1,0:T(8,128)(2,1)S(1)}, u32[]{:S(2)}, u32[]{:S(2)}) collective-permute-start(bf16[128,128]{1,0:T(8,128)(2,1)} %bitcast.18), channel_id=1, source_target_pairs={{28,0},{24,4},{20,8},{16,12},{12,16},{8,20},{4,24},{0,28},{29,1},{... | collective-permute-start | bytes 98312 | tf_op jit(solution)/shard_map/ppermute | solution.py:40
  4.1 4.0 %collective-permute-start.1 = (bf16[128,128]{1,0:T(8,128)(2,1)}, bf16[128,128]{1,0:T(8,128)(2,1)S(1)}, u32[]{:S(2)}, u32[]{:S(2)}) collective-permute-start(bf16[128,128]{1,0:T(8,128)(2,1)} %bitcast.19), channel_id=1, source_target_pairs={{12,0},{16,4},{4,8},{24,12},{28,16},{0,20},{20,24},{8,28},{13,1},{... | collective-permute-start | bytes 98312 | tf_op jit(solution)/shard_map/ppermute | solution.py:40
  4.9 3.8 %collective-permute-start = (bf16[128,128]{1,0:T(8,128)(2,1)}, bf16[128,128]{1,0:T(8,128)(2,1)S(1)}, u32[]{:S(2)}, u32[]{:S(2)}) collective-permute-start(bf16[128,128]{1,0:T(8,128)(2,1)} %bitcast.20), channel_id=1, source_target_pairs={{20,0},{8,4},{28,8},{0,12},{4,16},{24,20},{12,24},{16,28},{21,1},{... | collective-permute-start | bytes 98312 | tf_op jit(solution)/shard_map/ppermute | solution.py:40
  6.5 12.3 %copy-start = (bf16[256,172]{0,1:T(8,128)(2,1)S(1)}, bf16[256,172]{0,1:T(8,128)(2,1)}, u32[]{:S(2)}) copy-start(bf16[256,172]{0,1:T(8,128)(2,1)} %param.18) | copy-start | bytes 264196
  6.5 12.3 %copy-start.2 = (bf16[128,256]{1,0:T(8,128)(2,1)S(1)}, bf16[128,256]{1,0:T(8,128)(2,1)}, u32[]{:S(2)}) copy-start(bf16[128,256]{1,0:T(8,128)(2,1)} %refs_5_.1) | copy-start | bytes 196612
  6.5 12.3 %copy-start.5 = (f32[256]{0:T(256)S(1)}, f32[256]{0:T(256)}, u32[]{:S(2)}) copy-start(f32[256]{0:T(256)} %param.17) | copy-start | bytes 3076
  8.7 1.4 %collective-permute-start.3 = (bf16[512,128]{1,0:T(8,128)(2,1)S(1)}, bf16[512,128]{1,0:T(8,128)(2,1)S(1)}, u32[]{:S(2)}, u32[]{:S(2)}) collective-permute-start(bf16[512,128]{1,0:T(8,128)(2,1)S(1)} %shard_map.114.mine_ref.refs_0_), channel_id=1, source_target_pairs={{0,4},{4,0},{8,12},{12,8},{16,20},{20,16},{24,28},{28,24},{1,5},{5... | collective-permute-start | bytes 393224 | tf_op jit(solution)/shard_map/ppermute | solution.py:36
  9.2 6.1 %collective-permute-start.8 = (bf16[128,256]{1,0:T(8,128)(2,1)S(1)}, bf16[128,256]{1,0:T(8,128)(2,1)S(1)}, u32[]{:S(2)}, u32[]{:S(2)}) collective-permute-start(bf16[128,256]{1,0:T(8,128)(2,1)S(1)} %get-tuple-element.18), channel_id=1, source_target_pairs={{0,4},{4,0},{8,12},{12,8},{16,20},{20,16},{24,28},{28,24},{1,5},{5... | collective-permute-start | bytes 196616 | tf_op jit(solution)/shard_map/ppermute | solution.py:36
  10.4 5.8 %collective-permute-start.4 = (bf16[128,128]{1,0:T(8,128)(2,1)S(1)}, bf16[128,128]{1,0:T(8,128)(2,1)S(1)}, u32[]{:S(2)}, u32[]{:S(2)}) collective-permute-start(bf16[128,128]{1,0:T(8,128)(2,1)S(1)} %get-tuple-element.14), channel_id=1, source_target_pairs={{0,7},{1,6},{2,5},{3,4},{4,3},{5,2},{6,1},{7,0},{8,15},{9,14},{10,... | collective-permute-start | bytes 98312 | tf_op jit(solution)/shard_map/ppermute | solution.py:64
  14.5 4.2 %collective-permute-start.5 = (bf16[128,128]{1,0:T(8,128)(2,1)S(1)}, bf16[128,128]{1,0:T(8,128)(2,1)S(1)}, u32[]{:S(2)}, u32[]{:S(2)}) collective-permute-start(bf16[128,128]{1,0:T(8,128)(2,1)S(1)} %get-tuple-element.15), channel_id=1, source_target_pairs={{0,6},{1,7},{2,4},{3,5},{4,2},{5,3},{6,0},{7,1},{8,14},{9,15},{10,... | collective-permute-start | bytes 98312 | tf_op jit(solution)/shard_map/ppermute | solution.py:64
  14.5 4.2 %collective-permute-start.6 = (bf16[128,128]{1,0:T(8,128)(2,1)S(1)}, bf16[128,128]{1,0:T(8,128)(2,1)S(1)}, u32[]{:S(2)}, u32[]{:S(2)}) collective-permute-start(bf16[128,128]{1,0:T(8,128)(2,1)S(1)} %get-tuple-element.16), channel_id=1, source_target_pairs={{0,5},{1,4},{2,7},{3,6},{4,1},{5,0},{6,3},{7,2},{8,13},{9,12},{10,... | collective-permute-start | bytes 98312 | tf_op jit(solution)/shard_map/ppermute | solution.py:64
  15.0 3.8 %collective-permute-start.7 = (bf16[128,128]{1,0:T(8,128)(2,1)S(1)}, bf16[128,128]{1,0:T(8,128)(2,1)S(1)}, u32[]{:S(2)}, u32[]{:S(2)}) collective-permute-start(bf16[128,128]{1,0:T(8,128)(2,1)S(1)} %get-tuple-element.17), channel_id=1, source_target_pairs={{0,4},{1,5},{2,6},{3,7},{4,0},{5,1},{6,2},{7,3},{8,12},{9,13},{10,... | collective-permute-start | bytes 98312 | tf_op jit(solution)/shard_map/ppermute | solution.py:64
  19.1 4.7 %collective-permute-start.10 = (bf16[172,128]{1,0:T(8,128)(2,1)S(1)}, bf16[172,128]{1,0:T(8,128)(2,1)S(1)}, u32[]{:S(2)}, u32[]{:S(2)}) collective-permute-start(bf16[172,128]{1,0:T(8,128)(2,1)S(1)} %get-tuple-element.20.refs_0_), channel_id=1, source_target_pairs={{28,0},{24,4},{20,8},{16,12},{12,16},{8,20},{4,24},{0,28},{29,1},{... | collective-permute-start | bytes 132104 | tf_op jit(solution)/shard_map/ppermute | solution.py:40
  19.8 4.3 %collective-permute-start.9 = (bf16[172,128]{1,0:T(8,128)(2,1)S(1)}, bf16[172,128]{1,0:T(8,128)(2,1)S(1)}, u32[]{:S(2)}, u32[]{:S(2)}) collective-permute-start(bf16[172,128]{1,0:T(8,128)(2,1)S(1)} %get-tuple-element.20.refs_0_), channel_id=1, source_target_pairs={{12,0},{16,4},{4,8},{24,12},{28,16},{0,20},{20,24},{8,28},{13,1},{... | collective-permute-start | bytes 132104 | tf_op jit(solution)/shard_map/ppermute | solution.py:40
  20.6 4.5 %collective-permute-start.16 = (bf16[172,128]{1,0:T(8,128)(2,1)S(1)}, bf16[172,128]{1,0:T(8,128)(2,1)S(1)}, u32[]{:S(2)}, u32[]{:S(2)}) collective-permute-start(bf16[172,128]{1,0:T(8,128)(2,1)S(1)} %get-tuple-element.20.refs_0_), channel_id=1, source_target_pairs={{8,0},{20,4},{0,8},{28,12},{24,16},{4,20},{16,24},{12,28},{9,1},{2... | collective-permute-start | bytes 132104 | tf_op jit(solution)/shard_map/ppermute | solution.py:40
  22.4 3.5 %collective-permute-start.13 = (bf16[172,128]{1,0:T(8,128)(2,1)S(1)}, bf16[172,128]{1,0:T(8,128)(2,1)S(1)}, u32[]{:S(2)}, u32[]{:S(2)}) collective-permute-start(bf16[172,128]{1,0:T(8,128)(2,1)S(1)} %get-tuple-element.20.refs_0_), channel_id=1, source_target_pairs={{20,0},{8,4},{28,8},{0,12},{4,16},{24,20},{12,24},{16,28},{21,1},{... | collective-permute-start | bytes 132104 | tf_op jit(solution)/shard_map/ppermute | solution.py:40
  22.4 3.5 %collective-permute-start.12 = (bf16[172,128]{1,0:T(8,128)(2,1)S(1)}, bf16[172,128]{1,0:T(8,128)(2,1)S(1)}, u32[]{:S(2)}, u32[]{:S(2)}) collective-permute-start(bf16[172,128]{1,0:T(8,128)(2,1)S(1)} %get-tuple-element.20.refs_0_), channel_id=1, source_target_pairs={{0,4},{4,0},{8,12},{12,8},{16,20},{20,16},{24,28},{28,24},{1,5},{5... | collective-permute-start | bytes 132104 | tf_op jit(solution)/shard_map/ppermute | solution.py:36
  23.9 2.0 %collective-permute-start.14 = (bf16[172,128]{1,0:T(8,128)(2,1)S(1)}, bf16[172,128]{1,0:T(8,128)(2,1)S(1)}, u32[]{:S(2)}, u32[]{:S(2)}) collective-permute-start(bf16[172,128]{1,0:T(8,128)(2,1)S(1)} %collective-permute-done.10.refs_2_), channel_id=1, source_target_pairs={{0,4},{4,0},{8,12},{12,8},{16,20},{20,16},{24,28},{28,24},{1,5},{5... | collective-permute-start | bytes 132104 | tf_op jit(solution)/shard_map/ppermute | solution.py:36
  24.1 1.8 %collective-permute-start.15 = (bf16[172,128]{1,0:T(8,128)(2,1)S(1)}, bf16[172,128]{1,0:T(8,128)(2,1)S(1)}, u32[]{:S(2)}, u32[]{:S(2)}) collective-permute-start(bf16[172,128]{1,0:T(8,128)(2,1)S(1)} %collective-permute-done.9.refs_1_), channel_id=1, source_target_pairs={{0,4},{4,0},{8,12},{12,8},{16,20},{20,16},{24,28},{28,24},{1,5},{5... | collective-permute-start | bytes 132104 | tf_op jit(solution)/shard_map/ppermute | solution.py:36
  25.1 5.6 %collective-permute-start.11 = (bf16[128,256]{1,0:T(8,128)(2,1)S(1)}, bf16[128,256]{1,0:T(8,128)(2,1)S(1)}, u32[]{:S(2)}, u32[]{:S(2)}) collective-permute-start(bf16[128,256]{1,0:T(8,128)(2,1)S(1)} %shard_map.120), channel_id=1, source_target_pairs={{0,4},{4,0},{8,12},{12,8},{16,20},{20,16},{24,28},{28,24},{1,5},{5... | collective-permute-start | bytes 196616 | tf_op jit(solution)/shard_map/ppermute | solution.py:36
  26.3 6.2 %collective-permute-start.17 = (bf16[172,128]{1,0:T(8,128)(2,1)S(1)}, bf16[172,128]{1,0:T(8,128)(2,1)S(1)}, u32[]{:S(2)}, u32[]{:S(2)}) collective-permute-start(bf16[172,128]{1,0:T(8,128)(2,1)S(1)} %get-tuple-element.22), channel_id=1, source_target_pairs={{0,3},{1,2},{2,1},{3,0},{4,7},{5,6},{6,5},{7,4},{8,11},{9,10},{10,... | collective-permute-start | bytes 132104 | tf_op jit(solution)/shard_map/ppermute | solution.py:36
  28.4 5.5 %collective-permute-start.18 = (bf16[172,128]{1,0:T(8,128)(2,1)S(1)}, bf16[172,128]{1,0:T(8,128)(2,1)S(1)}, u32[]{:S(2)}, u32[]{:S(2)}) collective-permute-start(bf16[172,128]{1,0:T(8,128)(2,1)S(1)} %get-tuple-element.23), channel_id=1, source_target_pairs={{0,2},{1,3},{2,0},{3,1},{4,6},{5,7},{6,4},{7,5},{8,10},{9,11},{10,... | collective-permute-start | bytes 132104 | tf_op jit(solution)/shard_map/ppermute | solution.py:36
  28.4 5.5 %collective-permute-start.19 = (bf16[172,128]{1,0:T(8,128)(2,1)S(1)}, bf16[172,128]{1,0:T(8,128)(2,1)S(1)}, u32[]{:S(2)}, u32[]{:S(2)}) collective-permute-start(bf16[172,128]{1,0:T(8,128)(2,1)S(1)} %get-tuple-element.24), channel_id=1, source_target_pairs={{0,1},{1,0},{2,3},{3,2},{4,5},{5,4},{6,7},{7,6},{8,9},{9,8},{10,11... | collective-permute-start | bytes 132104 | tf_op jit(solution)/shard_map/ppermute | solution.py:36
  (3 other events, 25.0 us)

commit v7 on v4

--- a/solution.py
+++ b/solution.py
@@ -289,7 +289,7 @@
 
     if dense_form:
         anywhere = pl.BlockSpec(memory_space=pl.ANY)
-        chunks = 8
+        chunks = 16
         dense = call(
             functools.partial(build_kernel, n_row, n_col, chunks),
             shape((n_col * block, n_row * block), BF16),

time: 34.4 us -> 34.4 us (level)
  Pallas kernels: 5.27 us -> 4.82 us
  starting transfers between devices: 20.2 us -> 20.6 us
    ppermute x9, starting transfers between devices: 7.14 us -> 7.84 us  [permuted(): lax.ppermute(block, axis, [(i, partner(i, slot)) for i in range(size)])]
    ppermute x7, waiting for transfers between devices: 1.08 us -> 1.59 us  [fetched(): lax.ppermute(block, axis, [(partner(i, seen(slot, i)), i) for i in range(...]
    pallas_call x13, Pallas kernels: 5.27 us -> 4.82 us  [call(): pl.pallas_call(kernel, out_shape=out_shape, in_specs=specs or [vmem] * le...]
    ppermute x4, waiting for transfers between devices: 3.49 us -> 3.09 us  [send_across(): arrived.append(lax.ppermute(blocks[slot], ('row', 'col'), pairs))]
  transfers between devices with their start and end apart: 20 -> 20, of which waited for: 8 -> 8; matrix products, arithmetic and copies ran while one was open for 0% -> 0% of each run, Pallas kernels for 12% -> 11%
where the time goes in v7:
time: 34.4 us; the launch traced here: 34.3 us
  starting transfers between devices  20.6 us (60%)
  waiting for transfers between devices  7.41 us (22%)
  Pallas kernels  4.82 us (14%)
  between operations  1.48 us (4%)
    ppermute x7, starting transfers between devices, fetched(): lax.ppermute(block, axis, [(partner(i, seen(slot, i)), i) for i in range(...  8.44 us
    ppermute x9, starting transfers between devices, permuted(): lax.ppermute(block, axis, [(i, partner(i, slot)) for i in range(size)])  7.84 us
    pallas_call x13, Pallas kernels, call(): pl.pallas_call(kernel, out_shape=out_shape, in_specs=specs or [vmem] * le...  4.82 us
    ppermute x4, starting transfers between devices, send_across(): arrived.append(lax.ppermute(blocks[slot], ('row', 'col'), pairs))  4.3 us
    ppermute x4, waiting for transfers between devices, send_across(): arrived.append(lax.ppermute(blocks[slot], ('row', 'col'), pairs))  3.09 us
    ppermute x9, waiting for transfers between devices, permuted(): lax.ppermute(block, axis, [(i, partner(i, slot)) for i in range(size)])  2.73 us
    ppermute x7, waiting for transfers between devices, fetched(): lax.ppermute(block, axis, [(partner(i, seen(slot, i)), i) for i in range(...  1.59 us
  transfers between devices with their start and end apart: 20, of which 8 were waited for; matrix products, arithmetic and copies ran while one was open for 0% of the time, Pallas kernels for 11%

profile of v7, /device:TPU:0, one launch (start us, length us, event | category | flops | bytes accessed | tf_op | source)
XLA Modules:
  0.0 34.3 jit_solution(16018788806307836484)
XLA Ops:
  0.7 3.4 %collective-permute-start.2 = (bf16[128,128]{1,0:T(8,128)(2,1)}, bf16[128,128]{1,0:T(8,128)(2,1)S(1)}, u32[]{:S(2)}, u32[]{:S(2)}) collective-permute-start(bf16[128,128]{1,0:T(8,128)(2,1)} %bitcast.18), channel_id=1, source_target_pairs={{28,0},{24,4},{20,8},{16,12},{12,16},{8,20},{4,24},{0,28},{29,1},{... | collective-permute-start | bytes 98312 | tf_op jit(solution)/shard_map/ppermute | solution.py:40
  4.1 0.8 %collective-permute-start.1 = (bf16[128,128]{1,0:T(8,128)(2,1)}, bf16[128,128]{1,0:T(8,128)(2,1)S(1)}, u32[]{:S(2)}, u32[]{:S(2)}) collective-permute-start(bf16[128,128]{1,0:T(8,128)(2,1)} %bitcast.19), channel_id=1, source_target_pairs={{12,0},{16,4},{4,8},{24,12},{28,16},{0,20},{20,24},{8,28},{13,1},{... | collective-permute-start | bytes 98312 | tf_op jit(solution)/shard_map/ppermute | solution.py:40
  4.9 1.0 %collective-permute-start = (bf16[128,128]{1,0:T(8,128)(2,1)}, bf16[128,128]{1,0:T(8,128)(2,1)S(1)}, u32[]{:S(2)}, u32[]{:S(2)}) collective-permute-start(bf16[128,128]{1,0:T(8,128)(2,1)} %bitcast.20), channel_id=1, source_target_pairs={{20,0},{8,4},{28,8},{0,12},{4,16},{24,20},{12,24},{16,28},{21,1},{... | collective-permute-start | bytes 98312 | tf_op jit(solution)/shard_map/ppermute | solution.py:40
  6.5 1.6 %shard_map.113.refs_4_.dense_ref = bf16[512,1024]{1,0:T(8,128)(2,1)S(1)} custom-call(s32[1,1]{1,0:T(1,128)S(6)} %copy.13.count, s32[2,128]{1,0:T(2,128)} %bitcast.28, bf16[128,128,128]{2,1,0:T(8,128)(2,1)} %bitcast.25), custom_call_target="tpu_custom_call" | custom-call | flops 2097152 | bytes 4194304 | tf_op jit(solution)/shard_map/pallas_call | solution.py:74
  8.1 0.6 %collective-permute-done.refs_1_ = bf16[128,128]{1,0:T(8,128)(2,1)S(1)} collective-permute-done((bf16[128,128]{1,0:T(8,128)(2,1)}, bf16[128,128]{1,0:T(8,128)(2,1)S(1)}, u32[]{:S(2)}, u32[]{:S(2)}) %collective-permute-start) | collective-permute-done | bytes 32800 | tf_op jit(solution)/shard_map/ppermute | solution.py:40
  8.7 1.1 %collective-permute-start.3 = (bf16[512,128]{1,0:T(8,128)(2,1)S(1)}, bf16[512,128]{1,0:T(8,128)(2,1)S(1)}, u32[]{:S(2)}, u32[]{:S(2)}) collective-permute-start(bf16[512,128]{1,0:T(8,128)(2,1)S(1)} %shard_map.114.mine_ref.refs_0_), channel_id=1, source_target_pairs={{0,4},{4,0},{8,12},{12,8},{16,20},{20,16},{24,28},{28,24},{1,5},{5... | collective-permute-start | bytes 393224 | tf_op jit(solution)/shard_map/ppermute | solution.py:36
  10.4 0.5 %collective-permute-done.3.other_ref.refs_4_ = bf16[512,128]{1,0:T(8,128)(2,1)S(1)} collective-permute-done((bf16[512,128]{1,0:T(8,128)(2,1)S(1)}, bf16[512,128]{1,0:T(8,128)(2,1)S(1)}, u32[]{:S(2)}, u32[]{:S(2)}) %collective-permute-start.3) | collective-permute-done | bytes 131104 | tf_op jit(solution)/shard_map/ppermute | solution.py:36
  11.1 2.8 %collective-permute-start.4 = (bf16[128,128]{1,0:T(8,128)(2,1)S(1)}, bf16[128,128]{1,0:T(8,128)(2,1)S(1)}, u32[]{:S(2)}, u32[]{:S(2)}) collective-permute-start(bf16[128,128]{1,0:T(8,128)(2,1)S(1)} %get-tuple-element.14), channel_id=1, source_target_pairs={{0,7},{1,6},{2,5},{3,4},{4,3},{5,2},{6,1},{7,0},{8,15},{9,14},{10,... | collective-permute-start | bytes 98312 | tf_op jit(solution)/shard_map/ppermute | solution.py:64
  14.0 1.3 %collective-permute-start.6 = (bf16[128,128]{1,0:T(8,128)(2,1)S(1)}, bf16[128,128]{1,0:T(8,128)(2,1)S(1)}, u32[]{:S(2)}, u32[]{:S(2)}) collective-permute-start(bf16[128,128]{1,0:T(8,128)(2,1)S(1)} %get-tuple-element.16), channel_id=1, source_target_pairs={{0,5},{1,4},{2,7},{3,6},{4,1},{5,0},{6,3},{7,2},{8,13},{9,12},{10,... | collective-permute-start | bytes 98312 | tf_op jit(solution)/shard_map/ppermute | solution.py:64
  15.4 0.9 %collective-permute-done.4.refs_0_ = bf16[128,128]{1,0:T(8,128)(2,1)S(1)} collective-permute-done((bf16[128,128]{1,0:T(8,128)(2,1)S(1)}, bf16[128,128]{1,0:T(8,128)(2,1)S(1)}, u32[]{:S(2)}, u32[]{:S(2)}) %collective-permute-start.4) | collective-permute-done | bytes 32800 | tf_op jit(solution)/shard_map/ppermute | solution.py:64
  16.3 2.2 %collective-permute-done.5.refs_1_ = bf16[128,128]{1,0:T(8,128)(2,1)S(1)} collective-permute-done((bf16[128,128]{1,0:T(8,128)(2,1)S(1)}, bf16[128,128]{1,0:T(8,128)(2,1)S(1)}, u32[]{:S(2)}, u32[]{:S(2)}) %collective-permute-start.5) | collective-permute-done | bytes 32800 | tf_op jit(solution)/shard_map/ppermute | solution.py:64
  18.9 0.9 %collective-permute-start.10 = (bf16[172,128]{1,0:T(8,128)(2,1)S(1)}, bf16[172,128]{1,0:T(8,128)(2,1)S(1)}, u32[]{:S(2)}, u32[]{:S(2)}) collective-permute-start(bf16[172,128]{1,0:T(8,128)(2,1)S(1)} %get-tuple-element.20.refs_0_), channel_id=1, source_target_pairs={{28,0},{24,4},{20,8},{16,12},{12,16},{8,20},{4,24},{0,28},{29,1},{... | collective-permute-start | bytes 132104 | tf_op jit(solution)/shard_map/ppermute | solution.py:40
  19.8 0.8 %collective-permute-start.9 = (bf16[172,128]{1,0:T(8,128)(2,1)S(1)}, bf16[172,128]{1,0:T(8,128)(2,1)S(1)}, u32[]{:S(2)}, u32[]{:S(2)}) collective-permute-start(bf16[172,128]{1,0:T(8,128)(2,1)S(1)} %get-tuple-element.20.refs_0_), channel_id=1, source_target_pairs={{12,0},{16,4},{4,8},{24,12},{28,16},{0,20},{20,24},{8,28},{13,1},{... | collective-permute-start | bytes 132104 | tf_op jit(solution)/shard_map/ppermute | solution.py:40
  20.6 1.5 %collective-permute-start.16 = (bf16[172,128]{1,0:T(8,128)(2,1)S(1)}, bf16[172,128]{1,0:T(8,128)(2,1)S(1)}, u32[]{:S(2)}, u32[]{:S(2)}) collective-permute-start(bf16[172,128]{1,0:T(8,128)(2,1)S(1)} %get-tuple-element.20.refs_0_), channel_id=1, source_target_pairs={{8,0},{20,4},{0,8},{28,12},{24,16},{4,20},{16,24},{12,28},{9,1},{2... | collective-permute-start | bytes 132104 | tf_op jit(solution)/shard_map/ppermute | solution.py:40
  22.2 0.9 %collective-permute-start.12 = (bf16[172,128]{1,0:T(8,128)(2,1)S(1)}, bf16[172,128]{1,0:T(8,128)(2,1)S(1)}, u32[]{:S(2)}, u32[]{:S(2)}) collective-permute-start(bf16[172,128]{1,0:T(8,128)(2,1)S(1)} %get-tuple-element.20.refs_0_), channel_id=1, source_target_pairs={{0,4},{4,0},{8,12},{12,8},{16,20},{20,16},{24,28},{28,24},{1,5},{5... | collective-permute-start | bytes 132104 | tf_op jit(solution)/shard_map/ppermute | solution.py:36
  23.1 0.4 %collective-permute-done.10.refs_2_ = bf16[172,128]{1,0:T(8,128)(2,1)S(1)} collective-permute-done((bf16[172,128]{1,0:T(8,128)(2,1)S(1)}, bf16[172,128]{1,0:T(8,128)(2,1)S(1)}, u32[]{:S(2)}, u32[]{:S(2)}) %collective-permute-start.10) | collective-permute-done | bytes 44064 | tf_op jit(solution)/shard_map/ppermute | solution.py:40
  23.9 0.8 %collective-permute-start.15 = (bf16[172,128]{1,0:T(8,128)(2,1)S(1)}, bf16[172,128]{1,0:T(8,128)(2,1)S(1)}, u32[]{:S(2)}, u32[]{:S(2)}) collective-permute-start(bf16[172,128]{1,0:T(8,128)(2,1)S(1)} %collective-permute-done.9.refs_1_), channel_id=1, source_target_pairs={{0,4},{4,0},{8,12},{12,8},{16,20},{20,16},{24,28},{28,24},{1,5},{5... | collective-permute-start | bytes 132104 | tf_op jit(solution)/shard_map/ppermute | solution.py:36
  25.1 0.5 %collective-permute-done.13.near_ref = bf16[172,128]{1,0:T(8,128)(2,1)S(1)} collective-permute-done((bf16[172,128]{1,0:T(8,128)(2,1)S(1)}, bf16[172,128]{1,0:T(8,128)(2,1)S(1)}, u32[]{:S(2)}, u32[]{:S(2)}) %collective-permute-start.13) | collective-permute-done | bytes 44064 | tf_op jit(solution)/shard_map/ppermute | solution.py:40
  26.0 2.5 %collective-permute-start.17 = (bf16[172,128]{1,0:T(8,128)(2,1)S(1)}, bf16[172,128]{1,0:T(8,128)(2,1)S(1)}, u32[]{:S(2)}, u32[]{:S(2)}) collective-permute-start(bf16[172,128]{1,0:T(8,128)(2,1)S(1)} %get-tuple-element.24), channel_id=1, source_target_pairs={{0,3},{1,2},{2,1},{3,0},{4,7},{5,6},{6,5},{7,4},{8,11},{9,10},{10,... | collective-permute-start | bytes 132104 | tf_op jit(solution)/shard_map/ppermute | solution.py:36
  28.5 1.9 %collective-permute-start.19 = (bf16[172,128]{1,0:T(8,128)(2,1)S(1)}, bf16[172,128]{1,0:T(8,128)(2,1)S(1)}, u32[]{:S(2)}, u32[]{:S(2)}) collective-permute-start(bf16[172,128]{1,0:T(8,128)(2,1)S(1)} %get-tuple-element.23.refs_0_), channel_id=1, source_target_pairs={{0,1},{1,0},{2,3},{3,2},{4,5},{5,4},{6,7},{7,6},{8,9},{9,8},{10,11... | collective-permute-start | bytes 132104 | tf_op jit(solution)/shard_map/ppermute | solution.py:36
  30.7 0.6 %shard_map.121 = bf16[128,256]{1,0:T(8,128)(2,1)} custom-call(bf16[128,256]{1,0:T(8,128)(2,1)S(1)} %collective-permute-done.11.value), custom_call_target="tpu_custom_call" | custom-call | tf_op jit(solution)/shard_map/pallas_call | solution.py:74
  31.3 0.9 %collective-permute-done.17.refs_3_ = bf16[172,128]{1,0:T(8,128)(2,1)S(1)} collective-permute-done((bf16[172,128]{1,0:T(8,128)(2,1)S(1)}, bf16[172,128]{1,0:T(8,128)(2,1)S(1)}, u32[]{:S(2)}, u32[]{:S(2)}) %collective-permute-start.17) | collective-permute-done | bytes 44064 | tf_op jit(solution)/shard_map/ppermute | solution.py:36
  32.2 1.4 %collective-permute-done.18.refs_0_ = bf16[172,128]{1,0:T(8,128)(2,1)S(1)} collective-permute-done((bf16[172,128]{1,0:T(8,128)(2,1)S(1)}, bf16[172,128]{1,0:T(8,128)(2,1)S(1)}, u32[]{:S(2)}, u32[]{:S(2)}) %collective-permute-start.18) | collective-permute-done | bytes 44064 | tf_op jit(solution)/shard_map/ppermute | solution.py:36
  33.6 0.7 %shard_map.125 = f32[172,1,128]{2,1,0:T(1,128)} custom-call(f32[172,128]{1,0:T(8,128)S(1)} %shard_map.124.begun, bf16[172,128]{1,0:T(8,128)(2,1)S(1)} %collective-permute-done.18.refs_0_, bf16[172,128]{1,0:T(8,128)(2,1)S(1)} %collective-permute-done.19.refs_1_), custom_call_target="tpu_custom_call" | custom-call | tf_op jit(solution)/shard_map/pallas_call | solution.py:74
  (43 shorter events, 2.7 us)
Async XLA Ops:
  0.6 9.2 %copy-start.4 = (f32[172]{0:T(256)S(1)}, f32[172]{0:T(256)}, u32[]{:S(2)}) copy-start(f32[172]{0:T(256)} %param.19) | copy-start | bytes 2068
  0.7 7.4 %collective-permute-start.2 = (bf16[128,128]{1,0:T(8,128)(2,1)}, bf16[128,128]{1,0:T(8,128)(2,1)S(1)}, u32[]{:S(2)}, u32[]{:S(2)}) collective-permute-start(bf16[128,128]{1,0:T(8,128)(2,1)} %bitcast.18), channel_id=1, source_target_pairs={{28,0},{24,4},{20,8},{16,12},{12,16},{8,20},{4,24},{0,28},{29,1},{... | collective-permute-start | bytes 98312 | tf_op jit(solution)/shard_map/ppermute | solution.py:40
  4.1 4.0 %collective-permute-start.1 = (bf16[128,128]{1,0:T(8,128)(2,1)}, bf16[128,128]{1,0:T(8,128)(2,1)S(1)}, u32[]{:S(2)}, u32[]{:S(2)}) collective-permute-start(bf16[128,128]{1,0:T(8,128)(2,1)} %bitcast.19), channel_id=1, source_target_pairs={{12,0},{16,4},{4,8},{24,12},{28,16},{0,20},{20,24},{8,28},{13,1},{... | collective-permute-start | bytes 98312 | tf_op jit(solution)/shard_map/ppermute | solution.py:40
  4.9 3.8 %collective-permute-start = (bf16[128,128]{1,0:T(8,128)(2,1)}, bf16[128,128]{1,0:T(8,128)(2,1)S(1)}, u32[]{:S(2)}, u32[]{:S(2)}) collective-permute-start(bf16[128,128]{1,0:T(8,128)(2,1)} %bitcast.20), channel_id=1, source_target_pairs={{20,0},{8,4},{28,8},{0,12},{4,16},{24,20},{12,24},{16,28},{21,1},{... | collective-permute-start | bytes 98312 | tf_op jit(solution)/shard_map/ppermute | solution.py:40
  6.5 12.1 %copy-start = (bf16[256,172]{0,1:T(8,128)(2,1)S(1)}, bf16[256,172]{0,1:T(8,128)(2,1)}, u32[]{:S(2)}) copy-start(bf16[256,172]{0,1:T(8,128)(2,1)} %param.18) | copy-start | bytes 264196
  6.5 12.1 %copy-start.2 = (bf16[128,256]{1,0:T(8,128)(2,1)S(1)}, bf16[128,256]{1,0:T(8,128)(2,1)}, u32[]{:S(2)}) copy-start(bf16[128,256]{1,0:T(8,128)(2,1)} %refs_5_.1) | copy-start | bytes 196612
  6.5 12.1 %copy-start.5 = (f32[256]{0:T(256)S(1)}, f32[256]{0:T(256)}, u32[]{:S(2)}) copy-start(f32[256]{0:T(256)} %param.17) | copy-start | bytes 3076
  8.7 2.1 %collective-permute-start.3 = (bf16[512,128]{1,0:T(8,128)(2,1)S(1)}, bf16[512,128]{1,0:T(8,128)(2,1)S(1)}, u32[]{:S(2)}, u32[]{:S(2)}) collective-permute-start(bf16[512,128]{1,0:T(8,128)(2,1)S(1)} %shard_map.114.mine_ref.refs_0_), channel_id=1, source_target_pairs={{0,4},{4,0},{8,12},{12,8},{16,20},{20,16},{24,28},{28,24},{1,5},{5... | collective-permute-start | bytes 393224 | tf_op jit(solution)/shard_map/ppermute | solution.py:36
  10.0 5.5 %collective-permute-start.8 = (bf16[128,256]{1,0:T(8,128)(2,1)S(1)}, bf16[128,256]{1,0:T(8,128)(2,1)S(1)}, u32[]{:S(2)}, u32[]{:S(2)}) collective-permute-start(bf16[128,256]{1,0:T(8,128)(2,1)S(1)} %get-tuple-element.18), channel_id=1, source_target_pairs={{0,4},{4,0},{8,12},{12,8},{16,20},{20,16},{24,28},{28,24},{1,5},{5... | collective-permute-start | bytes 196616 | tf_op jit(solution)/shard_map/ppermute | solution.py:36
  11.1 5.2 %collective-permute-start.4 = (bf16[128,128]{1,0:T(8,128)(2,1)S(1)}, bf16[128,128]{1,0:T(8,128)(2,1)S(1)}, u32[]{:S(2)}, u32[]{:S(2)}) collective-permute-start(bf16[128,128]{1,0:T(8,128)(2,1)S(1)} %get-tuple-element.14), channel_id=1, source_target_pairs={{0,7},{1,6},{2,5},{3,4},{4,3},{5,2},{6,1},{7,0},{8,15},{9,14},{10,... | collective-permute-start | bytes 98312 | tf_op jit(solution)/shard_map/ppermute | solution.py:64
  13.9 4.6 %collective-permute-start.5 = (bf16[128,128]{1,0:T(8,128)(2,1)S(1)}, bf16[128,128]{1,0:T(8,128)(2,1)S(1)}, u32[]{:S(2)}, u32[]{:S(2)}) collective-permute-start(bf16[128,128]{1,0:T(8,128)(2,1)S(1)} %get-tuple-element.15), channel_id=1, source_target_pairs={{0,6},{1,7},{2,4},{3,5},{4,2},{5,3},{6,0},{7,1},{8,14},{9,15},{10,... | collective-permute-start | bytes 98312 | tf_op jit(solution)/shard_map/ppermute | solution.py:64
  14.0 4.6 %collective-permute-start.6 = (bf16[128,128]{1,0:T(8,128)(2,1)S(1)}, bf16[128,128]{1,0:T(8,128)(2,1)S(1)}, u32[]{:S(2)}, u32[]{:S(2)}) collective-permute-start(bf16[128,128]{1,0:T(8,128)(2,1)S(1)} %get-tuple-element.16), channel_id=1, source_target_pairs={{0,5},{1,4},{2,7},{3,6},{4,1},{5,0},{6,3},{7,2},{8,13},{9,12},{10,... | collective-permute-start | bytes 98312 | tf_op jit(solution)/shard_map/ppermute | solution.py:64
  15.3 3.3 %collective-permute-start.7 = (bf16[128,128]{1,0:T(8,128)(2,1)S(1)}, bf16[128,128]{1,0:T(8,128)(2,1)S(1)}, u32[]{:S(2)}, u32[]{:S(2)}) collective-permute-start(bf16[128,128]{1,0:T(8,128)(2,1)S(1)} %get-tuple-element.17), channel_id=1, source_target_pairs={{0,4},{1,5},{2,6},{3,7},{4,0},{5,1},{6,2},{7,3},{8,12},{9,13},{10,... | collective-permute-start | bytes 98312 | tf_op jit(solution)/shard_map/ppermute | solution.py:64
  18.9 4.7 %collective-permute-start.10 = (bf16[172,128]{1,0:T(8,128)(2,1)S(1)}, bf16[172,128]{1,0:T(8,128)(2,1)S(1)}, u32[]{:S(2)}, u32[]{:S(2)}) collective-permute-start(bf16[172,128]{1,0:T(8,128)(2,1)S(1)} %get-tuple-element.20.refs_0_), channel_id=1, source_target_pairs={{28,0},{24,4},{20,8},{16,12},{12,16},{8,20},{4,24},{0,28},{29,1},{... | collective-permute-start | bytes 132104 | tf_op jit(solution)/shard_map/ppermute | solution.py:40
  19.8 4.1 %collective-permute-start.9 = (bf16[172,128]{1,0:T(8,128)(2,1)S(1)}, bf16[172,128]{1,0:T(8,128)(2,1)S(1)}, u32[]{:S(2)}, u32[]{:S(2)}) collective-permute-start(bf16[172,128]{1,0:T(8,128)(2,1)S(1)} %get-tuple-element.20.refs_0_), channel_id=1, source_target_pairs={{12,0},{16,4},{4,8},{24,12},{28,16},{0,20},{20,24},{8,28},{13,1},{... | collective-permute-start | bytes 132104 | tf_op jit(solution)/shard_map/ppermute | solution.py:40
  20.6 4.4 %collective-permute-start.16 = (bf16[172,128]{1,0:T(8,128)(2,1)S(1)}, bf16[172,128]{1,0:T(8,128)(2,1)S(1)}, u32[]{:S(2)}, u32[]{:S(2)}) collective-permute-start(bf16[172,128]{1,0:T(8,128)(2,1)S(1)} %get-tuple-element.20.refs_0_), channel_id=1, source_target_pairs={{8,0},{20,4},{0,8},{28,12},{24,16},{4,20},{16,24},{12,28},{9,1},{2... | collective-permute-start | bytes 132104 | tf_op jit(solution)/shard_map/ppermute | solution.py:40
  22.2 3.5 %collective-permute-start.13 = (bf16[172,128]{1,0:T(8,128)(2,1)S(1)}, bf16[172,128]{1,0:T(8,128)(2,1)S(1)}, u32[]{:S(2)}, u32[]{:S(2)}) collective-permute-start(bf16[172,128]{1,0:T(8,128)(2,1)S(1)} %get-tuple-element.20.refs_0_), channel_id=1, source_target_pairs={{20,0},{8,4},{28,8},{0,12},{4,16},{24,20},{12,24},{16,28},{21,1},{... | collective-permute-start | bytes 132104 | tf_op jit(solution)/shard_map/ppermute | solution.py:40
  22.2 3.5 %collective-permute-start.12 = (bf16[172,128]{1,0:T(8,128)(2,1)S(1)}, bf16[172,128]{1,0:T(8,128)(2,1)S(1)}, u32[]{:S(2)}, u32[]{:S(2)}) collective-permute-start(bf16[172,128]{1,0:T(8,128)(2,1)S(1)} %get-tuple-element.20.refs_0_), channel_id=1, source_target_pairs={{0,4},{4,0},{8,12},{12,8},{16,20},{20,16},{24,28},{28,24},{1,5},{5... | collective-permute-start | bytes 132104 | tf_op jit(solution)/shard_map/ppermute | solution.py:36
  23.5 2.1 %collective-permute-start.14 = (bf16[172,128]{1,0:T(8,128)(2,1)S(1)}, bf16[172,128]{1,0:T(8,128)(2,1)S(1)}, u32[]{:S(2)}, u32[]{:S(2)}) collective-permute-start(bf16[172,128]{1,0:T(8,128)(2,1)S(1)} %collective-permute-done.10.refs_2_), channel_id=1, source_target_pairs={{0,4},{4,0},{8,12},{12,8},{16,20},{20,16},{24,28},{28,24},{1,5},{5... | collective-permute-start | bytes 132104 | tf_op jit(solution)/shard_map/ppermute | solution.py:36
  23.9 1.7 %collective-permute-start.15 = (bf16[172,128]{1,0:T(8,128)(2,1)S(1)}, bf16[172,128]{1,0:T(8,128)(2,1)S(1)}, u32[]{:S(2)}, u32[]{:S(2)}) collective-permute-start(bf16[172,128]{1,0:T(8,128)(2,1)S(1)} %collective-permute-done.9.refs_1_), channel_id=1, source_target_pairs={{0,4},{4,0},{8,12},{12,8},{16,20},{20,16},{24,28},{28,24},{1,5},{5... | collective-permute-start | bytes 132104 | tf_op jit(solution)/shard_map/ppermute | solution.py:36
  25.0 5.7 %collective-permute-start.11 = (bf16[128,256]{1,0:T(8,128)(2,1)S(1)}, bf16[128,256]{1,0:T(8,128)(2,1)S(1)}, u32[]{:S(2)}, u32[]{:S(2)}) collective-permute-start(bf16[128,256]{1,0:T(8,128)(2,1)S(1)} %shard_map.120), channel_id=1, source_target_pairs={{0,4},{4,0},{8,12},{12,8},{16,20},{20,16},{24,28},{28,24},{1,5},{5... | collective-permute-start | bytes 196616 | tf_op jit(solution)/shard_map/ppermute | solution.py:36
  26.0 6.2 %collective-permute-start.17 = (bf16[172,128]{1,0:T(8,128)(2,1)S(1)}, bf16[172,128]{1,0:T(8,128)(2,1)S(1)}, u32[]{:S(2)}, u32[]{:S(2)}) collective-permute-start(bf16[172,128]{1,0:T(8,128)(2,1)S(1)} %get-tuple-element.24), channel_id=1, source_target_pairs={{0,3},{1,2},{2,1},{3,0},{4,7},{5,6},{6,5},{7,4},{8,11},{9,10},{10,... | collective-permute-start | bytes 132104 | tf_op jit(solution)/shard_map/ppermute | solution.py:36
  28.5 5.1 %collective-permute-start.18 = (bf16[172,128]{1,0:T(8,128)(2,1)S(1)}, bf16[172,128]{1,0:T(8,128)(2,1)S(1)}, u32[]{:S(2)}, u32[]{:S(2)}) collective-permute-start(bf16[172,128]{1,0:T(8,128)(2,1)S(1)} %get-tuple-element.25), channel_id=1, source_target_pairs={{0,2},{1,3},{2,0},{3,1},{4,6},{5,7},{6,4},{7,5},{8,10},{9,11},{10,... | collective-permute-start | bytes 132104 | tf_op jit(solution)/shard_map/ppermute | solution.py:36
  28.5 5.1 %collective-permute-start.19 = (bf16[172,128]{1,0:T(8,128)(2,1)S(1)}, bf16[172,128]{1,0:T(8,128)(2,1)S(1)}, u32[]{:S(2)}, u32[]{:S(2)}) collective-permute-start(bf16[172,128]{1,0:T(8,128)(2,1)S(1)} %get-tuple-element.23.refs_0_), channel_id=1, source_target_pairs={{0,1},{1,0},{2,3},{3,2},{4,5},{5,4},{6,7},{7,6},{8,9},{9,8},{10,11... | collective-permute-start | bytes 132104 | tf_op jit(solution)/shard_map/ppermute | solution.py:36
  (3 other events, 26.4 us)
